TPU v7x, 32 devices: a whole 2x2x4 slice. The times are simulated.
32 devices in a mesh: groups: 2 (over y), tp: 8 (over z, x), dp: 2 (over core).
Axes of the slice: x: 2, y: 2, z: 4, core: 2. Of those that a mesh axis runs over, the one named last changes fastest.
Arguments:
- tokens: bfloat16 [4, 2, 8, 5120], P(('groups', 'dp'), None, 'tp'), parts along dimension 0, may hold values from -400 to 400
- norm_gain: float32 [5120], replicated, may hold values from 0.5 to 1.5
- gate_weight: bfloat16 [5120, 12800], P(None, 'tp'), may hold values from -0.125 to 0.125
- up_weight: bfloat16 [5120, 12800], P(None, 'tp'), may hold values from -0.125 to 0.125
- down_weight: bfloat16 [12800, 5120], P('tp'), may hold values from -0.0546875 to 0.0546875
- cotangent: bfloat16 [4, 2, 8, 5120], P(('groups', 'dp'), None, 'tp'), parts along dimension 0, may hold values from -6 to 6
Outputs:
- input_grad: bfloat16 [4, 2, 8, 5120], P(('groups', 'dp'), None, 'tp'), parts along dimension 0
- gain_grad: float32 [10240], P('groups'), parts along dimension 0
- gate_grad: bfloat16 [10240, 12800], P(('groups', 'dp'), 'tp'), parts along dimension 0
- up_grad: bfloat16 [10240, 12800], P(('groups', 'dp'), 'tp'), parts along dimension 0
- down_grad: bfloat16 [12800, 10240], P('tp', ('groups', 'dp')), parts along dimension 1
There are 2 independent parts, one for each index of `groups`. A program takes and returns all parts, laid end to end along the dimension named above; an argument that names none is the same for every part. Nothing has to cross between parts.
All inputs are finite; a program needn't handle non-finite values.
Results may differ from a plain program's by a relative error of at most 0.0074.
Values may be sent and summed in bfloat16 or wider, within the bound.
No kernel may reach another device: no remote copies, remote signals or barrier semaphores. Data moves between devices by JAX's collectives and lax.ppermute only.
A program may use at most 256 MiB of HBM per device.

v0:
```python
import jax
import jax.numpy as jnp
from jax import lax
from jax.sharding import PartitionSpec as P

EPSILON = 1e-06


def norm_tokens(values_in, norm_gain):
    values = values_in.astype(jnp.float32)
    inverse = lax.rsqrt(jnp.mean(values * values, axis=-1, keepdims=True) + EPSILON)
    scaled = values * inverse
    return (scaled, inverse, (scaled * norm_gain).astype(jnp.bfloat16))


def contract(left, right, left_dim, right_dim):
    return lax.dot_general(
        left, right, (((left_dim,), (right_dim,)), ((), ())), preferred_element_type=jnp.float32
    )


def local_pass(normed_all, grads_all, gate_weight, up_weight, down_weight):
    gate_value = jnp.dot(normed_all, gate_weight, preferred_element_type=jnp.float32)
    up_value = jnp.dot(normed_all, up_weight, preferred_element_type=jnp.float32)
    sigmoid_gate = jax.nn.sigmoid(gate_value)
    active = gate_value * sigmoid_gate
    hidden = (active * up_value).astype(jnp.bfloat16)
    grad_hidden = contract(grads_all, down_weight, 1, 1)
    grad_gate = (
        grad_hidden * up_value * sigmoid_gate * (1.0 + gate_value * (1.0 - sigmoid_gate))
    ).astype(jnp.bfloat16)
    grad_up = (grad_hidden * active).astype(jnp.bfloat16)
    partial_value = contract(grad_gate, gate_weight, 1, 1) + contract(grad_up, up_weight, 1, 1)
    gate_term = contract(normed_all, grad_gate, 0, 0)
    up_term = contract(normed_all, grad_up, 0, 0)
    down_term = contract(hidden, grads_all, 0, 0)
    return (partial_value, gate_term, up_term, down_term)


def body(tokens, norm_gain, gate_weight, up_weight, down_weight, cotangent):
    micro_count, own_tokens, model_width = (tokens.shape[1], tokens.shape[2], tokens.shape[3])
    tp_count = lax.axis_size("tp")
    scaled, inverse, normed = norm_tokens(tokens[0], norm_gain)
    normed_all, grads_all = (
        lax.all_gather(normed, "tp", axis=1, tiled=True),
        lax.all_gather(cotangent[0], "tp", axis=1, tiled=True),
    )
    partial_value, gate_term, up_term, down_term = local_pass(
        normed_all.reshape(-1, model_width),
        grads_all.reshape(-1, model_width),
        gate_weight,
        up_weight,
        down_weight,
    )
    pieces = lax.all_to_all(
        partial_value.reshape(micro_count, tp_count, own_tokens, model_width),
        "tp",
        split_axis=1,
        concat_axis=1,
        tiled=True,
    )
    grad_normed = jnp.sum(pieces, axis=1)
    grad_scaled = grad_normed * norm_gain
    projected = jnp.mean(grad_scaled * scaled, axis=-1, keepdims=True)
    input_rows = cotangent[0].astype(jnp.float32) + inverse * (grad_scaled - scaled * projected)
    gain_term = jnp.sum((grad_normed * scaled).reshape(-1, model_width), axis=0)
    gain_grad = lax.psum(gain_term, ("tp", "dp"))
    gate_grad, up_grad, down_grad = (
        lax.psum_scatter(
            gate_term.astype(jnp.bfloat16), "dp", scatter_dimension=0, tiled=True
        ).astype(jnp.float32),
        lax.psum_scatter(
            up_term.astype(jnp.bfloat16), "dp", scatter_dimension=0, tiled=True
        ).astype(jnp.float32),
        lax.psum_scatter(
            down_term.astype(jnp.bfloat16), "dp", scatter_dimension=1, tiled=True
        ).astype(jnp.float32),
    )
    return (
        input_rows.astype(jnp.bfloat16)[None],
        gain_grad,
        gate_grad.astype(jnp.bfloat16),
        up_grad.astype(jnp.bfloat16),
        down_grad.astype(jnp.bfloat16),
    )


def solution(mesh):
    placed = (
        P(("groups", "dp"), None, "tp", None),
        P(),
        P(None, "tp"),
        P(None, "tp"),
        P("tp", None),
        P(("groups", "dp"), None, "tp", None),
    )
    return jax.shard_map(
        body,
        mesh=mesh,
        in_specs=placed,
        out_specs=(
            P(("groups", "dp"), None, "tp", None),
            P("groups"),
            P(("groups", "dp"), "tp"),
            P(("groups", "dp"), "tp"),
            P("tp", ("groups", "dp")),
        ),
        check_vma=False,
    )
```

profile of v0, /device:TPU:0, one launch (start us, length us, event | category | flops | bytes accessed | tf_op | source)
XLA Modules:
  0.0 229.2 jit_solution(16333022478640776815)
XLA Ops:
  7.2 0.0 reduce-scatter.8.cloned.1.call-start
  7.2 0.9 fusion.19
  8.1 0.8 fusion.21
  8.9 32.4 %all_gather.7 = bf16[2,8,5120]{2,0,1:T(2,128)(2,1)S(1)} all-gather(bf16[2,1,5120]{2,0,1:T(2,128)(2,1)S(1)} %fusion.21), channel_id=1, replica_groups=mesh['groups'=2,'tp'=8,'dp'=2] {'tp'}, dimensions={1}, use_global_device_ids=true | all-gather | bytes 184320 | tf_op jit(solution)/shard_map/all_gather | solution.py:45
  41.3 10.0 %fusion.3 = f32[16,1600]{1,0:T(8,128)S(1)} fusion(bf16[5120,1600]{0,1:T(8,128)(2,1)} %param.8, bf16[2,8,5120]{2,0,1:T(2,128)(2,1)S(1)} %all_gather.7), kind=kOutput, calls=%fused_computation.7 | convolution fusion | flops 262144000 | bytes 16650240 | tf_op jit(solution)/shard_map/dot_general | solution.py:23
  51.3 10.0 %fusion.5 = f32[16,1600]{1,0:T(8,128)S(1)} fusion(bf16[5120,1600]{0,1:T(8,128)(2,1)} %param.9, bf16[2,8,5120]{2,0,1:T(2,128)(2,1)S(1)} %all_gather.7), kind=kOutput, calls=%fused_computation.9 | convolution fusion | flops 262144000 | bytes 16650240 | tf_op jit(solution)/shard_map/dot_general | solution.py:24
  61.3 30.6 %all-gather = bf16[1,2,8,5120]{3,1,0,2:T(2,128)(2,1)S(1)} all-gather(bf16[1,2,1,5120]{3,1,0,2:T(2,128)(2,1)S(1)} %bitcast.58), channel_id=2, replica_groups=mesh['groups'=2,'tp'=8,'dp'=2] {'tp'}, dimensions={2}, use_global_device_ids=true | all-gather | bytes 184320 | tf_op jit(solution)/shard_map/all_gather | solution.py:46
  91.9 8.0 %convolution_convert_fusion = bf16[1600,5120]{1,0:T(8,128)(2,1)} fusion(bf16[1,2,8,5120]{3,1,0,2:T(2,128)(2,1)S(1)} %all-gather, f32[16,1600]{1,0:T(8,128)S(1)} %fusion.5, f32[16,1600]{1,0:T(8,128)S(1)} %fusion.3), kind=kOutput, calls=%fused_computation | convolution fusion | flops 270489600 | bytes 16752640 | tf_op jit(solution)/shard_map/dot_general | solution.py:17
  99.9 0.0 reduce-scatter.8.cloned.1.call-update
  99.9 0.2 reduce-scatter.6.cloned.1.call-start
  100.2 10.0 %multiply_convert_fusion.1 = (bf16[16,1600]{1,0:T(8,128)(2,1)S(1)}, bf16[16,1600]{1,0:T(8,128)(2,1)S(1)}) fusion(f32[16,1600]{1,0:T(8,128)S(1)} %fusion.3, f32[16,1600]{1,0:T(8,128)S(1)} %fusion.5, bf16[1600,5120]{1,0:T(8,128)(2,1)} %param.10, bf16[1,2,8,5120]{3,1,0,2:T(2,128)(2,1)S(1)} %all-gather), kind=kOutput, calls=%fused_computation.17 | convolution fusion | flops 262476800 | bytes 16855040 | tf_op jit(solution)/shard_map/dot_general | solution.py:17
  110.2 11.7 %convolution_convert_fusion.1 = bf16[5120,1600]{0,1:T(8,128)(2,1)} fusion(bf16[16,1600]{1,0:T(8,128)(2,1)S(1)} %get-tuple-element.7, bf16[2,8,5120]{2,0,1:T(2,128)(2,1)S(1)} %all_gather.7), kind=kOutput, calls=%fused_computation.1 | convolution fusion | flops 270336000 | bytes 16599040 | tf_op jit(solution)/shard_map/dot_general | solution.py:17
  121.8 0.0 reduce-scatter.6.cloned.1.call-update
  121.8 0.0 reduce-scatter.4.cloned.1.call-start
  121.9 8.3 %convolution_convert_fusion.2 = bf16[5120,1600]{0,1:T(8,128)(2,1)} fusion(bf16[16,1600]{1,0:T(8,128)(2,1)S(1)} %get-tuple-element.8, bf16[2,8,5120]{2,0,1:T(2,128)(2,1)S(1)} %all_gather.7), kind=kOutput, calls=%fused_computation.2 | convolution fusion | flops 270336000 | bytes 16599040 | tf_op jit(solution)/shard_map/dot_general | solution.py:17
  130.2 0.0 reduce-scatter.4.cloned.1.call-update
  130.2 8.0 %fusion.34 = f32[16,5120]{1,0:T(8,128)S(1)} fusion(bf16[16,1600]{1,0:T(8,128)(2,1)S(1)} %get-tuple-element.8, bf16[5120,1600]{0,1:T(8,128)(2,1)} %param.8), kind=kOutput, calls=%fused_computation.47 | convolution fusion | flops 262144000 | bytes 16762880 | tf_op jit(solution)/shard_map/dot_general | solution.py:17
  138.2 11.4 %fusion = f32[2,8,1,5120]{3,1,0,2:T(8,128)S(1)} fusion(f32[16,5120]{1,0:T(8,128)S(1)} %fusion.34, bf16[16,1600]{1,0:T(8,128)(2,1)S(1)} %get-tuple-element.7, bf16[5120,1600]{0,1:T(8,128)(2,1)} %param.9), kind=kOutput, calls=%fused_computation.4 | convolution fusion | flops 262225920 | bytes 17090560 | tf_op jit(solution)/shard_map/dot_general | solution.py:17
  149.6 0.3 copy.17
  149.9 14.1 %all_to_all.5 = f32[2,8,1,5120]{3,0,2,1:T(2,128)S(1)} all-to-all(f32[2,8,1,5120]{3,0,2,1:T(2,128)S(1)} %copy.17), channel_id=1, replica_groups=mesh['groups'=2,'tp'=8,'dp'=2] {'tp'}, dimensions={1} | all-to-all | bytes 655360 | tf_op jit(solution)/shard_map/all_to_all | solution.py:55
  164.0 0.1 reduce_sum.39
  164.1 0.2 fusion.30
  164.3 57.6 %psum.7 = f32[5120]{0:T(1024)} all-reduce(f32[5120]{0:T(1024)S(1)} %get-tuple-element.5), channel_id=1, replica_groups=mesh['groups'=2,'tp'=8,'dp'=2] {'tp','dp'}, use_global_device_ids=true, to_apply=%region_4.0 | all-reduce | flops 5120 | bytes 40960 | tf_op jit(solution)/shard_map/psum | solution.py:67
  221.9 0.7 fusion.31
  (11 shorter events, 0.0 us)
Async XLA Ops:
  7.2 215.5 %reduce-scatter.8.cloned.1.call-start = ((), (), s32[]{:S(2)}) async-start(), calls=%async_computation.6 | async-start | bytes 24576000 | tf_op jit(solution)/shard_map/reduce_scatter | solution.py:75
  41.3 20.0 %copy-start.2 = (bf16[1,2,1,5120]{3,1,2,0:T(2,128)(2,1)S(1)}, bf16[1,2,1,5120]{3,1,2,0:T(2,128)(2,1)}, u32[]{:S(2)}) copy-start(bf16[1,2,1,5120]{3,1,2,0:T(2,128)(2,1)} %param.11) | copy-start | bytes 61444
  99.9 122.7 %reduce-scatter.6.cloned.1.call-start = ((), (), s32[]{:S(2)}) async-start(), calls=%async_computation.5 | async-start | bytes 24576000 | tf_op jit(solution)/shard_map/reduce_scatter | solution.py:72
  121.8 100.8 %reduce-scatter.4.cloned.1.call-start = ((), (), s32[]{:S(2)}) async-start(), calls=%async_computation.4 | async-start | bytes 24576000 | tf_op jit(solution)/shard_map/reduce_scatter | solution.py:69
  138.2 25.9 %copy-start = (bf16[1,2,1,5120]{3,1,2,0:T(2,128)(2,1)S(1)}, bf16[1,2,1,5120]{3,1,2,0:T(2,128)(2,1)}, u32[]{:S(2)}) copy-start(bf16[1,2,1,5120]{3,1,2,0:T(2,128)(2,1)} %param.6) | copy-start | bytes 61444
  138.2 25.9 %copy-start.1 = (f32[5120]{0:T(1024)S(1)}, f32[5120]{0:T(1024)}, u32[]{:S(2)}) copy-start(f32[5120]{0:T(1024)} %param.7) | copy-start | bytes 61444
Sparse Core Ops, SparseCore 0:
  100.1 26.8 reduce-scatter.7
  130.0 27.2 reduce-scatter.5
  160.2 27.2 reduce-scatter.3
where the time goes:
time: 230 us; the launch traced here: 229 us
  blocking collectives  135 us (59%)
  matrix products  77.3 us (34%)
  between operations  13.8 us (6%)
  other arithmetic  2.78 us (1%)
    psum x1, blocking collectives, body(): gain_grad = lax.psum(gain_term, ('tp', 'dp'))  57.6 us
    dot_general x6, matrix products, contract(): lax.dot_general(left, right, (((left_dim,), (right_dim,)), ((), ())), pre...  57.3 us
    all_gather x1, blocking collectives, body(): lax.all_gather(normed, 'tp', axis=1, tiled=True)  32.4 us
    all_gather x1, blocking collectives, body(): lax.all_gather(cotangent[0], 'tp', axis=1, tiled=True)  30.6 us
    all_to_all x1, blocking collectives, body(): lax.all_to_all(partial_value.reshape(micro_count, tp_count, own_tokens, m...  14.1 us
    dot_general x1, matrix products, local_pass(): jnp.dot(normed_all, up_weight, preferred_element_type=jnp.float32)  9.99 us
    dot_general x1, matrix products, local_pass(): jnp.dot(normed_all, gate_weight, preferred_element_type=jnp.float32)  9.98 us
  transfers between devices with their start and end apart: 3, of which 0 were waited for; matrix products, arithmetic and copies ran while one was open for 22% of the time, Pallas kernels for 0%

commit v1 on v0

--- a/solution.py
+++ b/solution.py
@@ -1,9 +1,21 @@
+import functools
+
 import jax
 import jax.numpy as jnp
 from jax import lax
+from jax.experimental import pallas as pl
+from jax.experimental.pallas import tpu as pltpu
 from jax.sharding import PartitionSpec as P
 
 EPSILON = 1e-06
+LANES = 128
+MIB = 1 << 20
+
+
+def contract(left, right, left_dim, right_dim):
+    return lax.dot_general(
+        left, right, (((left_dim,), (right_dim,)), ((), ())), preferred_element_type=jnp.float32
+    )
 
 
 def norm_tokens(values_in, norm_gain):
@@ -11,12 +23,6 @@
     inverse = lax.rsqrt(jnp.mean(values * values, axis=-1, keepdims=True) + EPSILON)
     scaled = values * inverse
     return (scaled, inverse, (scaled * norm_gain).astype(jnp.bfloat16))
-
-
-def contract(left, right, left_dim, right_dim):
-    return lax.dot_general(
-        left, right, (((left_dim,), (right_dim,)), ((), ())), preferred_element_type=jnp.float32
-    )
 
 
 def local_pass(normed_all, grads_all, gate_weight, up_weight, down_weight):
@@ -37,7 +43,7 @@
     return (partial_value, gate_term, up_term, down_term)
 
 
-def body(tokens, norm_gain, gate_weight, up_weight, down_weight, cotangent):
+def general_body(tokens, norm_gain, gate_weight, up_weight, down_weight, cotangent):
     micro_count, own_tokens, model_width = (tokens.shape[1], tokens.shape[2], tokens.shape[3])
     tp_count = lax.axis_size("tp")
     scaled, inverse, normed = norm_tokens(tokens[0], norm_gain)
@@ -66,23 +72,321 @@
     gain_term = jnp.sum((grad_normed * scaled).reshape(-1, model_width), axis=0)
     gain_grad = lax.psum(gain_term, ("tp", "dp"))
     gate_grad, up_grad, down_grad = (
-        lax.psum_scatter(
-            gate_term.astype(jnp.bfloat16), "dp", scatter_dimension=0, tiled=True
-        ).astype(jnp.float32),
-        lax.psum_scatter(
-            up_term.astype(jnp.bfloat16), "dp", scatter_dimension=0, tiled=True
-        ).astype(jnp.float32),
-        lax.psum_scatter(
-            down_term.astype(jnp.bfloat16), "dp", scatter_dimension=1, tiled=True
-        ).astype(jnp.float32),
+        lax.psum_scatter(gate_term.astype(jnp.bfloat16), "dp", scatter_dimension=0, tiled=True),
+        lax.psum_scatter(up_term.astype(jnp.bfloat16), "dp", scatter_dimension=0, tiled=True),
+        lax.psum_scatter(down_term.astype(jnp.bfloat16), "dp", scatter_dimension=1, tiled=True),
+    )
+    return (input_rows.astype(jnp.bfloat16)[None], gain_grad, gate_grad, up_grad, down_grad)
+
+
+VMEM_SPEC = pl.BlockSpec(memory_space=pltpu.VMEM)
+ANY_SPEC = pl.BlockSpec(memory_space=pl.ANY)
+
+
+def exchange(value, axis, bits):
+    count = lax.axis_size(axis)
+    return lax.ppermute(value, axis, [(i, i ^ bits) for i in range(count)])
+
+
+def gather_kernel(rows, *refs):
+    pieces, out_ref, held = refs[:-2], refs[-2], refs[-1]
+    count = len(pieces)
+    for k, piece in enumerate(pieces):
+        value = piece[...].astype(jnp.float32)
+        held[rows * k : rows * (k + 1), :] = value[:rows]
+        held[rows * (count + k) : rows * (count + k + 1), :] = value[rows:]
+    out_ref[...] = held[...].astype(jnp.bfloat16)
+
+
+def gather_rows(pieces, rows):
+    width = pieces[0].shape[1]
+    total = 2 * rows * len(pieces)
+    return pl.pallas_call(
+        functools.partial(gather_kernel, rows),
+        out_shape=jax.ShapeDtypeStruct((total, width), jnp.bfloat16),
+        in_specs=[VMEM_SPEC] * len(pieces),
+        out_specs=VMEM_SPEC,
+        scratch_shapes=[pltpu.VMEM((total, width), jnp.float32)],
+        compiler_params=pltpu.CompilerParams(vmem_limit_bytes=8 * MIB),
+        name="gather_rows",
+    )(*pieces)
+
+
+def hidden_kernel(
+    chunks, own_ref, peer_ref, gain_ref, gate_hbm, up_hbm, down_hbm,
+    packed_ref, mine_ref, theirs_ref, gain_part_ref, rows_ref,
+    gate_buf, up_buf, down_buf, x_buf, c_buf, inverse_buf, acc_g, acc_u, acc_h, left_buf, sems,
+):
+    half = acc_g.shape[0]
+    toks = x_buf.shape[1]
+    each = toks // 2
+    width = x_buf.shape[2]
+    first = pl.multiple_of(lax.axis_index("dp") * half, 16)
+    weights = ((gate_hbm, gate_buf), (up_hbm, up_buf), (down_hbm, down_buf))
+
+    def fetch(c, w):
+        source, target = weights[w]
+        at = pl.ds(pl.multiple_of(c * width, LANES), width)
+        return pltpu.make_async_copy(
+            source.at[pl.ds(first, half), at], target.at[c], sems.at[w, c]
+        )
+
+    for c in range(chunks):
+        for w in range(3):
+            fetch(c, w).start()
+
+    squares = jnp.zeros((toks, 1), jnp.float32)
+    for c in range(chunks):
+        at = slice(c * width, (c + 1) * width)
+        value = jnp.concatenate([own_ref[:each, at], peer_ref[:each, at]], axis=0)
+        value = value.astype(jnp.float32)
+        squares = squares + jnp.sum(value * value, axis=-1, keepdims=True)
+    inverse = lax.rsqrt(squares / (chunks * width) + EPSILON)
+    inverse_buf[...] = jnp.broadcast_to(inverse, inverse_buf.shape)
+    for c in range(chunks):
+        at = slice(c * width, (c + 1) * width)
+        value = jnp.concatenate([own_ref[:each, at], peer_ref[:each, at]], axis=0)
+        normed = (value.astype(jnp.float32) * inverse * gain_ref[:, at]).astype(jnp.bfloat16)
+        incoming = jnp.concatenate([own_ref[each:, at], peer_ref[each:, at]], axis=0)
+        x_buf[c] = normed
+        c_buf[c] = incoming
+        rows_ref[:toks, at] = normed
+        rows_ref[toks:, at] = incoming
+    acc_g[...] = jnp.zeros_like(acc_g)
+    acc_u[...] = jnp.zeros_like(acc_u)
+    acc_h[...] = jnp.zeros_like(acc_h)
+
+    def forward(c, carry):
+        for w in range(3):
+            fetch(c, w).wait()
+        acc_g[...] += contract(gate_buf[c], x_buf[c], 1, 1)
+        acc_u[...] += contract(up_buf[c], x_buf[c], 1, 1)
+        acc_h[...] += contract(down_buf[c], c_buf[c], 1, 1)
+        return carry
+
+    lax.fori_loop(0, chunks, forward, 0)
+
+    step = 80 if half % 80 == 0 else 16
+
+    def pointwise(i, carry):
+        at = pl.ds(pl.multiple_of(i * step, 16), step)
+        gate, up, grad = acc_g[at, :], acc_u[at, :], acc_h[at, :]
+        sigmoid = jax.nn.sigmoid(gate)
+        active = gate * sigmoid
+        grad_gate = grad * up * sigmoid * (1.0 + gate * (1.0 - sigmoid))
+        parts = [grad_gate, grad * active, active * up, jnp.zeros_like(active)]
+        packed_ref[at, :] = jnp.concatenate(parts, axis=1).astype(jnp.bfloat16)
+        return carry
+
+    lax.fori_loop(0, half // step, pointwise, 0)
+    left_buf[...] = packed_ref[...].astype(jnp.float32).T.astype(jnp.bfloat16)
+
+    def backward(c, carry):
+        at = pl.ds(pl.multiple_of(c * width, LANES), width)
+        part = jnp.dot(left_buf[:toks, :], gate_buf[c], preferred_element_type=jnp.float32)
+        part += jnp.dot(
+            left_buf[toks : 2 * toks, :], up_buf[c], preferred_element_type=jnp.float32
+        )
+        value = jnp.concatenate([own_ref[:each, at], peer_ref[:each, at]], axis=0)
+        scaled = value.astype(jnp.float32) * inverse_buf[:, :1]
+        gain_part_ref[:, at] = jnp.sum(part * scaled, axis=0, keepdims=True)
+        mine_ref[:, at] = part[:each]
+        theirs_ref[:, at] = part[each:].astype(jnp.bfloat16)
+        return carry
+
+    lax.fori_loop(0, chunks, backward, 0)
+
+
+def hidden_pass(own, peer, gain, gate_t, up_t, down):
+    ffw, model = down.shape
+    half, toks = ffw // 2, own.shape[0]
+    each = toks // 2
+    chunks = model // 512
+    width = model // chunks
+    big = pltpu.VMEM((chunks, half, width), jnp.bfloat16)
+    small = pltpu.VMEM((chunks, toks, width), jnp.bfloat16)
+    acc = pltpu.VMEM((half, toks), jnp.float32)
+    return pl.pallas_call(
+        functools.partial(hidden_kernel, chunks),
+        out_shape=(
+            jax.ShapeDtypeStruct((half, LANES), jnp.bfloat16),
+            jax.ShapeDtypeStruct((each, model), jnp.float32),
+            jax.ShapeDtypeStruct((each, model), jnp.bfloat16),
+            jax.ShapeDtypeStruct((1, model), jnp.float32),
+            jax.ShapeDtypeStruct((2 * toks, model), jnp.bfloat16),
+        ),
+        in_specs=[VMEM_SPEC] * 3 + [ANY_SPEC] * 3,
+        out_specs=(VMEM_SPEC,) * 5,
+        scratch_shapes=[
+            big, big, big, small, small,
+            pltpu.VMEM((toks, LANES), jnp.float32),
+            acc, acc, acc,
+            pltpu.VMEM((LANES, half), jnp.bfloat16),
+            pltpu.SemaphoreType.DMA((3, chunks)),
+        ],
+        compiler_params=pltpu.CompilerParams(vmem_limit_bytes=48 * MIB),
+        cost_estimate=pl.CostEstimate(
+            flops=10 * toks * half * model, bytes_accessed=6 * half * model, transcendentals=half * toks
+        ),
+        name="hidden_pass",
+    )(own, peer, gain, gate_t, up_t, down)
+
+
+def weight_kernel(toks, swapped, place_ref, packed_ref, rows_ref, *refs):
+    outs = refs[-3:]
+    width = rows_ref.shape[1]
+    each = toks // 2
+    normed, incoming = rows_ref[:toks, :], rows_ref[toks:, :]
+    if swapped:
+        normed = jnp.concatenate([normed[each:], normed[:each]], axis=0)
+        incoming = jnp.concatenate([incoming[each:], incoming[:each]], axis=0)
+    for k, right in enumerate((normed, normed, incoming)):
+        left = packed_ref[:, k * toks : (k + 1) * toks]
+        outs[k][...] = jnp.dot(left, right, preferred_element_type=jnp.float32).astype(jnp.bfloat16)
+
+
+def weight_pass(place, packed, rows, ffw, swapped, before=()):
+    half, toks, model = packed.shape[0], rows.shape[0] // 2, rows.shape[1]
+    own_width = model // 2
+    width = 512 if own_width % 512 == 0 else LANES
+    steps = own_width // width
+    row = (lambda place: 1 - place[0]) if swapped else (lambda place: place[0])
+    out = jax.ShapeDtypeStruct((ffw, own_width), jnp.bfloat16)
+    return pl.pallas_call(
+        functools.partial(weight_kernel, toks, swapped),
+        out_shape=(out,) * 3,
+        grid_spec=pltpu.PrefetchScalarGridSpec(
+            num_scalar_prefetch=1,
+            grid=(steps,),
+            in_specs=[
+                pl.BlockSpec((half, LANES), lambda j, place: (0, 0)),
+                pl.BlockSpec((2 * toks, width), lambda j, place: (0, place[0] * steps + j)),
+            ]
+            + [ANY_SPEC] * len(before),
+            out_specs=(pl.BlockSpec((half, width), lambda j, place: (row(place), j)),) * 3,
+        ),
+        input_output_aliases={3 + i: i for i in range(len(before))},
+        compiler_params=pltpu.CompilerParams(vmem_limit_bytes=24 * MIB),
+        cost_estimate=pl.CostEstimate(
+            flops=6 * toks * half * own_width, bytes_accessed=6 * half * own_width, transcendentals=0
+        ),
+        name="weight_pass",
+    )(place, packed, rows, *before)
+
+
+def split_kernel(rows, mine_ref, theirs_ref, gain_ref, their_gain_ref, own_ref, gain_out_ref, *refs):
+    outs, held = refs[:-1], refs[-1]
+    held[...] = mine_ref[...] + theirs_ref[...].astype(jnp.float32)
+    gain = gain_ref[...] + their_gain_ref[...]
+    high = gain.astype(jnp.bfloat16)
+    low = (gain - high.astype(jnp.float32)).astype(jnp.bfloat16)
+    own_ref[...] = held[:rows, :]
+    gain_out_ref[...] = gain
+    for k, out in enumerate(outs):
+        piece = held[rows * (k + 1) : rows * (k + 2), :]
+        out[:rows, :] = piece.astype(jnp.bfloat16)
+        out[rows : rows + 1, :] = high
+        out[rows + 1 : rows + 2, :] = low
+
+
+def split_rows(rows, mine, theirs, gain, their_gain):
+    total, model = mine.shape
+    count = total // rows
+    f32, bf16 = jnp.float32, jnp.bfloat16
+    return pl.pallas_call(
+        functools.partial(split_kernel, rows),
+        out_shape=(
+            jax.ShapeDtypeStruct((rows, model), f32),
+            jax.ShapeDtypeStruct((1, model), f32),
+        )
+        + (jax.ShapeDtypeStruct((rows + 2, model), bf16),) * (count - 1),
+        in_specs=[VMEM_SPEC] * 4,
+        out_specs=(VMEM_SPEC,) * (count + 1),
+        scratch_shapes=[pltpu.VMEM((total, model), f32)],
+        compiler_params=pltpu.CompilerParams(vmem_limit_bytes=8 * MIB),
+        name="split_rows",
+    )(mine, theirs, gain, their_gain)
+
+
+def finish_kernel(rows, tokens_ref, incoming_ref, norm_gain_ref, own_ref, gain_ref, *refs):
+    pieces, input_ref, gain_out_ref = refs[:-2], refs[-2], refs[-1]
+    grad_normed, gain = own_ref[...], gain_ref[...]
+    for piece in pieces:
+        value = piece[...].astype(jnp.float32)
+        grad_normed = grad_normed + value[:rows]
+        gain = gain + (value[rows : rows + 1] + value[rows + 1 : rows + 2])
+    gain_out_ref[...] = gain
+    values = tokens_ref[...].astype(jnp.float32)
+    inverse = lax.rsqrt(jnp.mean(values * values, axis=-1, keepdims=True) + EPSILON)
+    scaled = values * inverse
+    grad_scaled = grad_normed * norm_gain_ref[...]
+    projected = jnp.mean(grad_scaled * scaled, axis=-1, keepdims=True)
+    result = incoming_ref[...].astype(jnp.float32) + inverse * (grad_scaled - scaled * projected)
+    input_ref[...] = result.astype(jnp.bfloat16)
+
+
+def finish(rows, tokens, incoming, norm_gain, own, gain, pieces):
+    model = tokens.shape[1]
+    return pl.pallas_call(
+        functools.partial(finish_kernel, rows),
+        out_shape=(
+            jax.ShapeDtypeStruct((rows, model), jnp.bfloat16),
+            jax.ShapeDtypeStruct((1, model), jnp.float32),
+        ),
+        in_specs=[VMEM_SPEC] * (5 + len(pieces)),
+        out_specs=(VMEM_SPEC,) * 2,
+        compiler_params=pltpu.CompilerParams(vmem_limit_bytes=8 * MIB),
+        name="finish",
+    )(tokens, incoming, norm_gain, own, gain, *pieces)
+
+
+def small_body(tokens, norm_gain, gate_weight, up_weight, down_weight, cotangent):
+    rows, model = tokens.shape[1] * tokens.shape[2], tokens.shape[3]
+    ffw = down_weight.shape[0]
+    tp_count = lax.axis_size("tp")
+    place = lax.axis_index("dp").astype(jnp.int32).reshape(1)
+    own_tokens, own_incoming = tokens.reshape(rows, model), cotangent.reshape(rows, model)
+    gain_row = norm_gain.reshape(1, model)
+
+    piece = jnp.concatenate([own_tokens, own_incoming], axis=0)
+    pieces = [piece] + [exchange(piece, "tp", k) for k in range(1, tp_count)]
+    own = gather_rows(pieces, rows)
+    peer = exchange(own, "dp", 1)
+    packed, mine, theirs, gain_part, all_rows = hidden_pass(
+        own, peer, gain_row, gate_weight.T, up_weight.T, down_weight
+    )
+    peer_packed = exchange(packed, "dp", 1)
+    from_peer, gain_from_peer = exchange(theirs, "dp", 1), exchange(gain_part, "dp", 1)
+    grads = weight_pass(place, packed, all_rows, ffw, False)
+    own_sum, gain_sum, *sends = split_rows(rows, mine, from_peer, gain_part, gain_from_peer)
+    received = [exchange(send, "tp", k + 1) for k, send in enumerate(sends)]
+    gate_t, up_t, down_grad = weight_pass(place, peer_packed, all_rows, ffw, True, grads)
+    input_rows, gain_grad = finish(
+        rows, own_tokens, own_incoming, gain_row, own_sum, gain_sum, received
     )
     return (
-        input_rows.astype(jnp.bfloat16)[None],
-        gain_grad,
-        gate_grad.astype(jnp.bfloat16),
-        up_grad.astype(jnp.bfloat16),
-        down_grad.astype(jnp.bfloat16),
-    )
+        input_rows.reshape(tokens.shape),
+        gain_grad.reshape(model),
+        gate_t.T,
+        up_t.T,
+        down_grad,
+    )
+
+
+def body(tokens, norm_gain, gate_weight, up_weight, down_weight, cotangent):
+    tp_count, dp_count = lax.axis_size("tp"), lax.axis_size("dp")
+    ffw, model = down_weight.shape
+    toks = tokens.shape[1] * tokens.shape[2] * tp_count * dp_count
+    small = (
+        dp_count == 2
+        and tp_count & (tp_count - 1) == 0
+        and toks == 32
+        and model % 1024 == 0
+        and ffw % 32 == 0
+        and 3 * ffw * model <= 40 * MIB
+    )
+    chosen = small_body if small else general_body
+    return chosen(tokens, norm_gain, gate_weight, up_weight, down_weight, cotangent)
 
 
 def solution(mesh):

time: 230 us -> 61.5 us (0.27)
  blocking collectives: 135 us -> 0 us
  matrix products: 77.3 us -> 0 us
  Pallas kernels: 0 us -> 28.2 us
  starting transfers between devices: 0.3 us -> 24.5 us
  between operations: 13.8 us -> 0.72 us
  waiting for transfers between devices: 0.05 us -> 6.27 us
    dot_general x8 -> x0, matrix products: 77.3 us -> none  [the longest x6 57.3 us: contract(): lax.dot_general(left, right, (((left_dim,), (right_dim,)), ((), ())), pre...]
    all_gather x2 -> x0, blocking collectives: 62.9 us -> none  [the longest x1 32.4 us: body(): lax.all_gather(normed, 'tp', axis=1, tiled=True)]
    psum x1 -> x0, blocking collectives: 57.6 us -> none  [body(): gain_grad = lax.psum(gain_term, ('tp', 'dp'))]
    pallas_call x0 -> x6, Pallas kernels: none -> 28.2 us  [the longest x1 15 us: hidden_pass(): pl.pallas_call(functools.partial(hidden_kernel, chunks), out_shape=(jax.S...]
    ppermute x0 -> x18, starting transfers between devices: none -> 24.5 us  [exchange(): return lax.ppermute(value, axis, [(i, i ^ bits) for i in range(count)])]
    all_to_all x1 -> x0, blocking collectives: 14.1 us -> none  [body(): lax.all_to_all(partial_value.reshape(micro_count, tp_count, own_tokens, m...]
    ppermute x0 -> x18, waiting for transfers between devices: none -> 6.27 us  [exchange(): return lax.ppermute(value, axis, [(i, i ^ bits) for i in range(count)])]
  transfers between devices with their start and end apart: 3 -> 18, of which waited for: 0 -> 7; matrix products, arithmetic and copies ran while one was open for 22% -> 0% of each run, Pallas kernels for 0% -> 20%
where the time goes in v1:
time: 61.5 us; the launch traced here: 61.2 us
  Pallas kernels  28.2 us (46%)
  starting transfers between devices  24.5 us (40%)
  waiting for transfers between devices  6.27 us (10%)
  other arithmetic  0.79 us (1%)
  local copies, waits for them, and re-layouts  0.74 us (1%)
  between operations  0.72 us (1%)
    ppermute x18, starting transfers between devices, exchange(): return lax.ppermute(value, axis, [(i, i ^ bits) for i in range(count)])  24.5 us
    pallas_call x1, Pallas kernels, hidden_pass(): pl.pallas_call(functools.partial(hidden_kernel, chunks), out_shape=(jax.S...  15 us
    pallas_call x2, Pallas kernels, weight_pass(): pl.pallas_call(functools.partial(weight_kernel, toks, swapped), out_shape...  11.8 us
    ppermute x18, waiting for transfers between devices, exchange(): return lax.ppermute(value, axis, [(i, i ^ bits) for i in range(count)])  6.27 us
  transfers between devices with their start and end apart: 18, of which 7 were waited for; matrix products, arithmetic and copies ran while one was open for 0% of the time, Pallas kernels for 20%

profile of v1, /device:TPU:0, one launch (start us, length us, event | category | flops | bytes accessed | tf_op | source)
XLA Modules:
  0.0 61.2 jit_solution(5532732702996516686)
XLA Ops:
  0.6 0.8 %pad_maximum_fusion.refs_0_ = bf16[4,5120]{1,0:T(4,128)(2,1)S(1)} fusion(bf16[2,5120]{1,0:T(2,128)(2,1)} %bitcast.14, bf16[2,5120]{1,0:T(2,128)(2,1)} %bitcast.12), kind=kLoop, calls=%fused_computation | loop fusion | flops 81920 | bytes 81920 | tf_op jit(solution)/shard_map/concatenate | solution.py:351
  1.4 6.0 %collective-permute-start.6 = (bf16[4,5120]{1,0:T(4,128)(2,1)S(1)}, bf16[4,5120]{1,0:T(4,128)(2,1)S(1)}, u32[]{:S(2)}, u32[]{:S(2)}) collective-permute-start(bf16[4,5120]{1,0:T(4,128)(2,1)S(1)} %pad_maximum_fusion.refs_0_), channel_id=1, source_target_pairs={{0,14},{2,12},{4,10},{6,8},{8,6},{10,4},{12,2},{14,0},{1,15},{3,13... | collective-permute-start | bytes 122888 | tf_op jit(solution)/shard_map/ppermute | solution.py:88
  7.7 0.8 %collective-permute-start.4 = (bf16[4,5120]{1,0:T(4,128)(2,1)S(1)}, bf16[4,5120]{1,0:T(4,128)(2,1)S(1)}, u32[]{:S(2)}, u32[]{:S(2)}) collective-permute-start(bf16[4,5120]{1,0:T(4,128)(2,1)S(1)} %pad_maximum_fusion.refs_0_), channel_id=1, source_target_pairs={{0,10},{2,8},{4,14},{6,12},{8,2},{10,0},{12,6},{14,4},{1,11},{3,9}... | collective-permute-start | bytes 122888 | tf_op jit(solution)/shard_map/ppermute | solution.py:88
  8.5 2.0 %collective-permute-start.3 = (bf16[4,5120]{1,0:T(4,128)(2,1)S(1)}, bf16[4,5120]{1,0:T(4,128)(2,1)S(1)}, u32[]{:S(2)}, u32[]{:S(2)}) collective-permute-start(bf16[4,5120]{1,0:T(4,128)(2,1)S(1)} %pad_maximum_fusion.refs_0_), channel_id=1, source_target_pairs={{0,8},{2,10},{4,12},{6,14},{8,0},{10,2},{12,4},{14,6},{1,9},{3,11}... | collective-permute-start | bytes 122888 | tf_op jit(solution)/shard_map/ppermute | solution.py:88
  10.5 2.3 %collective-permute-start.2 = (bf16[4,5120]{1,0:T(4,128)(2,1)S(1)}, bf16[4,5120]{1,0:T(4,128)(2,1)S(1)}, u32[]{:S(2)}, u32[]{:S(2)}) collective-permute-start(bf16[4,5120]{1,0:T(4,128)(2,1)S(1)} %pad_maximum_fusion.refs_0_), channel_id=1, source_target_pairs={{0,6},{2,4},{4,2},{6,0},{8,14},{10,12},{12,10},{14,8},{1,7},{3,5},... | collective-permute-start | bytes 122888 | tf_op jit(solution)/shard_map/ppermute | solution.py:88
  12.8 0.8 %collective-permute-start.1 = (bf16[4,5120]{1,0:T(4,128)(2,1)S(1)}, bf16[4,5120]{1,0:T(4,128)(2,1)S(1)}, u32[]{:S(2)}, u32[]{:S(2)}) collective-permute-start(bf16[4,5120]{1,0:T(4,128)(2,1)S(1)} %pad_maximum_fusion.refs_0_), channel_id=1, source_target_pairs={{0,4},{2,6},{4,0},{6,2},{8,12},{10,14},{12,8},{14,10},{1,5},{3,7},... | collective-permute-start | bytes 122888 | tf_op jit(solution)/shard_map/ppermute | solution.py:88
  14.0 0.5 collective-permute-done.4.refs_5_
  14.6 1.2 %collective-permute-done.2.refs_3_ = bf16[4,5120]{1,0:T(4,128)(2,1)S(1)} collective-permute-done((bf16[4,5120]{1,0:T(4,128)(2,1)S(1)}, bf16[4,5120]{1,0:T(4,128)(2,1)S(1)}, u32[]{:S(2)}, u32[]{:S(2)}) %collective-permute-start.2) | collective-permute-done | bytes 40992 | tf_op jit(solution)/shard_map/ppermute | solution.py:88
  15.8 1.0 %collective-permute-done.1.refs_2_ = bf16[4,5120]{1,0:T(4,128)(2,1)S(1)} collective-permute-done((bf16[4,5120]{1,0:T(4,128)(2,1)S(1)}, bf16[4,5120]{1,0:T(4,128)(2,1)S(1)}, u32[]{:S(2)}, u32[]{:S(2)}) %collective-permute-start.1) | collective-permute-done | bytes 40992 | tf_op jit(solution)/shard_map/ppermute | solution.py:88
  16.8 0.8 %collective-permute-done.refs_1_ = bf16[4,5120]{1,0:T(4,128)(2,1)S(1)} collective-permute-done((bf16[4,5120]{1,0:T(4,128)(2,1)S(1)}, bf16[4,5120]{1,0:T(4,128)(2,1)S(1)}, u32[]{:S(2)}, u32[]{:S(2)}) %collective-permute-start) | collective-permute-done | bytes 40992 | tf_op jit(solution)/shard_map/ppermute | solution.py:88
  17.8 1.6 %collective-permute-done.7.peer_ref = bf16[32,5120]{1,0:T(8,128)(2,1)S(1)} collective-permute-done((bf16[32,5120]{1,0:T(8,128)(2,1)S(1)}, bf16[32,5120]{1,0:T(8,128)(2,1)S(1)}, u32[]{:S(2)}, u32[]{:S(2)}) %collective-permute-start.7) | collective-permute-done | bytes 327712 | tf_op jit(solution)/shard_map/ppermute | solution.py:88
  19.5 0.7 %copy-done = f32[5120]{0:T(1024)S(1)} copy-done((f32[5120]{0:T(1024)S(1)}, f32[5120]{0:T(1024)}, u32[]{:S(2)}) %copy-start) | copy-done | bytes 20504
  20.2 15.0 %hidden_pass.1 = (bf16[800,128]{1,0:T(8,128)(2,1)S(1)}, f32[16,5120]{1,0:T(8,128)S(1)}, bf16[16,5120]{1,0:T(8,128)(2,1)S(1)}, f32[1,5120]{1,0:T(1,128)S(1)}, bf16[64,5120]{1,0:T(8,128)(2,1)S(1)}) custom-call(bf16[32,5120]{1,0:T(8,128)(2,1)S(1)} %gather_rows.1.own_ref, bf16[32,5120]{1,0:T(8,128)(2,1)S(1)} %collective-permute-done.7.peer_ref, ...), custom_call_target="tpu_custom_call" | custom-call | flops 1310720000 | bytes 24576000 | tf_op jit(solution)/shard_map/hidden_pass/pallas_call | solution.py:209
  35.9 1.0 %collective-permute-done.9.their_gain_ref = f32[1,5120]{1,0:T(1,128)S(1)} collective-permute-done((f32[1,5120]{1,0:T(1,128)S(1)}, f32[1,5120]{1,0:T(1,128)S(1)}, u32[]{:S(2)}, u32[]{:S(2)}) %collective-permute-start.9) | collective-permute-done | bytes 20512 | tf_op jit(solution)/shard_map/ppermute | solution.py:88
  37.2 0.5 collective-permute-start.10
  37.7 1.4 %collective-permute-start.11 = (bf16[4,5120]{1,0:T(4,128)(2,1)S(1)}, bf16[4,5120]{1,0:T(4,128)(2,1)S(1)}, u32[]{:S(2)}, u32[]{:S(2)}) collective-permute-start(bf16[4,5120]{1,0:T(4,128)(2,1)S(1)} %get-tuple-element.33), channel_id=1, source_target_pairs={{0,4},{2,6},{4,0},{6,2},{8,12},{10,14},{12,8},{14,10},{1,5},{3,7},... | collective-permute-start | bytes 122888 | tf_op jit(solution)/shard_map/ppermute | solution.py:88
  39.1 1.7 %collective-permute-start.12 = (bf16[4,5120]{1,0:T(4,128)(2,1)S(1)}, bf16[4,5120]{1,0:T(4,128)(2,1)S(1)}, u32[]{:S(2)}, u32[]{:S(2)}) collective-permute-start(bf16[4,5120]{1,0:T(4,128)(2,1)S(1)} %get-tuple-element.34), channel_id=1, source_target_pairs={{0,6},{2,4},{4,2},{6,0},{8,14},{10,12},{12,10},{14,8},{1,7},{3,5},... | collective-permute-start | bytes 122888 | tf_op jit(solution)/shard_map/ppermute | solution.py:88
  40.7 2.2 %collective-permute-start.13 = (bf16[4,5120]{1,0:T(4,128)(2,1)S(1)}, bf16[4,5120]{1,0:T(4,128)(2,1)S(1)}, u32[]{:S(2)}, u32[]{:S(2)}) collective-permute-start(bf16[4,5120]{1,0:T(4,128)(2,1)S(1)} %get-tuple-element.35), channel_id=1, source_target_pairs={{0,8},{2,10},{4,12},{6,14},{8,0},{10,2},{12,4},{14,6},{1,9},{3,11}... | collective-permute-start | bytes 122888 | tf_op jit(solution)/shard_map/ppermute | solution.py:88
  43.0 0.6 collective-permute-start.14
  43.6 3.7 %collective-permute-start.15 = (bf16[4,5120]{1,0:T(4,128)(2,1)S(1)}, bf16[4,5120]{1,0:T(4,128)(2,1)S(1)}, u32[]{:S(2)}, u32[]{:S(2)}) collective-permute-start(bf16[4,5120]{1,0:T(4,128)(2,1)S(1)} %get-tuple-element.37), channel_id=1, source_target_pairs={{0,12},{2,14},{4,8},{6,10},{8,4},{10,6},{12,0},{14,2},{1,13},{3,15... | collective-permute-start | bytes 122888 | tf_op jit(solution)/shard_map/ppermute | solution.py:88
  47.3 1.1 %collective-permute-start.16 = (bf16[4,5120]{1,0:T(4,128)(2,1)S(1)}, bf16[4,5120]{1,0:T(4,128)(2,1)S(1)}, u32[]{:S(2)}, u32[]{:S(2)}) collective-permute-start(bf16[4,5120]{1,0:T(4,128)(2,1)S(1)} %get-tuple-element.38), channel_id=1, source_target_pairs={{0,14},{2,12},{4,10},{6,8},{8,6},{10,4},{12,2},{14,0},{1,15},{3,13... | collective-permute-start | bytes 122888 | tf_op jit(solution)/shard_map/ppermute | solution.py:88
  48.4 5.9 %weight_pass.2 = (bf16[1600,2560]{1,0:T(8,128)(2,1)}, bf16[1600,2560]{1,0:T(8,128)(2,1)}, bf16[1600,2560]{1,0:T(8,128)(2,1)}) custom-call(s32[1]{0:T(128)} %bitcast.7.place_ref, bf16[800,128]{1,0:T(8,128)(2,1)S(1)} %get-tuple-element.41.packed_ref, bf16[64,5120]{1,0:T(8,128)(2,1)S(1)} %get-tuple-element.42.rows_ref), custom_call_target="tpu_custom_call" | custom-call | flops 393216000 | bytes 12288000 | tf_op jit(solution)/shard_map/weight_pass/pallas_call | solution.py:255
  54.3 6.0 %weight_pass.3 = (bf16[1600,2560]{1,0:T(8,128)(2,1)}, bf16[1600,2560]{1,0:T(8,128)(2,1)}, bf16[1600,2560]{1,0:T(8,128)(2,1)}) custom-call(s32[1]{0:T(128)} %bitcast.7.place_ref, bf16[800,128]{1,0:T(8,128)(2,1)S(1)} %collective-permute-done.17.packed_ref, ...), custom_call_target="tpu_custom_call", output_to_operand_aliasing={{0}: (3, {}), {1}: (4, {}), {2}: (5, {})} | custom-call | flops 393216000 | bytes 12288000 | tf_op jit(solution)/shard_map/weight_pass/pallas_call | solution.py:255
  60.3 0.9 %finish.1 = (bf16[2,5120]{1,0:T(2,128)(2,1)}, f32[1,5120]{1,0:T(1,128)}) custom-call(bf16[2,5120]{1,0:T(2,128)(2,1)S(1)} %bitcast.13, bf16[2,5120]{1,0:T(2,128)(2,1)S(1)} %bitcast.15, f32[1,5120]{1,0:T(1,128)S(1)} %bitcast.11, f32[2,5120]{1,0:T(2,128)S(1)} %get-tuple-element.30.own_ref, f32[1,5120]{1,0:T(1,128)S(1)} %get-tuple-element.31.gain_ref, ...), custom_call_target="tpu_custom_call" | custom-call | tf_op jit(solution)/shard_map/finish/pallas_call | solution.py:330
  (27 shorter events, 2.0 us)
Async XLA Ops:
  1.4 11.3 %collective-permute-start.6 = (bf16[4,5120]{1,0:T(4,128)(2,1)S(1)}, bf16[4,5120]{1,0:T(4,128)(2,1)S(1)}, u32[]{:S(2)}, u32[]{:S(2)}) collective-permute-start(bf16[4,5120]{1,0:T(4,128)(2,1)S(1)} %pad_maximum_fusion.refs_0_), channel_id=1, source_target_pairs={{0,14},{2,12},{4,10},{6,8},{8,6},{10,4},{12,2},{14,0},{1,15},{3,13... | collective-permute-start | bytes 122888 | tf_op jit(solution)/shard_map/ppermute | solution.py:88
  7.5 6.1 %collective-permute-start.5 = (bf16[4,5120]{1,0:T(4,128)(2,1)S(1)}, bf16[4,5120]{1,0:T(4,128)(2,1)S(1)}, u32[]{:S(2)}, u32[]{:S(2)}) collective-permute-start(bf16[4,5120]{1,0:T(4,128)(2,1)S(1)} %pad_maximum_fusion.refs_0_), channel_id=1, source_target_pairs={{0,12},{2,14},{4,8},{6,10},{8,4},{10,6},{12,0},{14,2},{1,13},{3,15... | collective-permute-start | bytes 122888 | tf_op jit(solution)/shard_map/ppermute | solution.py:88
  7.7 6.8 %collective-permute-start.4 = (bf16[4,5120]{1,0:T(4,128)(2,1)S(1)}, bf16[4,5120]{1,0:T(4,128)(2,1)S(1)}, u32[]{:S(2)}, u32[]{:S(2)}) collective-permute-start(bf16[4,5120]{1,0:T(4,128)(2,1)S(1)} %pad_maximum_fusion.refs_0_), channel_id=1, source_target_pairs={{0,10},{2,8},{4,14},{6,12},{8,2},{10,0},{12,6},{14,4},{1,11},{3,9}... | collective-permute-start | bytes 122888 | tf_op jit(solution)/shard_map/ppermute | solution.py:88
  8.5 6.2 %collective-permute-start.3 = (bf16[4,5120]{1,0:T(4,128)(2,1)S(1)}, bf16[4,5120]{1,0:T(4,128)(2,1)S(1)}, u32[]{:S(2)}, u32[]{:S(2)}) collective-permute-start(bf16[4,5120]{1,0:T(4,128)(2,1)S(1)} %pad_maximum_fusion.refs_0_), channel_id=1, source_target_pairs={{0,8},{2,10},{4,12},{6,14},{8,0},{10,2},{12,4},{14,6},{1,9},{3,11}... | collective-permute-start | bytes 122888 | tf_op jit(solution)/shard_map/ppermute | solution.py:88
  10.5 5.3 %collective-permute-start.2 = (bf16[4,5120]{1,0:T(4,128)(2,1)S(1)}, bf16[4,5120]{1,0:T(4,128)(2,1)S(1)}, u32[]{:S(2)}, u32[]{:S(2)}) collective-permute-start(bf16[4,5120]{1,0:T(4,128)(2,1)S(1)} %pad_maximum_fusion.refs_0_), channel_id=1, source_target_pairs={{0,6},{2,4},{4,2},{6,0},{8,14},{10,12},{12,10},{14,8},{1,7},{3,5},... | collective-permute-start | bytes 122888 | tf_op jit(solution)/shard_map/ppermute | solution.py:88
  12.8 4.0 %collective-permute-start.1 = (bf16[4,5120]{1,0:T(4,128)(2,1)S(1)}, bf16[4,5120]{1,0:T(4,128)(2,1)S(1)}, u32[]{:S(2)}, u32[]{:S(2)}) collective-permute-start(bf16[4,5120]{1,0:T(4,128)(2,1)S(1)} %pad_maximum_fusion.refs_0_), channel_id=1, source_target_pairs={{0,4},{2,6},{4,0},{6,2},{8,12},{10,14},{12,8},{14,10},{1,5},{3,7},... | collective-permute-start | bytes 122888 | tf_op jit(solution)/shard_map/ppermute | solution.py:88
  13.6 4.0 %collective-permute-start = (bf16[4,5120]{1,0:T(4,128)(2,1)S(1)}, bf16[4,5120]{1,0:T(4,128)(2,1)S(1)}, u32[]{:S(2)}, u32[]{:S(2)}) collective-permute-start(bf16[4,5120]{1,0:T(4,128)(2,1)S(1)} %pad_maximum_fusion.refs_0_), channel_id=1, source_target_pairs={{0,2},{2,0},{4,6},{6,4},{8,10},{10,8},{12,14},{14,12},{1,3},{3,1},... | collective-permute-start | bytes 122888 | tf_op jit(solution)/shard_map/ppermute | solution.py:88
  17.8 1.7 %collective-permute-start.7 = (bf16[32,5120]{1,0:T(8,128)(2,1)S(1)}, bf16[32,5120]{1,0:T(8,128)(2,1)S(1)}, u32[]{:S(2)}, u32[]{:S(2)}) collective-permute-start(bf16[32,5120]{1,0:T(8,128)(2,1)S(1)} %gather_rows.1.own_ref), channel_id=1, source_target_pairs={{0,1},{1,0},{2,3},{3,2},{4,5},{5,4},{6,7},{7,6},{8,9},{9,8},{10,11... | collective-permute-start | bytes 983048 | tf_op jit(solution)/shard_map/ppermute | solution.py:88
  19.5 0.7 %copy-start = (f32[5120]{0:T(1024)S(1)}, f32[5120]{0:T(1024)}, u32[]{:S(2)}) copy-start(f32[5120]{0:T(1024)} %param.7) | copy-start | bytes 61444
  35.2 1.8 %collective-permute-start.8 = (bf16[16,5120]{1,0:T(8,128)(2,1)S(1)}, bf16[16,5120]{1,0:T(8,128)(2,1)S(1)}, u32[]{:S(2)}, u32[]{:S(2)}) collective-permute-start(bf16[16,5120]{1,0:T(8,128)(2,1)S(1)} %get-tuple-element.28), channel_id=1, source_target_pairs={{0,1},{1,0},{2,3},{3,2},{4,5},{5,4},{6,7},{7,6},{8,9},{9,8},{10,11... | collective-permute-start | bytes 491528 | tf_op jit(solution)/shard_map/ppermute | solution.py:88
  35.4 7.6 %collective-permute-start.17 = (bf16[800,128]{1,0:T(8,128)(2,1)S(1)}, bf16[800,128]{1,0:T(8,128)(2,1)S(1)}, u32[]{:S(2)}, u32[]{:S(2)}) collective-permute-start(bf16[800,128]{1,0:T(8,128)(2,1)S(1)} %get-tuple-element.41.packed_ref), channel_id=1, source_target_pairs={{0,1},{1,0},{2,3},{3,2},{4,5},{5,4},{6,7},{7,6},{8,9},{9,8},{10,11... | collective-permute-start | bytes 614408 | tf_op jit(solution)/shard_map/ppermute | solution.py:88
  35.8 1.2 %collective-permute-start.9 = (f32[1,5120]{1,0:T(1,128)S(1)}, f32[1,5120]{1,0:T(1,128)S(1)}, u32[]{:S(2)}, u32[]{:S(2)}) collective-permute-start(f32[1,5120]{1,0:T(1,128)S(1)} %get-tuple-element.29.gain_ref), channel_id=1, source_target_pairs={{0,1},{1,0},{2,3},{3,2},{4,5},{5,4},{6,7},{7,6},{8,9},{9,8},{10,11... | collective-permute-start | bytes 61448 | tf_op jit(solution)/shard_map/ppermute | solution.py:88
  37.2 6.4 %collective-permute-start.10 = (bf16[4,5120]{1,0:T(4,128)(2,1)S(1)}, bf16[4,5120]{1,0:T(4,128)(2,1)S(1)}, u32[]{:S(2)}, u32[]{:S(2)}) collective-permute-start(bf16[4,5120]{1,0:T(4,128)(2,1)S(1)} %get-tuple-element.32), channel_id=1, source_target_pairs={{0,2},{2,0},{4,6},{6,4},{8,10},{10,8},{12,14},{14,12},{1,3},{3,1},... | collective-permute-start | bytes 122888 | tf_op jit(solution)/shard_map/ppermute | solution.py:88
  37.7 9.6 %collective-permute-start.11 = (bf16[4,5120]{1,0:T(4,128)(2,1)S(1)}, bf16[4,5120]{1,0:T(4,128)(2,1)S(1)}, u32[]{:S(2)}, u32[]{:S(2)}) collective-permute-start(bf16[4,5120]{1,0:T(4,128)(2,1)S(1)} %get-tuple-element.33), channel_id=1, source_target_pairs={{0,4},{2,6},{4,0},{6,2},{8,12},{10,14},{12,8},{14,10},{1,5},{3,7},... | collective-permute-start | bytes 122888 | tf_op jit(solution)/shard_map/ppermute | solution.py:88
  39.1 21.2 %collective-permute-start.12 = (bf16[4,5120]{1,0:T(4,128)(2,1)S(1)}, bf16[4,5120]{1,0:T(4,128)(2,1)S(1)}, u32[]{:S(2)}, u32[]{:S(2)}) collective-permute-start(bf16[4,5120]{1,0:T(4,128)(2,1)S(1)} %get-tuple-element.34), channel_id=1, source_target_pairs={{0,6},{2,4},{4,2},{6,0},{8,14},{10,12},{12,10},{14,8},{1,7},{3,5},... | collective-permute-start | bytes 122888 | tf_op jit(solution)/shard_map/ppermute | solution.py:88
  40.7 19.5 %collective-permute-start.13 = (bf16[4,5120]{1,0:T(4,128)(2,1)S(1)}, bf16[4,5120]{1,0:T(4,128)(2,1)S(1)}, u32[]{:S(2)}, u32[]{:S(2)}) collective-permute-start(bf16[4,5120]{1,0:T(4,128)(2,1)S(1)} %get-tuple-element.35), channel_id=1, source_target_pairs={{0,8},{2,10},{4,12},{6,14},{8,0},{10,2},{12,4},{14,6},{1,9},{3,11}... | collective-permute-start | bytes 122888 | tf_op jit(solution)/shard_map/ppermute | solution.py:88
  43.0 17.3 %collective-permute-start.14 = (bf16[4,5120]{1,0:T(4,128)(2,1)S(1)}, bf16[4,5120]{1,0:T(4,128)(2,1)S(1)}, u32[]{:S(2)}, u32[]{:S(2)}) collective-permute-start(bf16[4,5120]{1,0:T(4,128)(2,1)S(1)} %get-tuple-element.36), channel_id=1, source_target_pairs={{0,10},{2,8},{4,14},{6,12},{8,2},{10,0},{12,6},{14,4},{1,11},{3,9}... | collective-permute-start | bytes 122888 | tf_op jit(solution)/shard_map/ppermute | solution.py:88
  43.6 16.7 %collective-permute-start.15 = (bf16[4,5120]{1,0:T(4,128)(2,1)S(1)}, bf16[4,5120]{1,0:T(4,128)(2,1)S(1)}, u32[]{:S(2)}, u32[]{:S(2)}) collective-permute-start(bf16[4,5120]{1,0:T(4,128)(2,1)S(1)} %get-tuple-element.37), channel_id=1, source_target_pairs={{0,12},{2,14},{4,8},{6,10},{8,4},{10,6},{12,0},{14,2},{1,13},{3,15... | collective-permute-start | bytes 122888 | tf_op jit(solution)/shard_map/ppermute | solution.py:88
  47.3 13.0 %collective-permute-start.16 = (bf16[4,5120]{1,0:T(4,128)(2,1)S(1)}, bf16[4,5120]{1,0:T(4,128)(2,1)S(1)}, u32[]{:S(2)}, u32[]{:S(2)}) collective-permute-start(bf16[4,5120]{1,0:T(4,128)(2,1)S(1)} %get-tuple-element.38), channel_id=1, source_target_pairs={{0,14},{2,12},{4,10},{6,8},{8,6},{10,4},{12,2},{14,0},{1,15},{3,13... | collective-permute-start | bytes 122888 | tf_op jit(solution)/shard_map/ppermute | solution.py:88
  54.3 6.0 %copy-start.1 = (f32[5120]{0:T(1024)S(1)}, f32[5120]{0:T(1024)}, u32[]{:S(2)}) copy-start(f32[5120]{0:T(1024)} %param.7) | copy-start | bytes 61444
  54.3 6.0 %copy-start.2 = (bf16[1,2,1,5120]{3,1,2,0:T(2,128)(2,1)S(1)}, bf16[1,2,1,5120]{3,1,2,0:T(2,128)(2,1)}, u32[]{:S(2)}) copy-start(bf16[1,2,1,5120]{3,1,2,0:T(2,128)(2,1)} %param.6) | copy-start | bytes 61444
  54.3 6.0 %copy-start.3 = (bf16[1,2,1,5120]{3,1,2,0:T(2,128)(2,1)S(1)}, bf16[1,2,1,5120]{3,1,2,0:T(2,128)(2,1)}, u32[]{:S(2)}) copy-start(bf16[1,2,1,5120]{3,1,2,0:T(2,128)(2,1)} %param.11) | copy-start | bytes 61444

commit v2 on v1

--- a/solution.py
+++ b/solution.py
@@ -88,34 +88,51 @@
     return lax.ppermute(value, axis, [(i, i ^ bits) for i in range(count)])
 
 
-def gather_kernel(rows, *refs):
-    pieces, out_ref, held = refs[:-2], refs[-2], refs[-1]
-    count = len(pieces)
-    for k, piece in enumerate(pieces):
-        value = piece[...].astype(jnp.float32)
-        held[rows * k : rows * (k + 1), :] = value[:rows]
-        held[rows * (count + k) : rows * (count + k + 1), :] = value[rows:]
+def high_part(value):
+    return value.astype(jnp.bfloat16)
+
+
+def low_part(value):
+    return (value - value.astype(jnp.bfloat16).astype(jnp.float32)).astype(jnp.bfloat16)
+
+
+def join_kernel(first_ref, second_ref, out_ref, held):
+    count = first_ref.shape[0]
+    held[:count, :] = first_ref[...].astype(jnp.float32)
+    held[count:, :] = second_ref[...].astype(jnp.float32)
     out_ref[...] = held[...].astype(jnp.bfloat16)
 
 
-def gather_rows(pieces, rows):
-    width = pieces[0].shape[1]
-    total = 2 * rows * len(pieces)
+def sort_kernel(rows, first_ref, second_ref, out_ref, held):
+    pieces = first_ref.shape[0] // (2 * rows)
+    for half, ref in enumerate((first_ref, second_ref)):
+        value = ref[...].astype(jnp.float32)
+        for k in range(pieces):
+            at = rows * (pieces * half + k)
+            held[at : at + rows, :] = value[2 * rows * k : 2 * rows * k + rows]
+            at += 2 * rows * pieces
+            held[at : at + rows, :] = value[2 * rows * k + rows : 2 * rows * (k + 1)]
+    out_ref[...] = held[...].astype(jnp.bfloat16)
+
+
+def stack_rows(kernel, first, second, name):
+    shape = (2 * first.shape[0], first.shape[1])
     return pl.pallas_call(
-        functools.partial(gather_kernel, rows),
-        out_shape=jax.ShapeDtypeStruct((total, width), jnp.bfloat16),
-        in_specs=[VMEM_SPEC] * len(pieces),
+        kernel,
+        out_shape=jax.ShapeDtypeStruct(shape, jnp.bfloat16),
+        in_specs=[VMEM_SPEC] * 2,
         out_specs=VMEM_SPEC,
-        scratch_shapes=[pltpu.VMEM((total, width), jnp.float32)],
+        scratch_shapes=[pltpu.VMEM(shape, jnp.float32)],
         compiler_params=pltpu.CompilerParams(vmem_limit_bytes=8 * MIB),
-        name="gather_rows",
-    )(*pieces)
+        name=name,
+    )(first, second)
 
 
 def hidden_kernel(
-    chunks, own_ref, peer_ref, gain_ref, gate_hbm, up_hbm, down_hbm,
+    chunks, own_ref, peer_ref, gain_hbm, gate_hbm, up_hbm, down_hbm,
     packed_ref, mine_ref, theirs_ref, gain_part_ref, rows_ref,
-    gate_buf, up_buf, down_buf, x_buf, c_buf, inverse_buf, acc_g, acc_u, acc_h, left_buf, sems,
+    gate_buf, up_buf, down_buf, x_buf, c_buf, inverse_buf, acc_g, acc_u, acc_h, left_buf, gain_ref,
+    sems, gain_sem,
 ):
     half = acc_g.shape[0]
     toks = x_buf.shape[1]
@@ -131,6 +148,8 @@
             source.at[pl.ds(first, half), at], target.at[c], sems.at[w, c]
         )
 
+    gain_copy = pltpu.make_async_copy(gain_hbm, gain_ref, gain_sem)
+    gain_copy.start()
     for c in range(chunks):
         for w in range(3):
             fetch(c, w).start()
@@ -143,6 +162,7 @@
         squares = squares + jnp.sum(value * value, axis=-1, keepdims=True)
     inverse = lax.rsqrt(squares / (chunks * width) + EPSILON)
     inverse_buf[...] = jnp.broadcast_to(inverse, inverse_buf.shape)
+    gain_copy.wait()
     for c in range(chunks):
         at = slice(c * width, (c + 1) * width)
         value = jnp.concatenate([own_ref[:each, at], peer_ref[:each, at]], axis=0)
@@ -189,9 +209,12 @@
         )
         value = jnp.concatenate([own_ref[:each, at], peer_ref[:each, at]], axis=0)
         scaled = value.astype(jnp.float32) * inverse_buf[:, :1]
-        gain_part_ref[:, at] = jnp.sum(part * scaled, axis=0, keepdims=True)
+        gain = jnp.sum(part * scaled, axis=0, keepdims=True)
+        gain_part_ref[:, at] = gain
         mine_ref[:, at] = part[:each]
-        theirs_ref[:, at] = part[each:].astype(jnp.bfloat16)
+        theirs_ref[:each, at] = part[each:].astype(jnp.bfloat16)
+        theirs_ref[each : each + 1, at] = high_part(gain)
+        theirs_ref[each + 1 : each + 2, at] = low_part(gain)
         return carry
 
     lax.fori_loop(0, chunks, backward, 0)
@@ -211,18 +234,20 @@
         out_shape=(
             jax.ShapeDtypeStruct((half, LANES), jnp.bfloat16),
             jax.ShapeDtypeStruct((each, model), jnp.float32),
-            jax.ShapeDtypeStruct((each, model), jnp.bfloat16),
+            jax.ShapeDtypeStruct((each + 2, model), jnp.bfloat16),
             jax.ShapeDtypeStruct((1, model), jnp.float32),
             jax.ShapeDtypeStruct((2 * toks, model), jnp.bfloat16),
         ),
-        in_specs=[VMEM_SPEC] * 3 + [ANY_SPEC] * 3,
+        in_specs=[VMEM_SPEC] * 2 + [ANY_SPEC] * 4,
         out_specs=(VMEM_SPEC,) * 5,
         scratch_shapes=[
             big, big, big, small, small,
             pltpu.VMEM((toks, LANES), jnp.float32),
             acc, acc, acc,
             pltpu.VMEM((LANES, half), jnp.bfloat16),
+            pltpu.VMEM((1, model), jnp.float32),
             pltpu.SemaphoreType.DMA((3, chunks)),
+            pltpu.SemaphoreType.DMA(()),
         ],
         compiler_params=pltpu.CompilerParams(vmem_limit_bytes=48 * MIB),
         cost_estimate=pl.CostEstimate(
@@ -232,11 +257,15 @@
     )(own, peer, gain, gate_t, up_t, down)
 
 
-def weight_kernel(toks, swapped, place_ref, packed_ref, rows_ref, *refs):
-    outs = refs[-3:]
-    width = rows_ref.shape[1]
+def weight_kernel(toks, swapped, first, place_ref, packed_ref, rows_ref, *refs):
+    outs, written_ref = refs[-4:-1], refs[-1]
+    width = outs[0].shape[1]
     each = toks // 2
-    normed, incoming = rows_ref[:toks, :], rows_ref[toks:, :]
+    written_ref[...] = jnp.zeros_like(written_ref)
+    own_width = rows_ref.shape[1] // 2
+    start = place_ref[0] * own_width + (first + pl.program_id(0)) * width
+    at = pl.ds(pl.multiple_of(start, LANES), width)
+    normed, incoming = rows_ref[:toks, at], rows_ref[toks:, at]
     if swapped:
         normed = jnp.concatenate([normed[each:], normed[:each]], axis=0)
         incoming = jnp.concatenate([incoming[each:], incoming[:each]], axis=0)
@@ -245,67 +274,62 @@
         outs[k][...] = jnp.dot(left, right, preferred_element_type=jnp.float32).astype(jnp.bfloat16)
 
 
-def weight_pass(place, packed, rows, ffw, swapped, before=()):
+def weight_pass(place, packed, rows, ffw, swapped, part, parts, before=(), after=()):
     half, toks, model = packed.shape[0], rows.shape[0] // 2, rows.shape[1]
     own_width = model // 2
-    width = 512 if own_width % 512 == 0 else LANES
-    steps = own_width // width
+    width = 256
+    steps = own_width // width // parts
+    first = part * steps
     row = (lambda place: 1 - place[0]) if swapped else (lambda place: place[0])
     out = jax.ShapeDtypeStruct((ffw, own_width), jnp.bfloat16)
     return pl.pallas_call(
-        functools.partial(weight_kernel, toks, swapped),
-        out_shape=(out,) * 3,
+        functools.partial(weight_kernel, toks, swapped, first),
+        out_shape=(out,) * 3 + (jax.ShapeDtypeStruct((8, LANES), jnp.float32),),
         grid_spec=pltpu.PrefetchScalarGridSpec(
             num_scalar_prefetch=1,
             grid=(steps,),
-            in_specs=[
-                pl.BlockSpec((half, LANES), lambda j, place: (0, 0)),
-                pl.BlockSpec((2 * toks, width), lambda j, place: (0, place[0] * steps + j)),
-            ]
-            + [ANY_SPEC] * len(before),
-            out_specs=(pl.BlockSpec((half, width), lambda j, place: (row(place), j)),) * 3,
+            in_specs=[VMEM_SPEC] * 2 + [ANY_SPEC] * (len(before) + len(after)),
+            out_specs=(pl.BlockSpec((half, width), lambda j, place: (row(place), first + j)),) * 3
+            + (pl.BlockSpec((8, LANES), lambda j, place: (0, 0)),),
         ),
         input_output_aliases={3 + i: i for i in range(len(before))},
-        compiler_params=pltpu.CompilerParams(vmem_limit_bytes=24 * MIB),
+        compiler_params=pltpu.CompilerParams(vmem_limit_bytes=16 * MIB),
         cost_estimate=pl.CostEstimate(
-            flops=6 * toks * half * own_width, bytes_accessed=6 * half * own_width, transcendentals=0
+            flops=6 * toks * half * own_width // parts,
+            bytes_accessed=6 * half * own_width // parts,
+            transcendentals=0,
         ),
         name="weight_pass",
-    )(place, packed, rows, *before)
-
-
-def split_kernel(rows, mine_ref, theirs_ref, gain_ref, their_gain_ref, own_ref, gain_out_ref, *refs):
-    outs, held = refs[:-1], refs[-1]
-    held[...] = mine_ref[...] + theirs_ref[...].astype(jnp.float32)
-    gain = gain_ref[...] + their_gain_ref[...]
-    high = gain.astype(jnp.bfloat16)
-    low = (gain - high.astype(jnp.float32)).astype(jnp.bfloat16)
-    own_ref[...] = held[:rows, :]
+    )(place, packed, rows, *before, *after)
+
+
+def fold_kernel(kept_ref, gain_ref, arrived_ref, _, keep_ref, gain_out_ref, send_ref, held):
+    count = kept_ref.shape[0]
+    arrived = arrived_ref[...].astype(jnp.float32)
+    gain = gain_ref[...] + (arrived[count : count + 1] + arrived[count + 1 : count + 2])
+    held[...] = kept_ref[...] + arrived[:count]
+    keep_ref[...] = held[: count // 2, :]
     gain_out_ref[...] = gain
-    for k, out in enumerate(outs):
-        piece = held[rows * (k + 1) : rows * (k + 2), :]
-        out[:rows, :] = piece.astype(jnp.bfloat16)
-        out[rows : rows + 1, :] = high
-        out[rows + 1 : rows + 2, :] = low
-
-
-def split_rows(rows, mine, theirs, gain, their_gain):
-    total, model = mine.shape
-    count = total // rows
-    f32, bf16 = jnp.float32, jnp.bfloat16
+    send_ref[: count // 2, :] = held[count // 2 :, :].astype(jnp.bfloat16)
+    send_ref[count // 2 : count // 2 + 1, :] = high_part(gain)
+    send_ref[count // 2 + 1 :, :] = low_part(gain)
+
+
+def fold(kept, gain, arrived, written):
+    count, model = kept.shape
     return pl.pallas_call(
-        functools.partial(split_kernel, rows),
+        fold_kernel,
         out_shape=(
-            jax.ShapeDtypeStruct((rows, model), f32),
-            jax.ShapeDtypeStruct((1, model), f32),
-        )
-        + (jax.ShapeDtypeStruct((rows + 2, model), bf16),) * (count - 1),
-        in_specs=[VMEM_SPEC] * 4,
-        out_specs=(VMEM_SPEC,) * (count + 1),
-        scratch_shapes=[pltpu.VMEM((total, model), f32)],
+            jax.ShapeDtypeStruct((count // 2, model), jnp.float32),
+            jax.ShapeDtypeStruct((1, model), jnp.float32),
+            jax.ShapeDtypeStruct((count // 2 + 2, model), jnp.bfloat16),
+        ),
+        in_specs=[VMEM_SPEC] * 3 + [ANY_SPEC],
+        out_specs=(VMEM_SPEC,) * 3,
+        scratch_shapes=[pltpu.VMEM((count, model), jnp.float32)],
         compiler_params=pltpu.CompilerParams(vmem_limit_bytes=8 * MIB),
-        name="split_rows",
-    )(mine, theirs, gain, their_gain)
+        name="fold",
+    )(kept, gain, arrived, written)
 
 
 def finish_kernel(rows, tokens_ref, incoming_ref, norm_gain_ref, own_ref, gain_ref, *refs):
@@ -348,21 +372,32 @@
     own_tokens, own_incoming = tokens.reshape(rows, model), cotangent.reshape(rows, model)
     gain_row = norm_gain.reshape(1, model)
 
-    piece = jnp.concatenate([own_tokens, own_incoming], axis=0)
-    pieces = [piece] + [exchange(piece, "tp", k) for k in range(1, tp_count)]
-    own = gather_rows(pieces, rows)
-    peer = exchange(own, "dp", 1)
-    packed, mine, theirs, gain_part, all_rows = hidden_pass(
-        own, peer, gain_row, gate_weight.T, up_weight.T, down_weight
+    held = jnp.concatenate([own_tokens, own_incoming], axis=0)
+    bits = tp_count // 2
+    while bits:
+        arrived = exchange(held, "tp", bits)
+        bits //= 2
+        kernel = join_kernel if bits else functools.partial(sort_kernel, rows)
+        held = stack_rows(kernel, held, arrived, "join_rows" if bits else "sort_rows")
+    peer = exchange(held, "dp", 1)
+    packed, kept, send, gain, all_rows = hidden_pass(
+        held, peer, gain_row, gate_weight.T, up_weight.T, down_weight
     )
     peer_packed = exchange(packed, "dp", 1)
-    from_peer, gain_from_peer = exchange(theirs, "dp", 1), exchange(gain_part, "dp", 1)
-    grads = weight_pass(place, packed, all_rows, ffw, False)
-    own_sum, gain_sum, *sends = split_rows(rows, mine, from_peer, gain_part, gain_from_peer)
-    received = [exchange(send, "tp", k + 1) for k, send in enumerate(sends)]
-    gate_t, up_t, down_grad = weight_pass(place, peer_packed, all_rows, ffw, True, grads)
+    arrived = exchange(send, "dp", 1)
+    *grads, written = weight_pass(place, packed, all_rows, ffw, False, 0, 2)
+    bits, part = 1, 1
+    while bits < tp_count:
+        kept, gain, send = fold(kept, gain, arrived, written)
+        arrived = exchange(send, "tp", bits)
+        source = packed if part < 2 else peer_packed
+        *grads, written = weight_pass(
+            place, source, all_rows, ffw, part >= 2, part % 2, 2, grads, (send,)
+        )
+        bits, part = bits * 2, part + 1
+    gate_t, up_t, down_grad = grads
     input_rows, gain_grad = finish(
-        rows, own_tokens, own_incoming, gain_row, own_sum, gain_sum, received
+        rows, own_tokens, own_incoming, gain_row, kept, gain, [arrived]
     )
     return (
         input_rows.reshape(tokens.shape),
@@ -379,7 +414,7 @@
     toks = tokens.shape[1] * tokens.shape[2] * tp_count * dp_count
     small = (
         dp_count == 2
-        and tp_count & (tp_count - 1) == 0
+        and tp_count == 8
         and toks == 32
         and model % 1024 == 0
         and ffw % 32 == 0

time: 61.5 us -> 60.8 us (0.989)
  starting transfers between devices: 24.5 us -> 14.3 us
  waiting for transfers between devices: 6.27 us -> 11.1 us
  Pallas kernels: 28.2 us -> 32.9 us
    ppermute x18 -> x9, starting transfers between devices: 24.5 us -> 14.3 us  [exchange(): return lax.ppermute(value, axis, [(i, i ^ bits) for i in range(count)])]
    ppermute x18 -> x9, waiting for transfers between devices: 6.27 us -> 11.1 us  [exchange(): return lax.ppermute(value, axis, [(i, i ^ bits) for i in range(count)])]
    pallas_call x4 -> x10, Pallas kernels: 12.3 us -> 16.9 us  [the longest x4 16.3 us: weight_pass(): pl.pallas_call(functools.partial(weight_kernel, toks, swapped, first), ou...]
  transfers between devices with their start and end apart: 18 -> 9, of which waited for: 7 -> 5; matrix products, arithmetic and copies ran while one was open for 0% -> 0% of each run, Pallas kernels for 20% -> 27%
where the time goes in v2:
time: 60.8 us; the launch traced here: 60.6 us
  Pallas kernels  32.9 us (54%)
  starting transfers between devices  14.3 us (24%)
  waiting for transfers between devices  11.1 us (18%)
  other arithmetic  0.79 us (1%)
  local copies, waits for them, and re-layouts  0.74 us (1%)
  between operations  0.7 us (1%)
    pallas_call x4, Pallas kernels, weight_pass(): pl.pallas_call(functools.partial(weight_kernel, toks, swapped, first), ou...  16.3 us
    pallas_call x1, Pallas kernels, hidden_pass(): pl.pallas_call(functools.partial(hidden_kernel, chunks), out_shape=(jax.S...  15.1 us
    ppermute x9, starting transfers between devices, exchange(): return lax.ppermute(value, axis, [(i, i ^ bits) for i in range(count)])  14.3 us
    ppermute x9, waiting for transfers between devices, exchange(): return lax.ppermute(value, axis, [(i, i ^ bits) for i in range(count)])  11.1 us
  transfers between devices with their start and end apart: 9, of which 5 were waited for; matrix products, arithmetic and copies ran while one was open for 0% of the time, Pallas kernels for 27%

profile of v2, /device:TPU:0, one launch (start us, length us, event | category | flops | bytes accessed | tf_op | source)
XLA Modules:
  0.0 60.6 jit_solution(7680787503289816127)
XLA Ops:
  0.6 0.8 %pad_maximum_fusion.first_ref = bf16[4,5120]{1,0:T(4,128)(2,1)S(1)} fusion(bf16[2,5120]{1,0:T(2,128)(2,1)} %bitcast.14, bf16[2,5120]{1,0:T(2,128)(2,1)} %bitcast.12), kind=kLoop, calls=%fused_computation | loop fusion | flops 81920 | bytes 81920 | tf_op jit(solution)/shard_map/concatenate | solution.py:375
  1.4 4.1 %collective-permute-start = (bf16[4,5120]{1,0:T(4,128)(2,1)S(1)}, bf16[4,5120]{1,0:T(4,128)(2,1)S(1)}, u32[]{:S(2)}, u32[]{:S(2)}) collective-permute-start(bf16[4,5120]{1,0:T(4,128)(2,1)S(1)} %pad_maximum_fusion.first_ref), channel_id=1, source_target_pairs={{0,8},{2,10},{4,12},{6,14},{8,0},{10,2},{12,4},{14,6},{1,9},{3,11}... | collective-permute-start | bytes 122888 | tf_op jit(solution)/shard_map/ppermute | solution.py:88
  5.5 2.4 %collective-permute-done.second_ref = bf16[4,5120]{1,0:T(4,128)(2,1)S(1)} collective-permute-done((bf16[4,5120]{1,0:T(4,128)(2,1)S(1)}, bf16[4,5120]{1,0:T(4,128)(2,1)S(1)}, u32[]{:S(2)}, u32[]{:S(2)}) %collective-permute-start) | collective-permute-done | bytes 40992 | tf_op jit(solution)/shard_map/ppermute | solution.py:88
  8.0 1.5 %collective-permute-start.1 = (bf16[8,5120]{1,0:T(8,128)(2,1)S(1)}, bf16[8,5120]{1,0:T(8,128)(2,1)S(1)}, u32[]{:S(2)}, u32[]{:S(2)}) collective-permute-start(bf16[8,5120]{1,0:T(8,128)(2,1)S(1)} %join_rows.2.first_ref), channel_id=1, source_target_pairs={{0,4},{2,6},{4,0},{6,2},{8,12},{10,14},{12,8},{14,10},{1,5},{3,7},... | collective-permute-start | bytes 245768 | tf_op jit(solution)/shard_map/ppermute | solution.py:88
  9.5 3.0 %collective-permute-done.1.second_ref = bf16[8,5120]{1,0:T(8,128)(2,1)S(1)} collective-permute-done((bf16[8,5120]{1,0:T(8,128)(2,1)S(1)}, bf16[8,5120]{1,0:T(8,128)(2,1)S(1)}, u32[]{:S(2)}, u32[]{:S(2)}) %collective-permute-start.1) | collective-permute-done | bytes 81952 | tf_op jit(solution)/shard_map/ppermute | solution.py:88
  12.5 1.8 %collective-permute-start.2 = (bf16[16,5120]{1,0:T(8,128)(2,1)S(1)}, bf16[16,5120]{1,0:T(8,128)(2,1)S(1)}, u32[]{:S(2)}, u32[]{:S(2)}) collective-permute-start(bf16[16,5120]{1,0:T(8,128)(2,1)S(1)} %join_rows.3.first_ref), channel_id=1, source_target_pairs={{0,2},{2,0},{4,6},{6,4},{8,10},{10,8},{12,14},{14,12},{1,3},{3,1},... | collective-permute-start | bytes 491528 | tf_op jit(solution)/shard_map/ppermute | solution.py:88
  14.3 3.6 %collective-permute-done.2.second_ref = bf16[16,5120]{1,0:T(8,128)(2,1)S(1)} collective-permute-done((bf16[16,5120]{1,0:T(8,128)(2,1)S(1)}, bf16[16,5120]{1,0:T(8,128)(2,1)S(1)}, u32[]{:S(2)}, u32[]{:S(2)}) %collective-permute-start.2) | collective-permute-done | bytes 163872 | tf_op jit(solution)/shard_map/ppermute | solution.py:88
  17.9 0.2 sort_rows.1.own_ref
  18.2 1.6 %collective-permute-done.3.peer_ref = bf16[32,5120]{1,0:T(8,128)(2,1)S(1)} collective-permute-done((bf16[32,5120]{1,0:T(8,128)(2,1)S(1)}, bf16[32,5120]{1,0:T(8,128)(2,1)S(1)}, u32[]{:S(2)}, u32[]{:S(2)}) %collective-permute-start.3) | collective-permute-done | bytes 327712 | tf_op jit(solution)/shard_map/ppermute | solution.py:88
  19.8 0.7 %copy-done = f32[5120]{0:T(1024)S(1)} copy-done((f32[5120]{0:T(1024)S(1)}, f32[5120]{0:T(1024)}, u32[]{:S(2)}) %copy-start) | copy-done | bytes 20504
  20.5 15.1 %hidden_pass.1 = (bf16[800,128]{1,0:T(8,128)(2,1)S(1)}, f32[16,5120]{1,0:T(8,128)S(1)}, bf16[18,5120]{1,0:T(8,128)(2,1)S(1)}, f32[1,5120]{1,0:T(1,128)S(1)}, bf16[64,5120]{1,0:T(8,128)(2,1)S(1)}) custom-call(bf16[32,5120]{1,0:T(8,128)(2,1)S(1)} %sort_rows.1.own_ref, bf16[32,5120]{1,0:T(8,128)(2,1)S(1)} %collective-permute-done.3.peer_ref, ...), custom_call_target="tpu_custom_call" | custom-call | flops 1310720000 | bytes 24576000 | tf_op jit(solution)/shard_map/hidden_pass/pallas_call | solution.py:232
  35.7 0.2 collective-permute-start.4
  35.8 0.4 collective-permute-start.7
  36.2 4.1 %weight_pass.4 = (bf16[1600,2560]{1,0:T(8,128)(2,1)}, bf16[1600,2560]{1,0:T(8,128)(2,1)}, bf16[1600,2560]{1,0:T(8,128)(2,1)}, f32[8,128]{1,0:T(8,128)S(1)}) custom-call(s32[1]{0:T(128)} %bitcast.5.place_ref, bf16[800,128]{1,0:T(8,128)(2,1)S(1)} %get-tuple-element.39.packed_ref, bf16[64,5120]{1,0:T(8,128)(2,1)S(1)} %get-tuple-element.40.rows_ref), custom_call_target="tpu_custom_call" | custom-call | flops 196608000 | bytes 6144000 | tf_op jit(solution)/shard_map/weight_pass/pallas_call | solution.py:285
  40.3 0.1 fold.3
  40.4 1.7 %collective-permute-start.5 = (bf16[10,5120]{1,0:T(8,128)(2,1)S(1)}, bf16[10,5120]{1,0:T(8,128)(2,1)S(1)}, u32[]{:S(2)}, u32[]{:S(2)}) collective-permute-start(bf16[10,5120]{1,0:T(8,128)(2,1)S(1)} %get-tuple-element.44.refs_3_), channel_id=1, source_target_pairs={{0,2},{2,0},{4,6},{6,4},{8,10},{10,8},{12,14},{14,12},{1,3},{3,1},... | collective-permute-start | bytes 307208 | tf_op jit(solution)/shard_map/ppermute | solution.py:88
  42.2 4.1 %weight_pass.5 = (bf16[1600,2560]{1,0:T(8,128)(2,1)}, bf16[1600,2560]{1,0:T(8,128)(2,1)}, bf16[1600,2560]{1,0:T(8,128)(2,1)}, f32[8,128]{1,0:T(8,128)S(1)}) custom-call(s32[1]{0:T(128)} %bitcast.5.place_ref, bf16[800,128]{1,0:T(8,128)(2,1)S(1)} %get-tuple-element.39.packed_ref, ...), custom_call_target="tpu_custom_call", output_to_operand_aliasing={{0}: (3, {}), {1}: (4, {}), {2}: (5, {})} | custom-call | flops 196608000 | bytes 6144000 | tf_op jit(solution)/shard_map/weight_pass/pallas_call | solution.py:285
  46.2 0.5 collective-permute-done.5.arrived_ref
  46.7 0.1 fold.4
  46.8 1.6 %collective-permute-start.6 = (bf16[6,5120]{1,0:T(8,128)(2,1)S(1)}, bf16[6,5120]{1,0:T(8,128)(2,1)S(1)}, u32[]{:S(2)}, u32[]{:S(2)}) collective-permute-start(bf16[6,5120]{1,0:T(8,128)(2,1)S(1)} %get-tuple-element.51.refs_3_), channel_id=1, source_target_pairs={{0,4},{2,6},{4,0},{6,2},{8,12},{10,14},{12,8},{14,10},{1,5},{3,7},... | collective-permute-start | bytes 184328 | tf_op jit(solution)/shard_map/ppermute | solution.py:88
  48.4 4.1 %weight_pass.6 = (bf16[1600,2560]{1,0:T(8,128)(2,1)}, bf16[1600,2560]{1,0:T(8,128)(2,1)}, bf16[1600,2560]{1,0:T(8,128)(2,1)}, f32[8,128]{1,0:T(8,128)S(1)}) custom-call(s32[1]{0:T(128)} %bitcast.5.place_ref, bf16[800,128]{1,0:T(8,128)(2,1)S(1)} %collective-permute-done.7.packed_ref, ...), custom_call_target="tpu_custom_call", output_to_operand_aliasing={{0}: (3, {}), {1}: (4, {}), {2}: (5, {})} | custom-call | flops 196608000 | bytes 6144000 | tf_op jit(solution)/shard_map/weight_pass/pallas_call | solution.py:285
  52.6 3.0 %collective-permute-start.8 = (bf16[4,5120]{1,0:T(4,128)(2,1)S(1)}, bf16[4,5120]{1,0:T(4,128)(2,1)S(1)}, u32[]{:S(2)}, u32[]{:S(2)}) collective-permute-start(bf16[4,5120]{1,0:T(4,128)(2,1)S(1)} %get-tuple-element.58.refs_3_), channel_id=1, source_target_pairs={{0,8},{2,10},{4,12},{6,14},{8,0},{10,2},{12,4},{14,6},{1,9},{3,11}... | collective-permute-start | bytes 122888 | tf_op jit(solution)/shard_map/ppermute | solution.py:88
  55.5 4.1 %weight_pass.7 = (bf16[1600,2560]{1,0:T(8,128)(2,1)}, bf16[1600,2560]{1,0:T(8,128)(2,1)}, bf16[1600,2560]{1,0:T(8,128)(2,1)}, f32[8,128]{1,0:T(8,128)}) custom-call(s32[1]{0:T(128)} %bitcast.5.place_ref, bf16[800,128]{1,0:T(8,128)(2,1)S(1)} %collective-permute-done.7.packed_ref, ...), custom_call_target="tpu_custom_call", output_to_operand_aliasing={{0}: (3, {}), {1}: (4, {}), {2}: (5, {})} | custom-call | flops 196608000 | bytes 6144000 | tf_op jit(solution)/shard_map/weight_pass/pallas_call | solution.py:285
  59.7 0.9 %finish.1 = (bf16[2,5120]{1,0:T(2,128)(2,1)}, f32[1,5120]{1,0:T(1,128)}) custom-call(bf16[2,5120]{1,0:T(2,128)(2,1)S(1)} %bitcast.13, bf16[2,5120]{1,0:T(2,128)(2,1)S(1)} %bitcast.15, f32[1,5120]{1,0:T(1,128)S(1)} %bitcast.11, f32[2,5120]{1,0:T(2,128)S(1)} %get-tuple-element.56.own_ref, f32[1,5120]{1,0:T(1,128)S(1)} %get-tuple-element.57.gain_ref, ...), custom_call_target="tpu_custom_call" | custom-call | tf_op jit(solution)/shard_map/finish/pallas_call | solution.py:354
  (15 shorter events, 0.2 us)
Async XLA Ops:
  1.4 6.5 %collective-permute-start = (bf16[4,5120]{1,0:T(4,128)(2,1)S(1)}, bf16[4,5120]{1,0:T(4,128)(2,1)S(1)}, u32[]{:S(2)}, u32[]{:S(2)}) collective-permute-start(bf16[4,5120]{1,0:T(4,128)(2,1)S(1)} %pad_maximum_fusion.first_ref), channel_id=1, source_target_pairs={{0,8},{2,10},{4,12},{6,14},{8,0},{10,2},{12,4},{14,6},{1,9},{3,11}... | collective-permute-start | bytes 122888 | tf_op jit(solution)/shard_map/ppermute | solution.py:88
  8.0 4.5 %collective-permute-start.1 = (bf16[8,5120]{1,0:T(8,128)(2,1)S(1)}, bf16[8,5120]{1,0:T(8,128)(2,1)S(1)}, u32[]{:S(2)}, u32[]{:S(2)}) collective-permute-start(bf16[8,5120]{1,0:T(8,128)(2,1)S(1)} %join_rows.2.first_ref), channel_id=1, source_target_pairs={{0,4},{2,6},{4,0},{6,2},{8,12},{10,14},{12,8},{14,10},{1,5},{3,7},... | collective-permute-start | bytes 245768 | tf_op jit(solution)/shard_map/ppermute | solution.py:88
  12.5 5.4 %collective-permute-start.2 = (bf16[16,5120]{1,0:T(8,128)(2,1)S(1)}, bf16[16,5120]{1,0:T(8,128)(2,1)S(1)}, u32[]{:S(2)}, u32[]{:S(2)}) collective-permute-start(bf16[16,5120]{1,0:T(8,128)(2,1)S(1)} %join_rows.3.first_ref), channel_id=1, source_target_pairs={{0,2},{2,0},{4,6},{6,4},{8,10},{10,8},{12,14},{14,12},{1,3},{3,1},... | collective-permute-start | bytes 491528 | tf_op jit(solution)/shard_map/ppermute | solution.py:88
  18.1 1.7 %collective-permute-start.3 = (bf16[32,5120]{1,0:T(8,128)(2,1)S(1)}, bf16[32,5120]{1,0:T(8,128)(2,1)S(1)}, u32[]{:S(2)}, u32[]{:S(2)}) collective-permute-start(bf16[32,5120]{1,0:T(8,128)(2,1)S(1)} %sort_rows.1.own_ref), channel_id=1, source_target_pairs={{0,1},{1,0},{2,3},{3,2},{4,5},{5,4},{6,7},{7,6},{8,9},{9,8},{10,11... | collective-permute-start | bytes 983048 | tf_op jit(solution)/shard_map/ppermute | solution.py:88
  19.8 0.7 %copy-start = (f32[5120]{0:T(1024)S(1)}, f32[5120]{0:T(1024)}, u32[]{:S(2)}) copy-start(f32[5120]{0:T(1024)} %param.7) | copy-start | bytes 61444
  35.7 4.6 %collective-permute-start.4 = (bf16[18,5120]{1,0:T(8,128)(2,1)S(1)}, bf16[18,5120]{1,0:T(8,128)(2,1)S(1)}, u32[]{:S(2)}, u32[]{:S(2)}) collective-permute-start(bf16[18,5120]{1,0:T(8,128)(2,1)S(1)} %get-tuple-element.38), channel_id=1, source_target_pairs={{0,1},{1,0},{2,3},{3,2},{4,5},{5,4},{6,7},{7,6},{8,9},{9,8},{10,11... | collective-permute-start | bytes 552968 | tf_op jit(solution)/shard_map/ppermute | solution.py:88
  35.8 12.6 %collective-permute-start.7 = (bf16[800,128]{1,0:T(8,128)(2,1)S(1)}, bf16[800,128]{1,0:T(8,128)(2,1)S(1)}, u32[]{:S(2)}, u32[]{:S(2)}) collective-permute-start(bf16[800,128]{1,0:T(8,128)(2,1)S(1)} %get-tuple-element.39.packed_ref), channel_id=1, source_target_pairs={{0,1},{1,0},{2,3},{3,2},{4,5},{5,4},{6,7},{7,6},{8,9},{9,8},{10,11... | collective-permute-start | bytes 614408 | tf_op jit(solution)/shard_map/ppermute | solution.py:88
  40.4 6.3 %collective-permute-start.5 = (bf16[10,5120]{1,0:T(8,128)(2,1)S(1)}, bf16[10,5120]{1,0:T(8,128)(2,1)S(1)}, u32[]{:S(2)}, u32[]{:S(2)}) collective-permute-start(bf16[10,5120]{1,0:T(8,128)(2,1)S(1)} %get-tuple-element.44.refs_3_), channel_id=1, source_target_pairs={{0,2},{2,0},{4,6},{6,4},{8,10},{10,8},{12,14},{14,12},{1,3},{3,1},... | collective-permute-start | bytes 307208 | tf_op jit(solution)/shard_map/ppermute | solution.py:88
  46.8 5.6 %collective-permute-start.6 = (bf16[6,5120]{1,0:T(8,128)(2,1)S(1)}, bf16[6,5120]{1,0:T(8,128)(2,1)S(1)}, u32[]{:S(2)}, u32[]{:S(2)}) collective-permute-start(bf16[6,5120]{1,0:T(8,128)(2,1)S(1)} %get-tuple-element.51.refs_3_), channel_id=1, source_target_pairs={{0,4},{2,6},{4,0},{6,2},{8,12},{10,14},{12,8},{14,10},{1,5},{3,7},... | collective-permute-start | bytes 184328 | tf_op jit(solution)/shard_map/ppermute | solution.py:88
  52.6 7.1 %collective-permute-start.8 = (bf16[4,5120]{1,0:T(4,128)(2,1)S(1)}, bf16[4,5120]{1,0:T(4,128)(2,1)S(1)}, u32[]{:S(2)}, u32[]{:S(2)}) collective-permute-start(bf16[4,5120]{1,0:T(4,128)(2,1)S(1)} %get-tuple-element.58.refs_3_), channel_id=1, source_target_pairs={{0,8},{2,10},{4,12},{6,14},{8,0},{10,2},{12,4},{14,6},{1,9},{3,11}... | collective-permute-start | bytes 122888 | tf_op jit(solution)/shard_map/ppermute | solution.py:88
  55.5 4.1 %copy-start.1 = (f32[5120]{0:T(1024)S(1)}, f32[5120]{0:T(1024)}, u32[]{:S(2)}) copy-start(f32[5120]{0:T(1024)} %param.7) | copy-start | bytes 61444
  55.5 4.1 %copy-start.2 = (bf16[1,2,1,5120]{3,1,2,0:T(2,128)(2,1)S(1)}, bf16[1,2,1,5120]{3,1,2,0:T(2,128)(2,1)}, u32[]{:S(2)}) copy-start(bf16[1,2,1,5120]{3,1,2,0:T(2,128)(2,1)} %param.6) | copy-start | bytes 61444
  55.5 4.1 %copy-start.3 = (bf16[1,2,1,5120]{3,1,2,0:T(2,128)(2,1)S(1)}, bf16[1,2,1,5120]{3,1,2,0:T(2,128)(2,1)}, u32[]{:S(2)}) copy-start(bf16[1,2,1,5120]{3,1,2,0:T(2,128)(2,1)} %param.11) | copy-start | bytes 61444

commit v3 on v1

v3 whole, which is shorter than its diff:
```python
import functools

import jax
import jax.numpy as jnp
from jax import lax
from jax.experimental import pallas as pl
from jax.experimental.pallas import tpu as pltpu
from jax.sharding import PartitionSpec as P

EPSILON = 1e-06
LANES = 128
MIB = 1 << 20
CHUNK = 512
BLOCK = 256
ALONG_Z = (2, 4, 6)


def contract(left, right, left_dim, right_dim):
    return lax.dot_general(
        left, right, (((left_dim,), (right_dim,)), ((), ())), preferred_element_type=jnp.float32
    )


def norm_tokens(values_in, norm_gain):
    values = values_in.astype(jnp.float32)
    inverse = lax.rsqrt(jnp.mean(values * values, axis=-1, keepdims=True) + EPSILON)
    scaled = values * inverse
    return (scaled, inverse, (scaled * norm_gain).astype(jnp.bfloat16))


def local_pass(normed_all, grads_all, gate_weight, up_weight, down_weight):
    gate_value = jnp.dot(normed_all, gate_weight, preferred_element_type=jnp.float32)
    up_value = jnp.dot(normed_all, up_weight, preferred_element_type=jnp.float32)
    sigmoid_gate = jax.nn.sigmoid(gate_value)
    active = gate_value * sigmoid_gate
    hidden = (active * up_value).astype(jnp.bfloat16)
    grad_hidden = contract(grads_all, down_weight, 1, 1)
    grad_gate = (
        grad_hidden * up_value * sigmoid_gate * (1.0 + gate_value * (1.0 - sigmoid_gate))
    ).astype(jnp.bfloat16)
    grad_up = (grad_hidden * active).astype(jnp.bfloat16)
    partial_value = contract(grad_gate, gate_weight, 1, 1) + contract(grad_up, up_weight, 1, 1)
    gate_term = contract(normed_all, grad_gate, 0, 0)
    up_term = contract(normed_all, grad_up, 0, 0)
    down_term = contract(hidden, grads_all, 0, 0)
    return (partial_value, gate_term, up_term, down_term)


def general_body(tokens, norm_gain, gate_weight, up_weight, down_weight, cotangent):
    micro_count, own_tokens, model_width = (tokens.shape[1], tokens.shape[2], tokens.shape[3])
    tp_count = lax.axis_size("tp")
    scaled, inverse, normed = norm_tokens(tokens[0], norm_gain)
    normed_all, grads_all = (
        lax.all_gather(normed, "tp", axis=1, tiled=True),
        lax.all_gather(cotangent[0], "tp", axis=1, tiled=True),
    )
    partial_value, gate_term, up_term, down_term = local_pass(
        normed_all.reshape(-1, model_width),
        grads_all.reshape(-1, model_width),
        gate_weight,
        up_weight,
        down_weight,
    )
    pieces = lax.all_to_all(
        partial_value.reshape(micro_count, tp_count, own_tokens, model_width),
        "tp",
        split_axis=1,
        concat_axis=1,
        tiled=True,
    )
    grad_normed = jnp.sum(pieces, axis=1)
    grad_scaled = grad_normed * norm_gain
    projected = jnp.mean(grad_scaled * scaled, axis=-1, keepdims=True)
    input_rows = cotangent[0].astype(jnp.float32) + inverse * (grad_scaled - scaled * projected)
    gain_term = jnp.sum((grad_normed * scaled).reshape(-1, model_width), axis=0)
    gain_grad = lax.psum(gain_term, ("tp", "dp"))
    gate_grad, up_grad, down_grad = (
        lax.psum_scatter(gate_term.astype(jnp.bfloat16), "dp", scatter_dimension=0, tiled=True),
        lax.psum_scatter(up_term.astype(jnp.bfloat16), "dp", scatter_dimension=0, tiled=True),
        lax.psum_scatter(down_term.astype(jnp.bfloat16), "dp", scatter_dimension=1, tiled=True),
    )
    return (input_rows.astype(jnp.bfloat16)[None], gain_grad, gate_grad, up_grad, down_grad)


VMEM_SPEC = pl.BlockSpec(memory_space=pltpu.VMEM)
ANY_SPEC = pl.BlockSpec(memory_space=pl.ANY)


def exchange(value, axis, bits):
    count = lax.axis_size(axis)
    return lax.ppermute(value, axis, [(i, i ^ bits) for i in range(count)])


def high_part(value):
    return value.astype(jnp.bfloat16)


def low_part(value):
    return (value - value.astype(jnp.bfloat16).astype(jnp.float32)).astype(jnp.bfloat16)


def relay_kernel(*refs):
    count = len(refs) // 2
    for source, target in zip(refs[:count], refs[count + 1 :]):
        target[...] = source[...]


def relay(pieces, fetched):
    return pl.pallas_call(
        relay_kernel,
        out_shape=tuple(jax.ShapeDtypeStruct(piece.shape, piece.dtype) for piece in pieces),
        in_specs=[VMEM_SPEC] * len(pieces) + [ANY_SPEC],
        out_specs=(VMEM_SPEC,) * len(pieces),
        compiler_params=pltpu.CompilerParams(vmem_limit_bytes=4 * MIB),
        name="relay",
    )(*pieces, fetched)


def sort_kernel(rows, *refs):
    pieces, out_ref, held = refs[:-3], refs[-2], refs[-1]
    count = len(pieces)
    for k, piece in enumerate(pieces):
        value = piece[...].astype(jnp.float32)
        held[rows * k : rows * (k + 1), :] = value[:rows]
        held[rows * (count + k) : rows * (count + k + 1), :] = value[rows:]
    out_ref[...] = held[...].astype(jnp.bfloat16)


def sort_rows(rows, pieces, fetched):
    shape = (2 * rows * len(pieces), pieces[0].shape[1])
    return pl.pallas_call(
        functools.partial(sort_kernel, rows),
        out_shape=jax.ShapeDtypeStruct(shape, jnp.bfloat16),
        in_specs=[VMEM_SPEC] * len(pieces) + [ANY_SPEC],
        out_specs=VMEM_SPEC,
        scratch_shapes=[pltpu.VMEM(shape, jnp.float32)],
        compiler_params=pltpu.CompilerParams(vmem_limit_bytes=8 * MIB),
        name="sort_rows",
    )(*pieces, fetched)


def fetch_kernel(first, *refs):
    sources, gain_hbm = refs[:3], refs[3]
    targets, gain_ref, done_ref, sems, gain_sem = refs[-7:-4], *refs[-4:]
    chunks, half, width = targets[0].shape
    top = pl.multiple_of(lax.axis_index("dp") * half, 16)
    copies = [pltpu.make_async_copy(gain_hbm, gain_ref, gain_sem)]
    for c in range(chunks):
        at = slice((first + c) * width, (first + c + 1) * width)
        for w, (source, target) in enumerate(zip(sources, targets)):
            block = source.at[pl.ds(top, half), at]
            copies.append(pltpu.make_async_copy(block, target.at[c], sems.at[w, c]))
    for copy in copies:
        copy.start()
    done_ref[...] = jnp.zeros_like(done_ref)
    for copy in copies:
        copy.wait()


def fetch_weights(weights, gain, first, chunks, width, after=()):
    ffw = weights[0].shape[0]
    fixed = [pltpu.with_memory_space_constraint(x, pltpu.HBM) for x in (*weights, gain)]
    *fetched, gain, done = pl.pallas_call(
        functools.partial(fetch_kernel, first),
        out_shape=(pltpu.VMEM((chunks, ffw // 2, width), jnp.bfloat16),) * 3
        + (pltpu.VMEM(gain.shape, gain.dtype), pltpu.VMEM((8, LANES), jnp.float32)),
        in_specs=[ANY_SPEC] * (4 + len(after)),
        out_specs=(VMEM_SPEC,) * 5,
        scratch_shapes=[pltpu.SemaphoreType.DMA((3, chunks)), pltpu.SemaphoreType.DMA(())],
        compiler_params=pltpu.CompilerParams(vmem_limit_bytes=4 * MIB),
        cost_estimate=pl.CostEstimate(
            flops=0, bytes_accessed=3 * ffw * chunks * width, transcendentals=0
        ),
        name="fetch_weights",
    )(*fixed, *after)
    return fetched, gain, done


def hidden_kernel(
    parts, own_ref, peer_ref, gain_ref, *refs
):
    weights, refs = refs[: 3 * parts], refs[3 * parts :]
    (packed_ref, mine_ref, theirs_ref, gain_part_ref, rows_ref,
     x_buf, c_buf, inverse_buf, acc_g, acc_u, acc_h, left_buf) = refs
    half = acc_g.shape[0]
    chunks, toks, width = x_buf.shape
    each = toks // 2
    part_chunks = chunks // parts

    squares = jnp.zeros((toks, 1), jnp.float32)
    for c in range(chunks):
        at = slice(c * width, (c + 1) * width)
        value = jnp.concatenate([own_ref[:each, at], peer_ref[:each, at]], axis=0)
        value = value.astype(jnp.float32)
        squares = squares + jnp.sum(value * value, axis=-1, keepdims=True)
    inverse = lax.rsqrt(squares / (chunks * width) + EPSILON)
    inverse_buf[...] = jnp.broadcast_to(inverse, inverse_buf.shape)
    for c in range(chunks):
        at = slice(c * width, (c + 1) * width)
        value = jnp.concatenate([own_ref[:each, at], peer_ref[:each, at]], axis=0)
        normed = (value.astype(jnp.float32) * inverse * gain_ref[:, at]).astype(jnp.bfloat16)
        incoming = jnp.concatenate([own_ref[each:, at], peer_ref[each:, at]], axis=0)
        x_buf[c] = normed
        c_buf[c] = incoming
        rows_ref[:toks, at] = normed
        rows_ref[toks:, at] = incoming
    acc_g[...] = jnp.zeros_like(acc_g)
    acc_u[...] = jnp.zeros_like(acc_u)
    acc_h[...] = jnp.zeros_like(acc_h)

    for part in range(parts):
        gate_buf, up_buf, down_buf = weights[3 * part : 3 * part + 3]

        def forward(c, carry):
            at = part * part_chunks + c
            acc_g[...] += contract(gate_buf[c], x_buf[at], 1, 1)
            acc_u[...] += contract(up_buf[c], x_buf[at], 1, 1)
            acc_h[...] += contract(down_buf[c], c_buf[at], 1, 1)
            return carry

        lax.fori_loop(0, part_chunks, forward, 0)

    step = 80 if half % 80 == 0 else 16

    def pointwise(i, carry):
        at = pl.ds(pl.multiple_of(i * step, 16), step)
        gate, up, grad = acc_g[at, :], acc_u[at, :], acc_h[at, :]
        sigmoid = jax.nn.sigmoid(gate)
        active = gate * sigmoid
        grad_gate = grad * up * sigmoid * (1.0 + gate * (1.0 - sigmoid))
        parts = [grad_gate, grad * active, active * up, jnp.zeros_like(active)]
        packed_ref[at, :] = jnp.concatenate(parts, axis=1).astype(jnp.bfloat16)
        return carry

    lax.fori_loop(0, half // step, pointwise, 0)
    left_buf[...] = packed_ref[...].astype(jnp.float32).T.astype(jnp.bfloat16)

    for part in range(parts):
        gate_buf, up_buf = weights[3 * part : 3 * part + 2]

        def backward(c, carry):
            at = pl.ds(pl.multiple_of((part * part_chunks + c) * width, LANES), width)
            total = jnp.dot(left_buf[:toks, :], gate_buf[c], preferred_element_type=jnp.float32)
            total += jnp.dot(
                left_buf[toks : 2 * toks, :], up_buf[c], preferred_element_type=jnp.float32
            )
            value = jnp.concatenate([own_ref[:each, at], peer_ref[:each, at]], axis=0)
            scaled = value.astype(jnp.float32) * inverse_buf[:, :1]
            gain = jnp.sum(total * scaled, axis=0, keepdims=True)
            gain_part_ref[:, at] = gain
            mine_ref[:, at] = total[:each]
            theirs_ref[:each, at] = total[each:].astype(jnp.bfloat16)
            theirs_ref[each : each + 1, at] = high_part(gain)
            theirs_ref[each + 1 : each + 2, at] = low_part(gain)
            return carry

        lax.fori_loop(0, part_chunks, backward, 0)


def hidden_pass(own, peer, gain, fetched):
    toks, model = own.shape
    each, parts = toks // 2, len(fetched)
    part_chunks, half, width = fetched[0][0].shape
    small = pltpu.VMEM((parts * part_chunks, toks, width), jnp.bfloat16)
    acc = pltpu.VMEM((half, toks), jnp.float32)
    weights = [pltpu.with_memory_space_constraint(w, pltpu.VMEM) for part in fetched for w in part]
    return pl.pallas_call(
        functools.partial(hidden_kernel, parts),
        out_shape=(
            jax.ShapeDtypeStruct((half, LANES), jnp.bfloat16),
            jax.ShapeDtypeStruct((each, model), jnp.float32),
            jax.ShapeDtypeStruct((each + 2, model), jnp.bfloat16),
            jax.ShapeDtypeStruct((1, model), jnp.float32),
            jax.ShapeDtypeStruct((2 * toks, model), jnp.bfloat16),
        ),
        in_specs=[VMEM_SPEC] * (3 + len(weights)),
        out_specs=(VMEM_SPEC,) * 5,
        scratch_shapes=[
            small, small, pltpu.VMEM((toks, LANES), jnp.float32), acc, acc, acc,
            pltpu.VMEM((LANES, half), jnp.bfloat16),
        ],
        compiler_params=pltpu.CompilerParams(vmem_limit_bytes=16 * MIB),
        cost_estimate=pl.CostEstimate(
            flops=10 * toks * half * model, bytes_accessed=6 * half * model, transcendentals=half * toks
        ),
        name="hidden_pass",
    )(own, peer, gain, *weights)


def weight_kernel(toks, spans, packs, *refs):
    rows_ref, refs = refs[packs], refs[:packs] + refs[packs + 1 :]
    outs, written_ref, buf, sems = refs[-6:-3], refs[-3], refs[-2], refs[-1]
    slots, _, half, width = buf.shape
    each = toks // 2
    place = lax.axis_index("dp")
    own_width = rows_ref.shape[1] // 2
    written_ref[...] = jnp.zeros_like(written_ref)

    def copy(k, slot, row, block):
        at = pl.ds(pl.multiple_of(block * width, LANES), width)
        target = outs[k].at[pl.ds(pl.multiple_of(row, 16), half), at]
        return pltpu.make_async_copy(buf.at[slot, k], target, sems.at[slot, k])

    done = 0
    for packed_ref, (swapped, first, last) in zip(refs[:packs], spans):
        row = (1 - place) * half if swapped else place * half

        def step(i, carry, packed_ref=packed_ref, swapped=swapped, row=row, base=done - first):
            slot = lax.rem(base + i, slots)

            @pl.when(base + i >= slots)
            def _():
                for k in range(3):
                    copy(k, slot, row, i).wait()

            at = pl.ds(pl.multiple_of(place * own_width + i * width, LANES), width)
            normed, incoming = rows_ref[:toks, at], rows_ref[toks:, at]
            if swapped:
                normed = jnp.concatenate([normed[each:], normed[:each]], axis=0)
                incoming = jnp.concatenate([incoming[each:], incoming[:each]], axis=0)
            for k, right in enumerate((normed, normed, incoming)):
                left = packed_ref[:, k * toks : (k + 1) * toks]
                value = jnp.dot(left, right, preferred_element_type=jnp.float32)
                buf[slot, k] = value.astype(jnp.bfloat16)
                copy(k, slot, row, i).start()
            return carry

        lax.fori_loop(first, last, step, 0)
        done += last - first
    for slot in range(min(slots, done)):
        for k in range(3):
            copy(k, slot, place * half, 0).wait()


def weight_pass(packs, rows, ffw, spans, before=(), after=()):
    half, toks, model = packs[0].shape[0], rows.shape[0] // 2, rows.shape[1]
    own_width = model // 2
    blocks = sum(last - first for _, first, last in spans)
    out = jax.ShapeDtypeStruct((ffw, own_width), jnp.bfloat16)
    return pl.pallas_call(
        functools.partial(weight_kernel, toks, spans, len(packs)),
        out_shape=(out,) * 3 + (jax.ShapeDtypeStruct((8, LANES), jnp.float32),),
        in_specs=[VMEM_SPEC] * (len(packs) + 1) + [ANY_SPEC] * (len(before) + len(after)),
        out_specs=(ANY_SPEC,) * 3 + (VMEM_SPEC,),
        scratch_shapes=[
            pltpu.VMEM((3, 3, half, BLOCK), jnp.bfloat16),
            pltpu.SemaphoreType.DMA((3, 3)),
        ],
        input_output_aliases={len(packs) + 1 + i: i for i in range(len(before))},
        compiler_params=pltpu.CompilerParams(vmem_limit_bytes=16 * MIB),
        cost_estimate=pl.CostEstimate(
            flops=6 * toks * half * BLOCK * blocks,
            bytes_accessed=6 * half * BLOCK * blocks,
            transcendentals=0,
        ),
        name="weight_pass",
    )(*packs, rows, *before, *after)


def add_arrived(kept_ref, gain_ref, arrived, extra, held, gain_out_ref):
    gain = gain_ref[...] + (extra[0:1] + extra[1:2])
    held[...] = kept_ref[...] + arrived
    gain_out_ref[...] = gain
    return gain


def fold_kernel(
    kept_ref, gain_ref, arrived_ref, _, keep_ref, gain_out_ref, send_ref, send_gain_ref, held
):
    count = kept_ref.shape[0]
    arrived = arrived_ref[...].astype(jnp.float32)
    gain = add_arrived(kept_ref, gain_ref, arrived[:count], arrived[count:], held, gain_out_ref)
    keep_ref[...] = held[: count // 2, :]
    send_ref[...] = held[count // 2 :, :].astype(jnp.bfloat16)
    send_gain_ref[:1, :] = high_part(gain)
    send_gain_ref[1:, :] = low_part(gain)


def spread_kernel(rows, kept_ref, gain_ref, arrived_ref, extra_ref, _, own_ref, gain_out_ref, *refs):
    outs, held = refs[:-1], refs[-1]
    arrived, extra = arrived_ref[...].astype(jnp.float32), extra_ref[...].astype(jnp.float32)
    gain = add_arrived(kept_ref, gain_ref, arrived, extra, held, gain_out_ref)
    own_ref[...] = held[:rows, :]
    for k, out in enumerate(outs):
        out[:rows, :] = held[rows * (k + 1) : rows * (k + 2), :].astype(jnp.bfloat16)
        out[rows : rows + 1, :] = high_part(gain)
        out[rows + 1 :, :] = low_part(gain)


def add_rows(kernel, kept, gain, arrived, written, kept_rows, sent_rows, name):
    count, model = kept.shape
    return pl.pallas_call(
        kernel,
        out_shape=(
            jax.ShapeDtypeStruct((kept_rows, model), jnp.float32),
            jax.ShapeDtypeStruct((1, model), jnp.float32),
        )
        + tuple(jax.ShapeDtypeStruct((n, model), jnp.bfloat16) for n in sent_rows),
        in_specs=[VMEM_SPEC] * (2 + len(arrived)) + [ANY_SPEC],
        out_specs=(VMEM_SPEC,) * (2 + len(sent_rows)),
        scratch_shapes=[pltpu.VMEM((count, model), jnp.float32)],
        compiler_params=pltpu.CompilerParams(vmem_limit_bytes=8 * MIB),
        name=name,
    )(kept, gain, *arrived, written)


def finish_kernel(rows, tokens_ref, incoming_ref, norm_gain_ref, own_ref, gain_ref, *refs):
    pieces, input_ref, gain_out_ref = refs[:-2], refs[-2], refs[-1]
    grad_normed, gain = own_ref[...], gain_ref[...]
    for piece in pieces:
        value = piece[...].astype(jnp.float32)
        grad_normed = grad_normed + value[:rows]
        gain = gain + (value[rows : rows + 1] + value[rows + 1 : rows + 2])
    gain_out_ref[...] = gain
    values = tokens_ref[...].astype(jnp.float32)
    inverse = lax.rsqrt(jnp.mean(values * values, axis=-1, keepdims=True) + EPSILON)
    scaled = values * inverse
    grad_scaled = grad_normed * norm_gain_ref[...]
    projected = jnp.mean(grad_scaled * scaled, axis=-1, keepdims=True)
    result = incoming_ref[...].astype(jnp.float32) + inverse * (grad_scaled - scaled * projected)
    input_ref[...] = result.astype(jnp.bfloat16)


def finish(rows, tokens, incoming, norm_gain, own, gain, pieces):
    model = tokens.shape[1]
    return pl.pallas_call(
        functools.partial(finish_kernel, rows),
        out_shape=(
            jax.ShapeDtypeStruct((rows, model), jnp.bfloat16),
            jax.ShapeDtypeStruct((1, model), jnp.float32),
        ),
        in_specs=[VMEM_SPEC] * (5 + len(pieces)),
        out_specs=(VMEM_SPEC,) * 2,
        compiler_params=pltpu.CompilerParams(vmem_limit_bytes=8 * MIB),
        name="finish",
    )(tokens, incoming, norm_gain, own, gain, *pieces)


def small_body(tokens, norm_gain, gate_weight, up_weight, down_weight, cotangent):
    rows, model = tokens.shape[1] * tokens.shape[2], tokens.shape[3]
    ffw = down_weight.shape[0]
    tp_count = lax.axis_size("tp")
    own_tokens, own_incoming = tokens.reshape(rows, model), cotangent.reshape(rows, model)
    gain_hbm = norm_gain.reshape(1, model)

    weights = (gate_weight.T, up_weight.T, down_weight)
    chunks = model // CHUNK
    piece = jnp.concatenate([own_tokens, own_incoming], axis=0)
    near = exchange(piece, "tp", 1)
    along = [exchange(piece, "tp", bits) for bits in ALONG_Z]
    fetched, gain_row, done = fetch_weights(weights, gain_hbm, 0, chunks // 2, CHUNK, (piece,))
    along = relay(along, done)
    across = [exchange(arrived, "tp", 1) for arrived in along]
    more, _, done = fetch_weights(
        weights, gain_hbm, chunks // 2, chunks - chunks // 2, CHUNK, (along[0],)
    )
    fetched = [fetched, more]
    own = sort_rows(rows, [piece, *along, near, *across], done)
    peer = exchange(own, "dp", 1)
    packed, kept, send, gain, all_rows = hidden_pass(own, peer, gain_row, fetched)
    arrived = exchange(send, "dp", 1)
    peer_packed = exchange(packed, "dp", 1)
    blocks = model // 2 // BLOCK
    cut = blocks // 2
    *grads, written = weight_pass([packed], all_rows, ffw, [(False, 0, cut)])
    kept, gain, send, send_gain = add_rows(
        fold_kernel, kept, gain, [arrived], written, kept.shape[0] // 2, (kept.shape[0] // 2, 2), "fold"
    )
    arrived = [exchange(send, "tp", 1), exchange(send_gain, "tp", 1)]
    *grads, written = weight_pass(
        [packed, peer_packed], all_rows, ffw, [(False, cut, blocks), (True, 0, 2)], grads, (send,)
    )
    kept, gain, *sends = add_rows(
        functools.partial(spread_kernel, rows), kept, gain, arrived, written, rows, (rows + 2,) * 3,
        "spread",
    )
    arrived = [exchange(send, "tp", bits) for send, bits in zip(sends, ALONG_Z)]
    gate_t, up_t, down_grad, _ = weight_pass(
        [peer_packed], all_rows, ffw, [(True, 2, blocks)], grads, (sends[0],)
    )
    input_rows, gain_grad = finish(
        rows, own_tokens, own_incoming, gain_row, kept, gain, arrived
    )
    return (
        input_rows.reshape(tokens.shape),
        gain_grad.reshape(model),
        gate_t.T,
        up_t.T,
        down_grad,
    )


def body(tokens, norm_gain, gate_weight, up_weight, down_weight, cotangent):
    tp_count, dp_count = lax.axis_size("tp"), lax.axis_size("dp")
    ffw, model = down_weight.shape
    toks = tokens.shape[1] * tokens.shape[2] * tp_count * dp_count
    small = (
        dp_count == 2
        and tp_count == 8
        and toks == 32
        and model % 1024 == 0
        and ffw % 32 == 0
        and 3 * ffw * model <= 40 * MIB
    )
    chosen = small_body if small else general_body
    return chosen(tokens, norm_gain, gate_weight, up_weight, down_weight, cotangent)


def solution(mesh):
    placed = (
        P(("groups", "dp"), None, "tp", None),
        P(),
        P(None, "tp"),
        P(None, "tp"),
        P("tp", None),
        P(("groups", "dp"), None, "tp", None),
    )
    return jax.shard_map(
        body,
        mesh=mesh,
        in_specs=placed,
        out_specs=(
            P(("groups", "dp"), None, "tp", None),
            P("groups"),
            P(("groups", "dp"), "tp"),
            P(("groups", "dp"), "tp"),
            P("tp", ("groups", "dp")),
        ),
        check_vma=False,
    )
```

time: 61.5 us -> 59.1 us (0.961)
  Pallas kernels: 28.2 us -> 38.6 us
  starting transfers between devices: 24.5 us -> 17 us
  waiting for transfers between devices: 6.27 us -> 1.65 us
  local copies, waits for them, and re-layouts: 0.74 us -> 0.01 us
    pallas_call x5 -> x10, Pallas kernels: 27.3 us -> 37.7 us  [the longest x3 13.6 us: weight_pass(): pl.pallas_call(functools.partial(weight_kernel, toks, spans, len(packs)),...]
    ppermute x18 -> x15, starting transfers between devices: 24.5 us -> 17 us  [exchange(): return lax.ppermute(value, axis, [(i, i ^ bits) for i in range(count)])]
    ppermute x18 -> x15, waiting for transfers between devices: 6.27 us -> 1.65 us  [exchange(): return lax.ppermute(value, axis, [(i, i ^ bits) for i in range(count)])]
    unnamed x8 -> x4, local copies, waits for them, and re-layouts: 0.74 us -> 0.01 us
  transfers between devices with their start and end apart: 18 -> 15, of which waited for: 7 -> 1; matrix products, arithmetic and copies ran while one was open for 0% -> 0% of each run, Pallas kernels for 20% -> 41%
where the time goes in v3:
time: 59.1 us; the launch traced here: 58.9 us
  Pallas kernels  38.6 us (65%)
  starting transfers between devices  17 us (29%)
  waiting for transfers between devices  1.65 us (3%)
  between operations  0.84 us (1%)
  other arithmetic  0.79 us (1%)
    ppermute x15, starting transfers between devices, exchange(): return lax.ppermute(value, axis, [(i, i ^ bits) for i in range(count)])  17 us
    pallas_call x3, Pallas kernels, weight_pass(): pl.pallas_call(functools.partial(weight_kernel, toks, spans, len(packs)),...  13.6 us
    pallas_call x1, Pallas kernels, hidden_pass(): pl.pallas_call(functools.partial(hidden_kernel, parts), out_shape=(jax.Sh...  13.5 us
    pallas_call x2, Pallas kernels, fetch_weights(): pl.pallas_call(functools.partial(fetch_kernel, first), out_shape=(pltpu.V...  10.1 us
    ppermute x15, waiting for transfers between devices, exchange(): return lax.ppermute(value, axis, [(i, i ^ bits) for i in range(count)])  1.65 us
  transfers between devices with their start and end apart: 15, of which 1 were waited for; matrix products, arithmetic and copies ran while one was open for 0% of the time, Pallas kernels for 41%

profile of v3, /device:TPU:0, one launch (start us, length us, event | category | flops | bytes accessed | tf_op | source)
XLA Modules:
  0.0 58.9 jit_solution(14562283272228980272)
XLA Ops:
  0.6 0.8 %pad_maximum_fusion.refs_4_.refs_0_ = bf16[4,5120]{1,0:T(4,128)(2,1)S(1)} fusion(bf16[2,5120]{1,0:T(2,128)(2,1)} %bitcast.11, bf16[2,5120]{1,0:T(2,128)(2,1)} %bitcast.9), kind=kLoop, calls=%fused_computation | loop fusion | flops 81920 | bytes 81920 | tf_op jit(solution)/shard_map/concatenate | solution.py:448
  1.4 5.1 %collective-permute-start.2 = (bf16[4,5120]{1,0:T(4,128)(2,1)S(1)}, bf16[4,5120]{1,0:T(4,128)(2,1)S(1)}, u32[]{:S(2)}, u32[]{:S(2)}) collective-permute-start(bf16[4,5120]{1,0:T(4,128)(2,1)S(1)} %pad_maximum_fusion.refs_4_.refs_0_), channel_id=1, source_target_pairs={{0,12},{2,14},{4,8},{6,10},{8,4},{10,6},{12,0},{14,2},{1,13},{3,15... | collective-permute-start | bytes 122888 | tf_op jit(solution)/shard_map/ppermute | solution.py:91
  6.5 0.6 %collective-permute-start = (bf16[4,5120]{1,0:T(4,128)(2,1)S(1)}, bf16[4,5120]{1,0:T(4,128)(2,1)S(1)}, u32[]{:S(2)}, u32[]{:S(2)}) collective-permute-start(bf16[4,5120]{1,0:T(4,128)(2,1)S(1)} %pad_maximum_fusion.refs_4_.refs_0_), channel_id=1, source_target_pairs={{0,4},{2,6},{4,0},{6,2},{8,12},{10,14},{12,8},{14,10},{1,5},{3,7},... | collective-permute-start | bytes 122888 | tf_op jit(solution)/shard_map/ppermute | solution.py:91
  7.2 1.6 %collective-permute-start.3 = (bf16[4,5120]{1,0:T(4,128)(2,1)S(1)}, bf16[4,5120]{1,0:T(4,128)(2,1)S(1)}, u32[]{:S(2)}, u32[]{:S(2)}) collective-permute-start(bf16[4,5120]{1,0:T(4,128)(2,1)S(1)} %pad_maximum_fusion.refs_4_.refs_0_), channel_id=1, source_target_pairs={{0,2},{2,0},{4,6},{6,4},{8,10},{10,8},{12,14},{14,12},{1,3},{3,1},... | collective-permute-start | bytes 122888 | tf_op jit(solution)/shard_map/ppermute | solution.py:91
  8.8 4.7 %fetch_weights.2 = (bf16[5,800,512]{2,1,0:T(8,128)(2,1)S(1)}, bf16[5,800,512]{2,1,0:T(8,128)(2,1)S(1)}, bf16[5,800,512]{2,1,0:T(8,128)(2,1)S(1)}, f32[1,5120]{1,0:T(1,128)S(1)}, f32[8,128]{1,0:T(8,128)S(1)}) custom-call(bf16[1600,5120]{1,0:T(8,128)(2,1)} %bitcast.13, bf16[1600,5120]{1,0:T(8,128)(2,1)} %bitcast.15, bf16[1600,5120]{1,0:T(8,128)(2,1)} %refs_2_.3, ...), custom_call_target="tpu_custom_call" | custom-call | bytes 12288000 | tf_op jit(solution)/shard_map/fetch_weights/pallas_call | solution.py:163
  13.6 0.5 collective-permute-start.5
  14.1 1.6 %collective-permute-start.6 = (bf16[4,5120]{1,0:T(4,128)(2,1)S(1)}, bf16[4,5120]{1,0:T(4,128)(2,1)S(1)}, u32[]{:S(2)}, u32[]{:S(2)}) collective-permute-start(bf16[4,5120]{1,0:T(4,128)(2,1)S(1)} %get-tuple-element.48.refs_3_), channel_id=1, source_target_pairs={{0,2},{2,0},{4,6},{6,4},{8,10},{10,8},{12,14},{14,12},{1,3},{3,1},... | collective-permute-start | bytes 122888 | tf_op jit(solution)/shard_map/ppermute | solution.py:91
  15.7 0.4 collective-permute-start.4
  16.1 5.3 %fetch_weights.3 = (bf16[5,800,512]{2,1,0:T(8,128)(2,1)S(1)}, bf16[5,800,512]{2,1,0:T(8,128)(2,1)S(1)}, bf16[5,800,512]{2,1,0:T(8,128)(2,1)S(1)}, f32[1,5120]{1,0:T(1,128)}, f32[8,128]{1,0:T(8,128)S(1)}) custom-call(bf16[1600,5120]{1,0:T(8,128)(2,1)} %bitcast.14, bf16[1600,5120]{1,0:T(8,128)(2,1)} %bitcast.16, bf16[1600,5120]{1,0:T(8,128)(2,1)} %refs_2_.3, ...), custom_call_target="tpu_custom_call" | custom-call | bytes 12288000 | tf_op jit(solution)/shard_map/fetch_weights/pallas_call | solution.py:163
  21.5 0.2 sort_rows.1.own_ref
  21.8 1.6 %collective-permute-done.7.peer_ref = bf16[32,5120]{1,0:T(8,128)(2,1)S(1)} collective-permute-done((bf16[32,5120]{1,0:T(8,128)(2,1)S(1)}, bf16[32,5120]{1,0:T(8,128)(2,1)S(1)}, u32[]{:S(2)}, u32[]{:S(2)}) %collective-permute-start.7) | collective-permute-done | bytes 327712 | tf_op jit(solution)/shard_map/ppermute | solution.py:91
  23.4 13.5 %hidden_pass.1 = (bf16[800,128]{1,0:T(8,128)(2,1)S(1)}, f32[16,5120]{1,0:T(8,128)S(1)}, bf16[18,5120]{1,0:T(8,128)(2,1)S(1)}, f32[1,5120]{1,0:T(1,128)S(1)}, bf16[64,5120]{1,0:T(8,128)(2,1)S(1)}) custom-call(bf16[32,5120]{1,0:T(8,128)(2,1)S(1)} %sort_rows.1.own_ref, bf16[32,5120]{1,0:T(8,128)(2,1)S(1)} %collective-permute-done.7.peer_ref, ...), custom_call_target="tpu_custom_call" | custom-call | flops 1310720000 | bytes 24576000 | tf_op jit(solution)/shard_map/hidden_pass/pallas_call | solution.py:267
  36.9 0.2 collective-permute-start.8
  37.1 0.4 collective-permute-start.11
  37.5 3.5 %weight_pass.3 = (bf16[1600,2560]{1,0:T(8,128)(2,1)}, bf16[1600,2560]{1,0:T(8,128)(2,1)}, bf16[1600,2560]{1,0:T(8,128)(2,1)}, f32[8,128]{1,0:T(8,128)S(1)}) custom-call(bf16[800,128]{1,0:T(8,128)(2,1)S(1)} %get-tuple-element.59.refs_0_, bf16[64,5120]{1,0:T(8,128)(2,1)S(1)} %get-tuple-element.60.refs_1_.refs_2_), custom_call_target="tpu_custom_call" | custom-call | flops 196608000 | bytes 6144000 | tf_op jit(solution)/shard_map/weight_pass/pallas_call | solution.py:340
  41.0 0.1 fold.1
  41.1 1.7 %collective-permute-start.9 = (bf16[8,5120]{1,0:T(8,128)(2,1)S(1)}, bf16[8,5120]{1,0:T(8,128)(2,1)S(1)}, u32[]{:S(2)}, u32[]{:S(2)}) collective-permute-start(bf16[8,5120]{1,0:T(8,128)(2,1)S(1)} %get-tuple-element.64.refs_6_), channel_id=1, source_target_pairs={{0,2},{2,0},{4,6},{6,4},{8,10},{10,8},{12,14},{14,12},{1,3},{3,1},... | collective-permute-start | bytes 245768 | tf_op jit(solution)/shard_map/ppermute | solution.py:91
  42.8 0.4 collective-permute-start.10
  43.2 4.5 %weight_pass.4 = (bf16[1600,2560]{1,0:T(8,128)(2,1)}, bf16[1600,2560]{1,0:T(8,128)(2,1)}, bf16[1600,2560]{1,0:T(8,128)(2,1)}, f32[8,128]{1,0:T(8,128)S(1)}) custom-call(bf16[800,128]{1,0:T(8,128)(2,1)S(1)} %get-tuple-element.59.refs_0_, ...), custom_call_target="tpu_custom_call", output_to_operand_aliasing={{0}: (3, {}), {1}: (4, {}), {2}: (5, {})} | custom-call | flops 275251200 | bytes 8601600 | tf_op jit(solution)/shard_map/weight_pass/pallas_call | solution.py:340
  47.9 2.4 %collective-permute-start.13 = (bf16[4,5120]{1,0:T(4,128)(2,1)S(1)}, bf16[4,5120]{1,0:T(4,128)(2,1)S(1)}, u32[]{:S(2)}, u32[]{:S(2)}) collective-permute-start(bf16[4,5120]{1,0:T(4,128)(2,1)S(1)} %get-tuple-element.73), channel_id=1, source_target_pairs={{0,8},{2,10},{4,12},{6,14},{8,0},{10,2},{12,4},{14,6},{1,9},{3,11}... | collective-permute-start | bytes 122888 | tf_op jit(solution)/shard_map/ppermute | solution.py:91
  50.2 1.5 %collective-permute-start.14 = (bf16[4,5120]{1,0:T(4,128)(2,1)S(1)}, bf16[4,5120]{1,0:T(4,128)(2,1)S(1)}, u32[]{:S(2)}, u32[]{:S(2)}) collective-permute-start(bf16[4,5120]{1,0:T(4,128)(2,1)S(1)} %get-tuple-element.74), channel_id=1, source_target_pairs={{0,12},{2,14},{4,8},{6,10},{8,4},{10,6},{12,0},{14,2},{1,13},{3,15... | collective-permute-start | bytes 122888 | tf_op jit(solution)/shard_map/ppermute | solution.py:91
  51.8 0.5 collective-permute-start.12
  52.3 5.6 %weight_pass.5 = (bf16[1600,2560]{1,0:T(8,128)(2,1)}, bf16[1600,2560]{1,0:T(8,128)(2,1)}, bf16[1600,2560]{1,0:T(8,128)(2,1)}, f32[8,128]{1,0:T(8,128)}) custom-call(bf16[800,128]{1,0:T(8,128)(2,1)S(1)} %collective-permute-done.11.refs_1_.refs_0_, ...), custom_call_target="tpu_custom_call", output_to_operand_aliasing={{0}: (2, {}), {1}: (3, {}), {2}: (4, {})} | custom-call | flops 314572800 | bytes 9830400 | tf_op jit(solution)/shard_map/weight_pass/pallas_call | solution.py:340
  58.0 0.9 %finish.1 = (bf16[2,5120]{1,0:T(2,128)(2,1)}, f32[1,5120]{1,0:T(1,128)}) custom-call(bf16[2,5120]{1,0:T(2,128)(2,1)S(1)} %bitcast.10, bf16[2,5120]{1,0:T(2,128)(2,1)S(1)} %bitcast.12, f32[1,5120]{1,0:T(1,128)S(1)} %get-tuple-element.44.gain_ref.norm_gain_ref, f32[2,5120]{1,0:T(2,128)S(1)} %get-tuple-element.70.own_ref, ...), custom_call_target="tpu_custom_call" | custom-call | tf_op jit(solution)/shard_map/finish/pallas_call | solution.py:426
  (22 shorter events, 0.3 us)
Async XLA Ops:
  1.4 12.1 %collective-permute-start.2 = (bf16[4,5120]{1,0:T(4,128)(2,1)S(1)}, bf16[4,5120]{1,0:T(4,128)(2,1)S(1)}, u32[]{:S(2)}, u32[]{:S(2)}) collective-permute-start(bf16[4,5120]{1,0:T(4,128)(2,1)S(1)} %pad_maximum_fusion.refs_4_.refs_0_), channel_id=1, source_target_pairs={{0,12},{2,14},{4,8},{6,10},{8,4},{10,6},{12,0},{14,2},{1,13},{3,15... | collective-permute-start | bytes 122888 | tf_op jit(solution)/shard_map/ppermute | solution.py:91
  6.5 7.0 %collective-permute-start.1 = (bf16[4,5120]{1,0:T(4,128)(2,1)S(1)}, bf16[4,5120]{1,0:T(4,128)(2,1)S(1)}, u32[]{:S(2)}, u32[]{:S(2)}) collective-permute-start(bf16[4,5120]{1,0:T(4,128)(2,1)S(1)} %pad_maximum_fusion.refs_4_.refs_0_), channel_id=1, source_target_pairs={{0,8},{2,10},{4,12},{6,14},{8,0},{10,2},{12,4},{14,6},{1,9},{3,11}... | collective-permute-start | bytes 122888 | tf_op jit(solution)/shard_map/ppermute | solution.py:91
  6.5 7.0 %collective-permute-start = (bf16[4,5120]{1,0:T(4,128)(2,1)S(1)}, bf16[4,5120]{1,0:T(4,128)(2,1)S(1)}, u32[]{:S(2)}, u32[]{:S(2)}) collective-permute-start(bf16[4,5120]{1,0:T(4,128)(2,1)S(1)} %pad_maximum_fusion.refs_4_.refs_0_), channel_id=1, source_target_pairs={{0,4},{2,6},{4,0},{6,2},{8,12},{10,14},{12,8},{14,10},{1,5},{3,7},... | collective-permute-start | bytes 122888 | tf_op jit(solution)/shard_map/ppermute | solution.py:91
  7.2 14.3 %collective-permute-start.3 = (bf16[4,5120]{1,0:T(4,128)(2,1)S(1)}, bf16[4,5120]{1,0:T(4,128)(2,1)S(1)}, u32[]{:S(2)}, u32[]{:S(2)}) collective-permute-start(bf16[4,5120]{1,0:T(4,128)(2,1)S(1)} %pad_maximum_fusion.refs_4_.refs_0_), channel_id=1, source_target_pairs={{0,2},{2,0},{4,6},{6,4},{8,10},{10,8},{12,14},{14,12},{1,3},{3,1},... | collective-permute-start | bytes 122888 | tf_op jit(solution)/shard_map/ppermute | solution.py:91
  13.6 7.8 %collective-permute-start.5 = (bf16[4,5120]{1,0:T(4,128)(2,1)S(1)}, bf16[4,5120]{1,0:T(4,128)(2,1)S(1)}, u32[]{:S(2)}, u32[]{:S(2)}) collective-permute-start(bf16[4,5120]{1,0:T(4,128)(2,1)S(1)} %get-tuple-element.47.refs_2_), channel_id=1, source_target_pairs={{0,2},{2,0},{4,6},{6,4},{8,10},{10,8},{12,14},{14,12},{1,3},{3,1},... | collective-permute-start | bytes 122888 | tf_op jit(solution)/shard_map/ppermute | solution.py:91
  14.1 7.4 %collective-permute-start.6 = (bf16[4,5120]{1,0:T(4,128)(2,1)S(1)}, bf16[4,5120]{1,0:T(4,128)(2,1)S(1)}, u32[]{:S(2)}, u32[]{:S(2)}) collective-permute-start(bf16[4,5120]{1,0:T(4,128)(2,1)S(1)} %get-tuple-element.48.refs_3_), channel_id=1, source_target_pairs={{0,2},{2,0},{4,6},{6,4},{8,10},{10,8},{12,14},{14,12},{1,3},{3,1},... | collective-permute-start | bytes 122888 | tf_op jit(solution)/shard_map/ppermute | solution.py:91
  15.7 5.8 %collective-permute-start.4 = (bf16[4,5120]{1,0:T(4,128)(2,1)S(1)}, bf16[4,5120]{1,0:T(4,128)(2,1)S(1)}, u32[]{:S(2)}, u32[]{:S(2)}) collective-permute-start(bf16[4,5120]{1,0:T(4,128)(2,1)S(1)} %get-tuple-element.46.refs_4_.refs_1_), channel_id=1, source_target_pairs={{0,2},{2,0},{4,6},{6,4},{8,10},{10,8},{12,14},{14,12},{1,3},{3,1},... | collective-permute-start | bytes 122888 | tf_op jit(solution)/shard_map/ppermute | solution.py:91
  21.7 1.7 %collective-permute-start.7 = (bf16[32,5120]{1,0:T(8,128)(2,1)S(1)}, bf16[32,5120]{1,0:T(8,128)(2,1)S(1)}, u32[]{:S(2)}, u32[]{:S(2)}) collective-permute-start(bf16[32,5120]{1,0:T(8,128)(2,1)S(1)} %sort_rows.1.own_ref), channel_id=1, source_target_pairs={{0,1},{1,0},{2,3},{3,2},{4,5},{5,4},{6,7},{7,6},{8,9},{9,8},{10,11... | collective-permute-start | bytes 983048 | tf_op jit(solution)/shard_map/ppermute | solution.py:91
  36.9 4.1 %collective-permute-start.8 = (bf16[18,5120]{1,0:T(8,128)(2,1)S(1)}, bf16[18,5120]{1,0:T(8,128)(2,1)S(1)}, u32[]{:S(2)}, u32[]{:S(2)}) collective-permute-start(bf16[18,5120]{1,0:T(8,128)(2,1)S(1)} %get-tuple-element.58), channel_id=1, source_target_pairs={{0,1},{1,0},{2,3},{3,2},{4,5},{5,4},{6,7},{7,6},{8,9},{9,8},{10,11... | collective-permute-start | bytes 552968 | tf_op jit(solution)/shard_map/ppermute | solution.py:91
  37.1 6.1 %collective-permute-start.11 = (bf16[800,128]{1,0:T(8,128)(2,1)S(1)}, bf16[800,128]{1,0:T(8,128)(2,1)S(1)}, u32[]{:S(2)}, u32[]{:S(2)}) collective-permute-start(bf16[800,128]{1,0:T(8,128)(2,1)S(1)} %get-tuple-element.59.refs_0_), channel_id=1, source_target_pairs={{0,1},{1,0},{2,3},{3,2},{4,5},{5,4},{6,7},{7,6},{8,9},{9,8},{10,11... | collective-permute-start | bytes 614408 | tf_op jit(solution)/shard_map/ppermute | solution.py:91
  41.1 6.6 %collective-permute-start.9 = (bf16[8,5120]{1,0:T(8,128)(2,1)S(1)}, bf16[8,5120]{1,0:T(8,128)(2,1)S(1)}, u32[]{:S(2)}, u32[]{:S(2)}) collective-permute-start(bf16[8,5120]{1,0:T(8,128)(2,1)S(1)} %get-tuple-element.64.refs_6_), channel_id=1, source_target_pairs={{0,2},{2,0},{4,6},{6,4},{8,10},{10,8},{12,14},{14,12},{1,3},{3,1},... | collective-permute-start | bytes 245768 | tf_op jit(solution)/shard_map/ppermute | solution.py:91
  42.8 4.9 %collective-permute-start.10 = (bf16[2,5120]{1,0:T(2,128)(2,1)S(1)}, bf16[2,5120]{1,0:T(2,128)(2,1)S(1)}, u32[]{:S(2)}, u32[]{:S(2)}) collective-permute-start(bf16[2,5120]{1,0:T(2,128)(2,1)S(1)} %get-tuple-element.65), channel_id=1, source_target_pairs={{0,2},{2,0},{4,6},{6,4},{8,10},{10,8},{12,14},{14,12},{1,3},{3,1},... | collective-permute-start | bytes 61448 | tf_op jit(solution)/shard_map/ppermute | solution.py:91
  47.9 10.0 %collective-permute-start.13 = (bf16[4,5120]{1,0:T(4,128)(2,1)S(1)}, bf16[4,5120]{1,0:T(4,128)(2,1)S(1)}, u32[]{:S(2)}, u32[]{:S(2)}) collective-permute-start(bf16[4,5120]{1,0:T(4,128)(2,1)S(1)} %get-tuple-element.73), channel_id=1, source_target_pairs={{0,8},{2,10},{4,12},{6,14},{8,0},{10,2},{12,4},{14,6},{1,9},{3,11}... | collective-permute-start | bytes 122888 | tf_op jit(solution)/shard_map/ppermute | solution.py:91
  50.2 7.7 %collective-permute-start.14 = (bf16[4,5120]{1,0:T(4,128)(2,1)S(1)}, bf16[4,5120]{1,0:T(4,128)(2,1)S(1)}, u32[]{:S(2)}, u32[]{:S(2)}) collective-permute-start(bf16[4,5120]{1,0:T(4,128)(2,1)S(1)} %get-tuple-element.74), channel_id=1, source_target_pairs={{0,12},{2,14},{4,8},{6,10},{8,4},{10,6},{12,0},{14,2},{1,13},{3,15... | collective-permute-start | bytes 122888 | tf_op jit(solution)/shard_map/ppermute | solution.py:91
  51.8 6.2 %collective-permute-start.12 = (bf16[4,5120]{1,0:T(4,128)(2,1)S(1)}, bf16[4,5120]{1,0:T(4,128)(2,1)S(1)}, u32[]{:S(2)}, u32[]{:S(2)}) collective-permute-start(bf16[4,5120]{1,0:T(4,128)(2,1)S(1)} %get-tuple-element.72.refs_5_), channel_id=1, source_target_pairs={{0,4},{2,6},{4,0},{6,2},{8,12},{10,14},{12,8},{14,10},{1,5},{3,7},... | collective-permute-start | bytes 122888 | tf_op jit(solution)/shard_map/ppermute | solution.py:91
  52.3 5.7 %copy-start = (bf16[1,2,1,5120]{3,1,2,0:T(2,128)(2,1)S(1)}, bf16[1,2,1,5120]{3,1,2,0:T(2,128)(2,1)}, u32[]{:S(2)}) copy-start(bf16[1,2,1,5120]{3,1,2,0:T(2,128)(2,1)} %param.6) | copy-start | bytes 61444
  52.3 5.7 %copy-start.1 = (bf16[1,2,1,5120]{3,1,2,0:T(2,128)(2,1)S(1)}, bf16[1,2,1,5120]{3,1,2,0:T(2,128)(2,1)}, u32[]{:S(2)}) copy-start(bf16[1,2,1,5120]{3,1,2,0:T(2,128)(2,1)} %param.11) | copy-start | bytes 61444

commit v4 on v3

--- a/solution.py
+++ b/solution.py
@@ -11,7 +11,6 @@
 LANES = 128
 MIB = 1 << 20
 CHUNK = 512
-BLOCK = 256
 ALONG_Z = (2, 4, 6)
 
 
@@ -139,17 +138,23 @@
     )(*pieces, fetched)
 
 
-def fetch_kernel(first, *refs):
+def chunk_copies(sources, top, chunk, pair_ref, down_ref, sems):
+    rows = down_ref.shape[0]
+    start = top + chunk * rows
+    at = pl.ds(start if isinstance(start, int) else pl.multiple_of(start, 16), rows)
+    targets = (pair_ref.at[pl.ds(0, rows)], pair_ref.at[pl.ds(rows, rows)], down_ref)
+    return [
+        pltpu.make_async_copy(source.at[at], target, sems.at[w])
+        for w, (source, target) in enumerate(zip(sources, targets))
+    ]
+
+
+def fetch_kernel(chunk, *refs):
     sources, gain_hbm = refs[:3], refs[3]
-    targets, gain_ref, done_ref, sems, gain_sem = refs[-7:-4], *refs[-4:]
-    chunks, half, width = targets[0].shape
-    top = pl.multiple_of(lax.axis_index("dp") * half, 16)
+    pair_ref, down_ref, gain_ref, done_ref, sems, gain_sem = refs[-6:]
+    top = lax.axis_index("dp") * (sources[2].shape[0] // 2)
     copies = [pltpu.make_async_copy(gain_hbm, gain_ref, gain_sem)]
-    for c in range(chunks):
-        at = slice((first + c) * width, (first + c + 1) * width)
-        for w, (source, target) in enumerate(zip(sources, targets)):
-            block = source.at[pl.ds(top, half), at]
-            copies.append(pltpu.make_async_copy(block, target.at[c], sems.at[w, c]))
+    copies += chunk_copies(sources, top, chunk, pair_ref, down_ref, sems)
     for copy in copies:
         copy.start()
     done_ref[...] = jnp.zeros_like(done_ref)
@@ -157,115 +162,108 @@
         copy.wait()
 
 
-def fetch_weights(weights, gain, first, chunks, width, after=()):
-    ffw = weights[0].shape[0]
-    fixed = [pltpu.with_memory_space_constraint(x, pltpu.HBM) for x in (*weights, gain)]
-    *fetched, gain, done = pl.pallas_call(
-        functools.partial(fetch_kernel, first),
-        out_shape=(pltpu.VMEM((chunks, ffw // 2, width), jnp.bfloat16),) * 3
-        + (pltpu.VMEM(gain.shape, gain.dtype), pltpu.VMEM((8, LANES), jnp.float32)),
+def in_hbm(arrays):
+    return [pltpu.with_memory_space_constraint(x, pltpu.HBM) for x in arrays]
+
+
+def fetch_weights(weights, gain, chunk, rows, after=()):
+    model = weights[0].shape[1]
+    pair, down, gain, done = pl.pallas_call(
+        functools.partial(fetch_kernel, chunk),
+        out_shape=(
+            pltpu.VMEM((2 * rows, model), jnp.bfloat16),
+            pltpu.VMEM((rows, model), jnp.bfloat16),
+            pltpu.VMEM(gain.shape, gain.dtype),
+            pltpu.VMEM((8, LANES), jnp.float32),
+        ),
         in_specs=[ANY_SPEC] * (4 + len(after)),
-        out_specs=(VMEM_SPEC,) * 5,
-        scratch_shapes=[pltpu.SemaphoreType.DMA((3, chunks)), pltpu.SemaphoreType.DMA(())],
+        out_specs=(VMEM_SPEC,) * 4,
+        scratch_shapes=[pltpu.SemaphoreType.DMA((3,)), pltpu.SemaphoreType.DMA(())],
         compiler_params=pltpu.CompilerParams(vmem_limit_bytes=4 * MIB),
         cost_estimate=pl.CostEstimate(
-            flops=0, bytes_accessed=3 * ffw * chunks * width, transcendentals=0
+            flops=0, bytes_accessed=6 * rows * model, transcendentals=0
         ),
         name="fetch_weights",
-    )(*fixed, *after)
-    return fetched, gain, done
-
-
-def hidden_kernel(
-    parts, own_ref, peer_ref, gain_ref, *refs
-):
-    weights, refs = refs[: 3 * parts], refs[3 * parts :]
-    (packed_ref, mine_ref, theirs_ref, gain_part_ref, rows_ref,
-     x_buf, c_buf, inverse_buf, acc_g, acc_u, acc_h, left_buf) = refs
-    half = acc_g.shape[0]
-    chunks, toks, width = x_buf.shape
+    )(*in_hbm((*weights, gain)), *after)
+    return (pair, down), gain, done
+
+
+def hidden_kernel(ready, own_ref, peer_ref, gain_ref, *refs):
+    sources, fetched, refs = refs[:3], refs[3 : 3 + 2 * ready], refs[3 + 2 * ready :]
+    packed_ref, mine_ref, theirs_ref, gain_part_ref, rows_ref = refs[:5]
+    pair_buf, down_buf, total, inverse_buf, sems = refs[5:]
+    rest, rows, model = down_buf.shape
+    toks = total.shape[0]
     each = toks // 2
-    part_chunks = chunks // parts
+    top = lax.axis_index("dp") * (sources[2].shape[0] // 2)
+
+    def copies(c):
+        return chunk_copies(sources, top, ready + c, pair_buf.at[c], down_buf.at[c], sems.at[c])
+
+    for c in range(rest):
+        for copy in copies(c):
+            copy.start()
+
+    def pieces(first):
+        return [slice(at, at + CHUNK) for at in range(first, model, CHUNK)]
 
     squares = jnp.zeros((toks, 1), jnp.float32)
-    for c in range(chunks):
-        at = slice(c * width, (c + 1) * width)
+    for at in pieces(0):
         value = jnp.concatenate([own_ref[:each, at], peer_ref[:each, at]], axis=0)
         value = value.astype(jnp.float32)
         squares = squares + jnp.sum(value * value, axis=-1, keepdims=True)
-    inverse = lax.rsqrt(squares / (chunks * width) + EPSILON)
+    inverse = lax.rsqrt(squares / model + EPSILON)
     inverse_buf[...] = jnp.broadcast_to(inverse, inverse_buf.shape)
-    for c in range(chunks):
-        at = slice(c * width, (c + 1) * width)
+    for at in pieces(0):
         value = jnp.concatenate([own_ref[:each, at], peer_ref[:each, at]], axis=0)
         normed = (value.astype(jnp.float32) * inverse * gain_ref[:, at]).astype(jnp.bfloat16)
-        incoming = jnp.concatenate([own_ref[each:, at], peer_ref[each:, at]], axis=0)
-        x_buf[c] = normed
-        c_buf[c] = incoming
         rows_ref[:toks, at] = normed
-        rows_ref[toks:, at] = incoming
-    acc_g[...] = jnp.zeros_like(acc_g)
-    acc_u[...] = jnp.zeros_like(acc_u)
-    acc_h[...] = jnp.zeros_like(acc_h)
-
-    for part in range(parts):
-        gate_buf, up_buf, down_buf = weights[3 * part : 3 * part + 3]
-
-        def forward(c, carry):
-            at = part * part_chunks + c
-            acc_g[...] += contract(gate_buf[c], x_buf[at], 1, 1)
-            acc_u[...] += contract(up_buf[c], x_buf[at], 1, 1)
-            acc_h[...] += contract(down_buf[c], c_buf[at], 1, 1)
-            return carry
-
-        lax.fori_loop(0, part_chunks, forward, 0)
-
-    step = 80 if half % 80 == 0 else 16
-
-    def pointwise(i, carry):
-        at = pl.ds(pl.multiple_of(i * step, 16), step)
-        gate, up, grad = acc_g[at, :], acc_u[at, :], acc_h[at, :]
+        rows_ref[toks:, at] = jnp.concatenate([own_ref[each:, at], peer_ref[each:, at]], axis=0)
+    total[...] = jnp.zeros_like(total)
+
+    def chunk_pass(pair_ref, down_ref, at):
+        both = contract(pair_ref[...], rows_ref[:toks, :], 1, 1)
+        grad = contract(down_ref[...], rows_ref[toks:, :], 1, 1)
+        gate, up = both[:rows], both[rows:]
         sigmoid = jax.nn.sigmoid(gate)
         active = gate * sigmoid
         grad_gate = grad * up * sigmoid * (1.0 + gate * (1.0 - sigmoid))
-        parts = [grad_gate, grad * active, active * up, jnp.zeros_like(active)]
+        grad_up = grad * active
+        parts = [grad_gate, grad_up, active * up, jnp.zeros_like(active)]
         packed_ref[at, :] = jnp.concatenate(parts, axis=1).astype(jnp.bfloat16)
+        left = jnp.concatenate([grad_gate, grad_up], axis=0).astype(jnp.bfloat16)
+        total[...] += contract(left, pair_ref[...], 0, 0)
+
+    for c in range(ready):
+        chunk_pass(fetched[2 * c], fetched[2 * c + 1], pl.ds(c * rows, rows))
+
+    def step(c, carry):
+        for copy in copies(c):
+            copy.wait()
+        at = pl.ds(pl.multiple_of((ready + c) * rows, 16), rows)
+        chunk_pass(pair_buf.at[c], down_buf.at[c], at)
         return carry
 
-    lax.fori_loop(0, half // step, pointwise, 0)
-    left_buf[...] = packed_ref[...].astype(jnp.float32).T.astype(jnp.bfloat16)
-
-    for part in range(parts):
-        gate_buf, up_buf = weights[3 * part : 3 * part + 2]
-
-        def backward(c, carry):
-            at = pl.ds(pl.multiple_of((part * part_chunks + c) * width, LANES), width)
-            total = jnp.dot(left_buf[:toks, :], gate_buf[c], preferred_element_type=jnp.float32)
-            total += jnp.dot(
-                left_buf[toks : 2 * toks, :], up_buf[c], preferred_element_type=jnp.float32
-            )
-            value = jnp.concatenate([own_ref[:each, at], peer_ref[:each, at]], axis=0)
-            scaled = value.astype(jnp.float32) * inverse_buf[:, :1]
-            gain = jnp.sum(total * scaled, axis=0, keepdims=True)
-            gain_part_ref[:, at] = gain
-            mine_ref[:, at] = total[:each]
-            theirs_ref[:each, at] = total[each:].astype(jnp.bfloat16)
-            theirs_ref[each : each + 1, at] = high_part(gain)
-            theirs_ref[each + 1 : each + 2, at] = low_part(gain)
-            return carry
-
-        lax.fori_loop(0, part_chunks, backward, 0)
-
-
-def hidden_pass(own, peer, gain, fetched):
+    lax.fori_loop(0, rest, step, 0)
+
+    for at in pieces(0):
+        value = jnp.concatenate([own_ref[:each, at], peer_ref[:each, at]], axis=0)
+        part = total[:, at]
+        gain = jnp.sum(part * (value.astype(jnp.float32) * inverse_buf[:, :1]), axis=0, keepdims=True)
+        gain_part_ref[:, at] = gain
+        mine_ref[:, at] = part[:each]
+        theirs_ref[:each, at] = part[each:].astype(jnp.bfloat16)
+        theirs_ref[each : each + 1, at] = high_part(gain)
+        theirs_ref[each + 1 : each + 2, at] = low_part(gain)
+
+
+def hidden_pass(own, peer, gain, weights, fetched):
     toks, model = own.shape
-    each, parts = toks // 2, len(fetched)
-    part_chunks, half, width = fetched[0][0].shape
-    small = pltpu.VMEM((parts * part_chunks, toks, width), jnp.bfloat16)
-    acc = pltpu.VMEM((half, toks), jnp.float32)
-    weights = [pltpu.with_memory_space_constraint(w, pltpu.VMEM) for part in fetched for w in part]
+    each, half, rows = toks // 2, weights[2].shape[0] // 2, fetched[0][1].shape[0]
+    rest = half // rows - len(fetched)
+    ready = [pltpu.with_memory_space_constraint(x, pltpu.VMEM) for part in fetched for x in part]
     return pl.pallas_call(
-        functools.partial(hidden_kernel, parts),
+        functools.partial(hidden_kernel, len(fetched)),
         out_shape=(
             jax.ShapeDtypeStruct((half, LANES), jnp.bfloat16),
             jax.ShapeDtypeStruct((each, model), jnp.float32),
@@ -273,67 +271,69 @@
             jax.ShapeDtypeStruct((1, model), jnp.float32),
             jax.ShapeDtypeStruct((2 * toks, model), jnp.bfloat16),
         ),
-        in_specs=[VMEM_SPEC] * (3 + len(weights)),
+        in_specs=[VMEM_SPEC] * 3 + [ANY_SPEC] * 3 + [VMEM_SPEC] * len(ready),
         out_specs=(VMEM_SPEC,) * 5,
         scratch_shapes=[
-            small, small, pltpu.VMEM((toks, LANES), jnp.float32), acc, acc, acc,
-            pltpu.VMEM((LANES, half), jnp.bfloat16),
+            pltpu.VMEM((rest, 2 * rows, model), jnp.bfloat16),
+            pltpu.VMEM((rest, rows, model), jnp.bfloat16),
+            pltpu.VMEM((toks, model), jnp.float32),
+            pltpu.VMEM((toks, LANES), jnp.float32),
+            pltpu.SemaphoreType.DMA((rest, 3)),
         ],
-        compiler_params=pltpu.CompilerParams(vmem_limit_bytes=16 * MIB),
+        compiler_params=pltpu.CompilerParams(vmem_limit_bytes=32 * MIB),
         cost_estimate=pl.CostEstimate(
             flops=10 * toks * half * model, bytes_accessed=6 * half * model, transcendentals=half * toks
         ),
         name="hidden_pass",
-    )(own, peer, gain, *weights)
+    )(own, peer, gain, *in_hbm(weights), *ready)
 
 
 def weight_kernel(toks, spans, packs, *refs):
     rows_ref, refs = refs[packs], refs[:packs] + refs[packs + 1 :]
     outs, written_ref, buf, sems = refs[-6:-3], refs[-3], refs[-2], refs[-1]
-    slots, _, half, width = buf.shape
-    each = toks // 2
+    slots, _, rows, own_width = buf.shape
+    half, each = outs[0].shape[0] // 2, toks // 2
     place = lax.axis_index("dp")
-    own_width = rows_ref.shape[1] // 2
     written_ref[...] = jnp.zeros_like(written_ref)
-
-    def copy(k, slot, row, block):
-        at = pl.ds(pl.multiple_of(block * width, LANES), width)
-        target = outs[k].at[pl.ds(pl.multiple_of(row, 16), half), at]
+    own = pl.ds(pl.multiple_of(place * own_width, LANES), own_width)
+
+    def copy(k, slot, row):
+        target = outs[k].at[pl.ds(pl.multiple_of(row, 16), rows)]
         return pltpu.make_async_copy(buf.at[slot, k], target, sems.at[slot, k])
 
     done = 0
     for packed_ref, (swapped, first, last) in zip(refs[:packs], spans):
-        row = (1 - place) * half if swapped else place * half
-
-        def step(i, carry, packed_ref=packed_ref, swapped=swapped, row=row, base=done - first):
+        top = (1 - place) * half if swapped else place * half
+
+        def step(i, carry, packed_ref=packed_ref, swapped=swapped, top=top, base=done - first):
             slot = lax.rem(base + i, slots)
 
             @pl.when(base + i >= slots)
             def _():
                 for k in range(3):
-                    copy(k, slot, row, i).wait()
-
-            at = pl.ds(pl.multiple_of(place * own_width + i * width, LANES), width)
-            normed, incoming = rows_ref[:toks, at], rows_ref[toks:, at]
+                    copy(k, slot, top + i * rows).wait()
+
+            normed, incoming = rows_ref[:toks, own], rows_ref[toks:, own]
             if swapped:
                 normed = jnp.concatenate([normed[each:], normed[:each]], axis=0)
                 incoming = jnp.concatenate([incoming[each:], incoming[:each]], axis=0)
+            at = pl.ds(pl.multiple_of(i * rows, 16), rows)
             for k, right in enumerate((normed, normed, incoming)):
-                left = packed_ref[:, k * toks : (k + 1) * toks]
+                left = packed_ref[at, :][:, k * toks : (k + 1) * toks]
                 value = jnp.dot(left, right, preferred_element_type=jnp.float32)
                 buf[slot, k] = value.astype(jnp.bfloat16)
-                copy(k, slot, row, i).start()
+                copy(k, slot, top + i * rows).start()
             return carry
 
         lax.fori_loop(first, last, step, 0)
         done += last - first
     for slot in range(min(slots, done)):
         for k in range(3):
-            copy(k, slot, place * half, 0).wait()
-
-
-def weight_pass(packs, rows, ffw, spans, before=(), after=()):
-    half, toks, model = packs[0].shape[0], rows.shape[0] // 2, rows.shape[1]
+            copy(k, slot, place * half).wait()
+
+
+def weight_pass(packs, rows, ffw, step_rows, spans, before=(), after=()):
+    toks, model = rows.shape[0] // 2, rows.shape[1]
     own_width = model // 2
     blocks = sum(last - first for _, first, last in spans)
     out = jax.ShapeDtypeStruct((ffw, own_width), jnp.bfloat16)
@@ -343,14 +343,14 @@
         in_specs=[VMEM_SPEC] * (len(packs) + 1) + [ANY_SPEC] * (len(before) + len(after)),
         out_specs=(ANY_SPEC,) * 3 + (VMEM_SPEC,),
         scratch_shapes=[
-            pltpu.VMEM((3, 3, half, BLOCK), jnp.bfloat16),
+            pltpu.VMEM((3, 3, step_rows, own_width), jnp.bfloat16),
             pltpu.SemaphoreType.DMA((3, 3)),
         ],
         input_output_aliases={len(packs) + 1 + i: i for i in range(len(before))},
         compiler_params=pltpu.CompilerParams(vmem_limit_bytes=16 * MIB),
         cost_estimate=pl.CostEstimate(
-            flops=6 * toks * half * BLOCK * blocks,
-            bytes_accessed=6 * half * BLOCK * blocks,
+            flops=6 * toks * step_rows * own_width * blocks,
+            bytes_accessed=6 * step_rows * own_width * blocks,
             transcendentals=0,
         ),
         name="weight_pass",
@@ -444,31 +444,29 @@
     gain_hbm = norm_gain.reshape(1, model)
 
     weights = (gate_weight.T, up_weight.T, down_weight)
-    chunks = model // CHUNK
+    step_rows = 160
+    blocks = ffw // 2 // step_rows
     piece = jnp.concatenate([own_tokens, own_incoming], axis=0)
     near = exchange(piece, "tp", 1)
     along = [exchange(piece, "tp", bits) for bits in ALONG_Z]
-    fetched, gain_row, done = fetch_weights(weights, gain_hbm, 0, chunks // 2, CHUNK, (piece,))
+    fetched, gain_row, done = fetch_weights(weights, gain_hbm, 0, step_rows, (piece,))
     along = relay(along, done)
     across = [exchange(arrived, "tp", 1) for arrived in along]
-    more, _, done = fetch_weights(
-        weights, gain_hbm, chunks // 2, chunks - chunks // 2, CHUNK, (along[0],)
-    )
-    fetched = [fetched, more]
+    more, _, done = fetch_weights(weights, gain_hbm, 1, step_rows, (along[0],))
     own = sort_rows(rows, [piece, *along, near, *across], done)
     peer = exchange(own, "dp", 1)
-    packed, kept, send, gain, all_rows = hidden_pass(own, peer, gain_row, fetched)
+    packed, kept, send, gain, all_rows = hidden_pass(own, peer, gain_row, weights, [fetched, more])
     arrived = exchange(send, "dp", 1)
     peer_packed = exchange(packed, "dp", 1)
-    blocks = model // 2 // BLOCK
-    cut = blocks // 2
-    *grads, written = weight_pass([packed], all_rows, ffw, [(False, 0, cut)])
+    cut, turn = blocks // 2, blocks // 3
+    *grads, written = weight_pass([packed], all_rows, ffw, step_rows, [(False, 0, cut)])
     kept, gain, send, send_gain = add_rows(
         fold_kernel, kept, gain, [arrived], written, kept.shape[0] // 2, (kept.shape[0] // 2, 2), "fold"
     )
     arrived = [exchange(send, "tp", 1), exchange(send_gain, "tp", 1)]
     *grads, written = weight_pass(
-        [packed, peer_packed], all_rows, ffw, [(False, cut, blocks), (True, 0, 2)], grads, (send,)
+        [packed, peer_packed], all_rows, ffw, step_rows,
+        [(False, cut, blocks), (True, 0, turn)], grads, (send,),
     )
     kept, gain, *sends = add_rows(
         functools.partial(spread_kernel, rows), kept, gain, arrived, written, rows, (rows + 2,) * 3,
@@ -476,7 +474,7 @@
     )
     arrived = [exchange(send, "tp", bits) for send, bits in zip(sends, ALONG_Z)]
     gate_t, up_t, down_grad, _ = weight_pass(
-        [peer_packed], all_rows, ffw, [(True, 2, blocks)], grads, (sends[0],)
+        [peer_packed], all_rows, ffw, step_rows, [(True, turn, blocks)], grads, (sends[0],)
     )
     input_rows, gain_grad = finish(
         rows, own_tokens, own_incoming, gain_row, kept, gain, arrived
@@ -499,7 +497,7 @@
         and tp_count == 8
         and toks == 32
         and model % 1024 == 0
-        and ffw % 32 == 0
+        and ffw % 320 == 0
         and 3 * ffw * model <= 40 * MIB
     )
     chosen = small_body if small else general_body

time: 59.1 us -> 55.6 us (0.941)
  Pallas kernels: 38.6 us -> 34.7 us
    pallas_call x3, Pallas kernels: 13.6 us -> 11.6 us  [weight_pass(): pl.pallas_call(functools.partial(weight_kernel, toks, spans, len(packs)),...]
    pallas_call x3, Pallas kernels: 23.6 us -> 21.7 us  [the longest x1 16.2 us: hidden_pass(): pl.pallas_call(functools.partial(hidden_kernel, len(fetched)), out_shape=...]
  transfers between devices with their start and end apart: 15 -> 15, of which waited for: 1 -> 2; matrix products, arithmetic and copies ran while one was open for 0% -> 0% of each run, Pallas kernels for 41% -> 31%
where the time goes in v4:
time: 55.6 us; the launch traced here: 55.4 us
  Pallas kernels  34.7 us (62%)
  starting transfers between devices  17.3 us (31%)
  waiting for transfers between devices  1.79 us (3%)
  between operations  0.82 us (1%)
  other arithmetic  0.79 us (1%)
    ppermute x15, starting transfers between devices, exchange(): return lax.ppermute(value, axis, [(i, i ^ bits) for i in range(count)])  17.3 us
    pallas_call x1, Pallas kernels, hidden_pass(): pl.pallas_call(functools.partial(hidden_kernel, len(fetched)), out_shape=...  16.2 us
    pallas_call x3, Pallas kernels, weight_pass(): pl.pallas_call(functools.partial(weight_kernel, toks, spans, len(packs)),...  11.6 us
    pallas_call x2, Pallas kernels, fetch_weights(): pl.pallas_call(functools.partial(fetch_kernel, chunk), out_shape=(pltpu.V...  5.54 us
    ppermute x15, waiting for transfers between devices, exchange(): return lax.ppermute(value, axis, [(i, i ^ bits) for i in range(count)])  1.79 us
  transfers between devices with their start and end apart: 15, of which 2 were waited for; matrix products, arithmetic and copies ran while one was open for 0% of the time, Pallas kernels for 31%

profile of v4, /device:TPU:0, one launch (start us, length us, event | category | flops | bytes accessed | tf_op | source)
XLA Modules:
  0.0 55.4 jit_solution(15230699377817976031)
XLA Ops:
  0.6 0.8 %pad_maximum_fusion.refs_4_.refs_0_ = bf16[4,5120]{1,0:T(4,128)(2,1)S(1)} fusion(bf16[2,5120]{1,0:T(2,128)(2,1)} %bitcast.11, bf16[2,5120]{1,0:T(2,128)(2,1)} %bitcast.9), kind=kLoop, calls=%fused_computation | loop fusion | flops 81920 | bytes 81920 | tf_op jit(solution)/shard_map/concatenate | solution.py:449
  1.4 5.1 %collective-permute-start.2 = (bf16[4,5120]{1,0:T(4,128)(2,1)S(1)}, bf16[4,5120]{1,0:T(4,128)(2,1)S(1)}, u32[]{:S(2)}, u32[]{:S(2)}) collective-permute-start(bf16[4,5120]{1,0:T(4,128)(2,1)S(1)} %pad_maximum_fusion.refs_4_.refs_0_), channel_id=1, source_target_pairs={{0,12},{2,14},{4,8},{6,10},{8,4},{10,6},{12,0},{14,2},{1,13},{3,15... | collective-permute-start | bytes 122888 | tf_op jit(solution)/shard_map/ppermute | solution.py:90
  6.5 0.6 %collective-permute-start = (bf16[4,5120]{1,0:T(4,128)(2,1)S(1)}, bf16[4,5120]{1,0:T(4,128)(2,1)S(1)}, u32[]{:S(2)}, u32[]{:S(2)}) collective-permute-start(bf16[4,5120]{1,0:T(4,128)(2,1)S(1)} %pad_maximum_fusion.refs_4_.refs_0_), channel_id=1, source_target_pairs={{0,4},{2,6},{4,0},{6,2},{8,12},{10,14},{12,8},{14,10},{1,5},{3,7},... | collective-permute-start | bytes 122888 | tf_op jit(solution)/shard_map/ppermute | solution.py:90
  7.2 1.6 %collective-permute-start.3 = (bf16[4,5120]{1,0:T(4,128)(2,1)S(1)}, bf16[4,5120]{1,0:T(4,128)(2,1)S(1)}, u32[]{:S(2)}, u32[]{:S(2)}) collective-permute-start(bf16[4,5120]{1,0:T(4,128)(2,1)S(1)} %pad_maximum_fusion.refs_4_.refs_0_), channel_id=1, source_target_pairs={{0,2},{2,0},{4,6},{6,4},{8,10},{10,8},{12,14},{14,12},{1,3},{3,1},... | collective-permute-start | bytes 122888 | tf_op jit(solution)/shard_map/ppermute | solution.py:90
  8.8 2.5 %fetch_weights.2 = (bf16[320,5120]{1,0:T(8,128)(2,1)S(1)}, bf16[160,5120]{1,0:T(8,128)(2,1)S(1)}, f32[1,5120]{1,0:T(1,128)S(1)}, f32[8,128]{1,0:T(8,128)S(1)}) custom-call(bf16[1600,5120]{1,0:T(8,128)(2,1)} %bitcast.13, bf16[1600,5120]{1,0:T(8,128)(2,1)} %bitcast.16, bf16[1600,5120]{1,0:T(8,128)(2,1)} %refs_2_.5, f32[1,5120]{1,0:T(1,128)} %bitcast.21, ...), custom_call_target="tpu_custom_call" | custom-call | bytes 4915200 | tf_op jit(solution)/shard_map/fetch_weights/pallas_call | solution.py:171
  11.3 0.1 collective-permute-done.1.refs_1_
  11.5 1.6 %collective-permute-start.5 = (bf16[4,5120]{1,0:T(4,128)(2,1)S(1)}, bf16[4,5120]{1,0:T(4,128)(2,1)S(1)}, u32[]{:S(2)}, u32[]{:S(2)}) collective-permute-start(bf16[4,5120]{1,0:T(4,128)(2,1)S(1)} %get-tuple-element.45.refs_2_), channel_id=1, source_target_pairs={{0,2},{2,0},{4,6},{6,4},{8,10},{10,8},{12,14},{14,12},{1,3},{3,1},... | collective-permute-start | bytes 122888 | tf_op jit(solution)/shard_map/ppermute | solution.py:90
  13.0 0.5 collective-permute-start.6
  13.6 1.5 %collective-permute-start.4 = (bf16[4,5120]{1,0:T(4,128)(2,1)S(1)}, bf16[4,5120]{1,0:T(4,128)(2,1)S(1)}, u32[]{:S(2)}, u32[]{:S(2)}) collective-permute-start(bf16[4,5120]{1,0:T(4,128)(2,1)S(1)} %get-tuple-element.44.refs_4_.refs_1_), channel_id=1, source_target_pairs={{0,2},{2,0},{4,6},{6,4},{8,10},{10,8},{12,14},{14,12},{1,3},{3,1},... | collective-permute-start | bytes 122888 | tf_op jit(solution)/shard_map/ppermute | solution.py:90
  15.0 3.1 %fetch_weights.3 = (bf16[320,5120]{1,0:T(8,128)(2,1)S(1)}, bf16[160,5120]{1,0:T(8,128)(2,1)S(1)}, f32[1,5120]{1,0:T(1,128)}, f32[8,128]{1,0:T(8,128)S(1)}) custom-call(bf16[1600,5120]{1,0:T(8,128)(2,1)} %bitcast.14, bf16[1600,5120]{1,0:T(8,128)(2,1)} %bitcast.17, bf16[1600,5120]{1,0:T(8,128)(2,1)} %refs_2_.5, f32[1,5120]{1,0:T(1,128)} %bitcast.22, ...), custom_call_target="tpu_custom_call" | custom-call | bytes 4915200 | tf_op jit(solution)/shard_map/fetch_weights/pallas_call | solution.py:171
  18.2 0.2 sort_rows.1.own_ref
  18.5 1.6 %collective-permute-done.7.peer_ref = bf16[32,5120]{1,0:T(8,128)(2,1)S(1)} collective-permute-done((bf16[32,5120]{1,0:T(8,128)(2,1)S(1)}, bf16[32,5120]{1,0:T(8,128)(2,1)S(1)}, u32[]{:S(2)}, u32[]{:S(2)}) %collective-permute-start.7) | collective-permute-done | bytes 327712 | tf_op jit(solution)/shard_map/ppermute | solution.py:90
  20.1 16.2 %hidden_pass.1 = (bf16[800,128]{1,0:T(8,128)(2,1)S(1)}, f32[16,5120]{1,0:T(8,128)S(1)}, bf16[18,5120]{1,0:T(8,128)(2,1)S(1)}, f32[1,5120]{1,0:T(1,128)S(1)}, bf16[64,5120]{1,0:T(8,128)(2,1)S(1)}) custom-call(bf16[32,5120]{1,0:T(8,128)(2,1)S(1)} %sort_rows.1.own_ref, bf16[32,5120]{1,0:T(8,128)(2,1)S(1)} %collective-permute-done.7.peer_ref, ...), custom_call_target="tpu_custom_call" | custom-call | flops 1310720000 | bytes 24576000 | tf_op jit(solution)/shard_map/hidden_pass/pallas_call | solution.py:265
  36.2 0.2 collective-permute-start.8
  36.5 0.4 collective-permute-start.11
  36.8 2.7 %weight_pass.3 = (bf16[1600,2560]{1,0:T(8,128)(2,1)}, bf16[1600,2560]{1,0:T(8,128)(2,1)}, bf16[1600,2560]{1,0:T(8,128)(2,1)}, f32[8,128]{1,0:T(8,128)S(1)}) custom-call(bf16[800,128]{1,0:T(8,128)(2,1)S(1)} %get-tuple-element.55.refs_0_, bf16[64,5120]{1,0:T(8,128)(2,1)S(1)} %get-tuple-element.56.refs_1_.refs_2_), custom_call_target="tpu_custom_call" | custom-call | flops 157286400 | bytes 4915200 | tf_op jit(solution)/shard_map/weight_pass/pallas_call | solution.py:340
  39.6 0.9 %collective-permute-start.9 = (bf16[8,5120]{1,0:T(8,128)(2,1)S(1)}, bf16[8,5120]{1,0:T(8,128)(2,1)S(1)}, u32[]{:S(2)}, u32[]{:S(2)}) collective-permute-start(bf16[8,5120]{1,0:T(8,128)(2,1)S(1)} %get-tuple-element.60.refs_6_), channel_id=1, source_target_pairs={{0,2},{2,0},{4,6},{6,4},{8,10},{10,8},{12,14},{14,12},{1,3},{3,1},... | collective-permute-start | bytes 245768 | tf_op jit(solution)/shard_map/ppermute | solution.py:90
  40.6 1.2 %collective-permute-start.10 = (bf16[2,5120]{1,0:T(2,128)(2,1)S(1)}, bf16[2,5120]{1,0:T(2,128)(2,1)S(1)}, u32[]{:S(2)}, u32[]{:S(2)}) collective-permute-start(bf16[2,5120]{1,0:T(2,128)(2,1)S(1)} %get-tuple-element.61), channel_id=1, source_target_pairs={{0,2},{2,0},{4,6},{6,4},{8,10},{10,8},{12,14},{14,12},{1,3},{3,1},... | collective-permute-start | bytes 61448 | tf_op jit(solution)/shard_map/ppermute | solution.py:90
  41.7 4.2 %weight_pass.4 = (bf16[1600,2560]{1,0:T(8,128)(2,1)}, bf16[1600,2560]{1,0:T(8,128)(2,1)}, bf16[1600,2560]{1,0:T(8,128)(2,1)}, f32[8,128]{1,0:T(8,128)S(1)}) custom-call(bf16[800,128]{1,0:T(8,128)(2,1)S(1)} %get-tuple-element.55.refs_0_, ...), custom_call_target="tpu_custom_call", output_to_operand_aliasing={{0}: (3, {}), {1}: (4, {}), {2}: (5, {})} | custom-call | flops 314572800 | bytes 9830400 | tf_op jit(solution)/shard_map/weight_pass/pallas_call | solution.py:340
  46.1 2.1 %collective-permute-start.13 = (bf16[4,5120]{1,0:T(4,128)(2,1)S(1)}, bf16[4,5120]{1,0:T(4,128)(2,1)S(1)}, u32[]{:S(2)}, u32[]{:S(2)}) collective-permute-start(bf16[4,5120]{1,0:T(4,128)(2,1)S(1)} %get-tuple-element.69), channel_id=1, source_target_pairs={{0,8},{2,10},{4,12},{6,14},{8,0},{10,2},{12,4},{14,6},{1,9},{3,11}... | collective-permute-start | bytes 122888 | tf_op jit(solution)/shard_map/ppermute | solution.py:90
  48.2 0.9 %collective-permute-start.14 = (bf16[4,5120]{1,0:T(4,128)(2,1)S(1)}, bf16[4,5120]{1,0:T(4,128)(2,1)S(1)}, u32[]{:S(2)}, u32[]{:S(2)}) collective-permute-start(bf16[4,5120]{1,0:T(4,128)(2,1)S(1)} %get-tuple-element.70), channel_id=1, source_target_pairs={{0,12},{2,14},{4,8},{6,10},{8,4},{10,6},{12,0},{14,2},{1,13},{3,15... | collective-permute-start | bytes 122888 | tf_op jit(solution)/shard_map/ppermute | solution.py:90
  49.1 0.5 collective-permute-start.12
  49.6 4.8 %weight_pass.5 = (bf16[1600,2560]{1,0:T(8,128)(2,1)}, bf16[1600,2560]{1,0:T(8,128)(2,1)}, bf16[1600,2560]{1,0:T(8,128)(2,1)}, f32[8,128]{1,0:T(8,128)}) custom-call(bf16[800,128]{1,0:T(8,128)(2,1)S(1)} %collective-permute-done.11.refs_1_.refs_0_, ...), custom_call_target="tpu_custom_call", output_to_operand_aliasing={{0}: (2, {}), {1}: (3, {}), {2}: (4, {})} | custom-call | flops 314572800 | bytes 9830400 | tf_op jit(solution)/shard_map/weight_pass/pallas_call | solution.py:340
  54.5 0.9 %finish.1 = (bf16[2,5120]{1,0:T(2,128)(2,1)}, f32[1,5120]{1,0:T(1,128)}) custom-call(bf16[2,5120]{1,0:T(2,128)(2,1)S(1)} %bitcast.10, bf16[2,5120]{1,0:T(2,128)(2,1)S(1)} %bitcast.12, f32[1,5120]{1,0:T(1,128)S(1)} %get-tuple-element.42.gain_ref.norm_gain_ref, f32[2,5120]{1,0:T(2,128)S(1)} %get-tuple-element.66.own_ref, ...), custom_call_target="tpu_custom_call" | custom-call | tf_op jit(solution)/shard_map/finish/pallas_call | solution.py:426
  (22 shorter events, 0.4 us)
Async XLA Ops:
  1.4 9.9 %collective-permute-start.2 = (bf16[4,5120]{1,0:T(4,128)(2,1)S(1)}, bf16[4,5120]{1,0:T(4,128)(2,1)S(1)}, u32[]{:S(2)}, u32[]{:S(2)}) collective-permute-start(bf16[4,5120]{1,0:T(4,128)(2,1)S(1)} %pad_maximum_fusion.refs_4_.refs_0_), channel_id=1, source_target_pairs={{0,12},{2,14},{4,8},{6,10},{8,4},{10,6},{12,0},{14,2},{1,13},{3,15... | collective-permute-start | bytes 122888 | tf_op jit(solution)/shard_map/ppermute | solution.py:90
  6.5 4.9 %collective-permute-start.1 = (bf16[4,5120]{1,0:T(4,128)(2,1)S(1)}, bf16[4,5120]{1,0:T(4,128)(2,1)S(1)}, u32[]{:S(2)}, u32[]{:S(2)}) collective-permute-start(bf16[4,5120]{1,0:T(4,128)(2,1)S(1)} %pad_maximum_fusion.refs_4_.refs_0_), channel_id=1, source_target_pairs={{0,8},{2,10},{4,12},{6,14},{8,0},{10,2},{12,4},{14,6},{1,9},{3,11}... | collective-permute-start | bytes 122888 | tf_op jit(solution)/shard_map/ppermute | solution.py:90
  6.5 4.9 %collective-permute-start = (bf16[4,5120]{1,0:T(4,128)(2,1)S(1)}, bf16[4,5120]{1,0:T(4,128)(2,1)S(1)}, u32[]{:S(2)}, u32[]{:S(2)}) collective-permute-start(bf16[4,5120]{1,0:T(4,128)(2,1)S(1)} %pad_maximum_fusion.refs_4_.refs_0_), channel_id=1, source_target_pairs={{0,4},{2,6},{4,0},{6,2},{8,12},{10,14},{12,8},{14,10},{1,5},{3,7},... | collective-permute-start | bytes 122888 | tf_op jit(solution)/shard_map/ppermute | solution.py:90
  7.2 10.9 %collective-permute-start.3 = (bf16[4,5120]{1,0:T(4,128)(2,1)S(1)}, bf16[4,5120]{1,0:T(4,128)(2,1)S(1)}, u32[]{:S(2)}, u32[]{:S(2)}) collective-permute-start(bf16[4,5120]{1,0:T(4,128)(2,1)S(1)} %pad_maximum_fusion.refs_4_.refs_0_), channel_id=1, source_target_pairs={{0,2},{2,0},{4,6},{6,4},{8,10},{10,8},{12,14},{14,12},{1,3},{3,1},... | collective-permute-start | bytes 122888 | tf_op jit(solution)/shard_map/ppermute | solution.py:90
  11.5 6.7 %collective-permute-start.5 = (bf16[4,5120]{1,0:T(4,128)(2,1)S(1)}, bf16[4,5120]{1,0:T(4,128)(2,1)S(1)}, u32[]{:S(2)}, u32[]{:S(2)}) collective-permute-start(bf16[4,5120]{1,0:T(4,128)(2,1)S(1)} %get-tuple-element.45.refs_2_), channel_id=1, source_target_pairs={{0,2},{2,0},{4,6},{6,4},{8,10},{10,8},{12,14},{14,12},{1,3},{3,1},... | collective-permute-start | bytes 122888 | tf_op jit(solution)/shard_map/ppermute | solution.py:90
  13.0 5.1 %collective-permute-start.6 = (bf16[4,5120]{1,0:T(4,128)(2,1)S(1)}, bf16[4,5120]{1,0:T(4,128)(2,1)S(1)}, u32[]{:S(2)}, u32[]{:S(2)}) collective-permute-start(bf16[4,5120]{1,0:T(4,128)(2,1)S(1)} %get-tuple-element.46.refs_3_), channel_id=1, source_target_pairs={{0,2},{2,0},{4,6},{6,4},{8,10},{10,8},{12,14},{14,12},{1,3},{3,1},... | collective-permute-start | bytes 122888 | tf_op jit(solution)/shard_map/ppermute | solution.py:90
  13.6 4.6 %collective-permute-start.4 = (bf16[4,5120]{1,0:T(4,128)(2,1)S(1)}, bf16[4,5120]{1,0:T(4,128)(2,1)S(1)}, u32[]{:S(2)}, u32[]{:S(2)}) collective-permute-start(bf16[4,5120]{1,0:T(4,128)(2,1)S(1)} %get-tuple-element.44.refs_4_.refs_1_), channel_id=1, source_target_pairs={{0,2},{2,0},{4,6},{6,4},{8,10},{10,8},{12,14},{14,12},{1,3},{3,1},... | collective-permute-start | bytes 122888 | tf_op jit(solution)/shard_map/ppermute | solution.py:90
  18.4 1.7 %collective-permute-start.7 = (bf16[32,5120]{1,0:T(8,128)(2,1)S(1)}, bf16[32,5120]{1,0:T(8,128)(2,1)S(1)}, u32[]{:S(2)}, u32[]{:S(2)}) collective-permute-start(bf16[32,5120]{1,0:T(8,128)(2,1)S(1)} %sort_rows.1.own_ref), channel_id=1, source_target_pairs={{0,1},{1,0},{2,3},{3,2},{4,5},{5,4},{6,7},{7,6},{8,9},{9,8},{10,11... | collective-permute-start | bytes 983048 | tf_op jit(solution)/shard_map/ppermute | solution.py:90
  36.2 3.2 %collective-permute-start.8 = (bf16[18,5120]{1,0:T(8,128)(2,1)S(1)}, bf16[18,5120]{1,0:T(8,128)(2,1)S(1)}, u32[]{:S(2)}, u32[]{:S(2)}) collective-permute-start(bf16[18,5120]{1,0:T(8,128)(2,1)S(1)} %get-tuple-element.54), channel_id=1, source_target_pairs={{0,1},{1,0},{2,3},{3,2},{4,5},{5,4},{6,7},{7,6},{8,9},{9,8},{10,11... | collective-permute-start | bytes 552968 | tf_op jit(solution)/shard_map/ppermute | solution.py:90
  36.5 5.3 %collective-permute-start.11 = (bf16[800,128]{1,0:T(8,128)(2,1)S(1)}, bf16[800,128]{1,0:T(8,128)(2,1)S(1)}, u32[]{:S(2)}, u32[]{:S(2)}) collective-permute-start(bf16[800,128]{1,0:T(8,128)(2,1)S(1)} %get-tuple-element.55.refs_0_), channel_id=1, source_target_pairs={{0,1},{1,0},{2,3},{3,2},{4,5},{5,4},{6,7},{7,6},{8,9},{9,8},{10,11... | collective-permute-start | bytes 614408 | tf_op jit(solution)/shard_map/ppermute | solution.py:90
  39.6 6.3 %collective-permute-start.9 = (bf16[8,5120]{1,0:T(8,128)(2,1)S(1)}, bf16[8,5120]{1,0:T(8,128)(2,1)S(1)}, u32[]{:S(2)}, u32[]{:S(2)}) collective-permute-start(bf16[8,5120]{1,0:T(8,128)(2,1)S(1)} %get-tuple-element.60.refs_6_), channel_id=1, source_target_pairs={{0,2},{2,0},{4,6},{6,4},{8,10},{10,8},{12,14},{14,12},{1,3},{3,1},... | collective-permute-start | bytes 245768 | tf_op jit(solution)/shard_map/ppermute | solution.py:90
  40.6 5.3 %collective-permute-start.10 = (bf16[2,5120]{1,0:T(2,128)(2,1)S(1)}, bf16[2,5120]{1,0:T(2,128)(2,1)S(1)}, u32[]{:S(2)}, u32[]{:S(2)}) collective-permute-start(bf16[2,5120]{1,0:T(2,128)(2,1)S(1)} %get-tuple-element.61), channel_id=1, source_target_pairs={{0,2},{2,0},{4,6},{6,4},{8,10},{10,8},{12,14},{14,12},{1,3},{3,1},... | collective-permute-start | bytes 61448 | tf_op jit(solution)/shard_map/ppermute | solution.py:90
  46.1 8.3 %collective-permute-start.13 = (bf16[4,5120]{1,0:T(4,128)(2,1)S(1)}, bf16[4,5120]{1,0:T(4,128)(2,1)S(1)}, u32[]{:S(2)}, u32[]{:S(2)}) collective-permute-start(bf16[4,5120]{1,0:T(4,128)(2,1)S(1)} %get-tuple-element.69), channel_id=1, source_target_pairs={{0,8},{2,10},{4,12},{6,14},{8,0},{10,2},{12,4},{14,6},{1,9},{3,11}... | collective-permute-start | bytes 122888 | tf_op jit(solution)/shard_map/ppermute | solution.py:90
  48.2 6.3 %collective-permute-start.14 = (bf16[4,5120]{1,0:T(4,128)(2,1)S(1)}, bf16[4,5120]{1,0:T(4,128)(2,1)S(1)}, u32[]{:S(2)}, u32[]{:S(2)}) collective-permute-start(bf16[4,5120]{1,0:T(4,128)(2,1)S(1)} %get-tuple-element.70), channel_id=1, source_target_pairs={{0,12},{2,14},{4,8},{6,10},{8,4},{10,6},{12,0},{14,2},{1,13},{3,15... | collective-permute-start | bytes 122888 | tf_op jit(solution)/shard_map/ppermute | solution.py:90
  49.1 5.3 %collective-permute-start.12 = (bf16[4,5120]{1,0:T(4,128)(2,1)S(1)}, bf16[4,5120]{1,0:T(4,128)(2,1)S(1)}, u32[]{:S(2)}, u32[]{:S(2)}) collective-permute-start(bf16[4,5120]{1,0:T(4,128)(2,1)S(1)} %get-tuple-element.68.refs_5_), channel_id=1, source_target_pairs={{0,4},{2,6},{4,0},{6,2},{8,12},{10,14},{12,8},{14,10},{1,5},{3,7},... | collective-permute-start | bytes 122888 | tf_op jit(solution)/shard_map/ppermute | solution.py:90
  49.6 4.8 %copy-start = (bf16[1,2,1,5120]{3,1,2,0:T(2,128)(2,1)S(1)}, bf16[1,2,1,5120]{3,1,2,0:T(2,128)(2,1)}, u32[]{:S(2)}) copy-start(bf16[1,2,1,5120]{3,1,2,0:T(2,128)(2,1)} %param.6) | copy-start | bytes 61444
  49.6 4.8 %copy-start.1 = (bf16[1,2,1,5120]{3,1,2,0:T(2,128)(2,1)S(1)}, bf16[1,2,1,5120]{3,1,2,0:T(2,128)(2,1)}, u32[]{:S(2)}) copy-start(bf16[1,2,1,5120]{3,1,2,0:T(2,128)(2,1)} %param.11) | copy-start | bytes 61444

commit v5 on v4

--- a/solution.py
+++ b/solution.py
@@ -222,17 +222,18 @@
     total[...] = jnp.zeros_like(total)
 
     def chunk_pass(pair_ref, down_ref, at):
-        both = contract(pair_ref[...], rows_ref[:toks, :], 1, 1)
-        grad = contract(down_ref[...], rows_ref[toks:, :], 1, 1)
-        gate, up = both[:rows], both[rows:]
+        gate_ref, up_ref = pair_ref.at[pl.ds(0, rows)], pair_ref.at[pl.ds(rows, rows)]
+        gate = contract(rows_ref[:toks, :], gate_ref[...], 1, 1)
+        up = contract(rows_ref[:toks, :], up_ref[...], 1, 1)
+        grad = contract(rows_ref[toks:, :], down_ref[...], 1, 1)
         sigmoid = jax.nn.sigmoid(gate)
         active = gate * sigmoid
         grad_gate = grad * up * sigmoid * (1.0 + gate * (1.0 - sigmoid))
         grad_up = grad * active
         parts = [grad_gate, grad_up, active * up, jnp.zeros_like(active)]
-        packed_ref[at, :] = jnp.concatenate(parts, axis=1).astype(jnp.bfloat16)
-        left = jnp.concatenate([grad_gate, grad_up], axis=0).astype(jnp.bfloat16)
-        total[...] += contract(left, pair_ref[...], 0, 0)
+        packed_ref[at, :] = jnp.concatenate(parts, axis=0).T.astype(jnp.bfloat16)
+        part = contract(grad_gate.astype(jnp.bfloat16), gate_ref[...], 1, 0)
+        total[...] += part + contract(grad_up.astype(jnp.bfloat16), up_ref[...], 1, 0)
 
     for c in range(ready):
         chunk_pass(fetched[2 * c], fetched[2 * c + 1], pl.ds(c * rows, rows))

time: 55.6 us -> 55 us (0.989)
  Pallas kernels: 34.7 us -> 34.1 us
    pallas_call x1, Pallas kernels: 16.2 us -> 15.6 us  [hidden_pass(): pl.pallas_call(functools.partial(hidden_kernel, len(fetched)), out_shape=...]
  transfers between devices with their start and end apart: 15 -> 15, of which waited for: 2 -> 2; matrix products, arithmetic and copies ran while one was open for 0% -> 0% of each run, Pallas kernels for 31% -> 32%
where the time goes in v5:
time: 55 us; the launch traced here: 54.8 us
  Pallas kernels  34.1 us (62%)
  starting transfers between devices  17.3 us (31%)
  waiting for transfers between devices  1.79 us (3%)
  between operations  0.82 us (1%)
  other arithmetic  0.79 us (1%)
    ppermute x15, starting transfers between devices, exchange(): return lax.ppermute(value, axis, [(i, i ^ bits) for i in range(count)])  17.3 us
    pallas_call x1, Pallas kernels, hidden_pass(): pl.pallas_call(functools.partial(hidden_kernel, len(fetched)), out_shape=...  15.6 us
    pallas_call x3, Pallas kernels, weight_pass(): pl.pallas_call(functools.partial(weight_kernel, toks, spans, len(packs)),...  11.6 us
    pallas_call x2, Pallas kernels, fetch_weights(): pl.pallas_call(functools.partial(fetch_kernel, chunk), out_shape=(pltpu.V...  5.54 us
    ppermute x15, waiting for transfers between devices, exchange(): return lax.ppermute(value, axis, [(i, i ^ bits) for i in range(count)])  1.79 us
  transfers between devices with their start and end apart: 15, of which 2 were waited for; matrix products, arithmetic and copies ran while one was open for 0% of the time, Pallas kernels for 32%

profile of v5, /device:TPU:0, one launch (start us, length us, event | category | flops | bytes accessed | tf_op | source)
XLA Modules:
  0.0 54.8 jit_solution(17509224912041366343)
XLA Ops:
  0.6 0.8 %pad_maximum_fusion.refs_4_.refs_0_ = bf16[4,5120]{1,0:T(4,128)(2,1)S(1)} fusion(bf16[2,5120]{1,0:T(2,128)(2,1)} %bitcast.11, bf16[2,5120]{1,0:T(2,128)(2,1)} %bitcast.9), kind=kLoop, calls=%fused_computation | loop fusion | flops 81920 | bytes 81920 | tf_op jit(solution)/shard_map/concatenate | solution.py:450
  1.4 5.1 %collective-permute-start.2 = (bf16[4,5120]{1,0:T(4,128)(2,1)S(1)}, bf16[4,5120]{1,0:T(4,128)(2,1)S(1)}, u32[]{:S(2)}, u32[]{:S(2)}) collective-permute-start(bf16[4,5120]{1,0:T(4,128)(2,1)S(1)} %pad_maximum_fusion.refs_4_.refs_0_), channel_id=1, source_target_pairs={{0,12},{2,14},{4,8},{6,10},{8,4},{10,6},{12,0},{14,2},{1,13},{3,15... | collective-permute-start | bytes 122888 | tf_op jit(solution)/shard_map/ppermute | solution.py:90
  6.5 0.6 %collective-permute-start = (bf16[4,5120]{1,0:T(4,128)(2,1)S(1)}, bf16[4,5120]{1,0:T(4,128)(2,1)S(1)}, u32[]{:S(2)}, u32[]{:S(2)}) collective-permute-start(bf16[4,5120]{1,0:T(4,128)(2,1)S(1)} %pad_maximum_fusion.refs_4_.refs_0_), channel_id=1, source_target_pairs={{0,4},{2,6},{4,0},{6,2},{8,12},{10,14},{12,8},{14,10},{1,5},{3,7},... | collective-permute-start | bytes 122888 | tf_op jit(solution)/shard_map/ppermute | solution.py:90
  7.2 1.6 %collective-permute-start.3 = (bf16[4,5120]{1,0:T(4,128)(2,1)S(1)}, bf16[4,5120]{1,0:T(4,128)(2,1)S(1)}, u32[]{:S(2)}, u32[]{:S(2)}) collective-permute-start(bf16[4,5120]{1,0:T(4,128)(2,1)S(1)} %pad_maximum_fusion.refs_4_.refs_0_), channel_id=1, source_target_pairs={{0,2},{2,0},{4,6},{6,4},{8,10},{10,8},{12,14},{14,12},{1,3},{3,1},... | collective-permute-start | bytes 122888 | tf_op jit(solution)/shard_map/ppermute | solution.py:90
  8.8 2.5 %fetch_weights.2 = (bf16[320,5120]{1,0:T(8,128)(2,1)S(1)}, bf16[160,5120]{1,0:T(8,128)(2,1)S(1)}, f32[1,5120]{1,0:T(1,128)S(1)}, f32[8,128]{1,0:T(8,128)S(1)}) custom-call(bf16[1600,5120]{1,0:T(8,128)(2,1)} %bitcast.13, bf16[1600,5120]{1,0:T(8,128)(2,1)} %bitcast.16, bf16[1600,5120]{1,0:T(8,128)(2,1)} %refs_2_.5, f32[1,5120]{1,0:T(1,128)} %bitcast.21, ...), custom_call_target="tpu_custom_call" | custom-call | bytes 4915200 | tf_op jit(solution)/shard_map/fetch_weights/pallas_call | solution.py:171
  11.3 0.1 collective-permute-done.1.refs_1_
  11.5 1.6 %collective-permute-start.5 = (bf16[4,5120]{1,0:T(4,128)(2,1)S(1)}, bf16[4,5120]{1,0:T(4,128)(2,1)S(1)}, u32[]{:S(2)}, u32[]{:S(2)}) collective-permute-start(bf16[4,5120]{1,0:T(4,128)(2,1)S(1)} %get-tuple-element.45.refs_2_), channel_id=1, source_target_pairs={{0,2},{2,0},{4,6},{6,4},{8,10},{10,8},{12,14},{14,12},{1,3},{3,1},... | collective-permute-start | bytes 122888 | tf_op jit(solution)/shard_map/ppermute | solution.py:90
  13.0 0.5 collective-permute-start.6
  13.6 1.5 %collective-permute-start.4 = (bf16[4,5120]{1,0:T(4,128)(2,1)S(1)}, bf16[4,5120]{1,0:T(4,128)(2,1)S(1)}, u32[]{:S(2)}, u32[]{:S(2)}) collective-permute-start(bf16[4,5120]{1,0:T(4,128)(2,1)S(1)} %get-tuple-element.44.refs_4_.refs_1_), channel_id=1, source_target_pairs={{0,2},{2,0},{4,6},{6,4},{8,10},{10,8},{12,14},{14,12},{1,3},{3,1},... | collective-permute-start | bytes 122888 | tf_op jit(solution)/shard_map/ppermute | solution.py:90
  15.0 3.1 %fetch_weights.3 = (bf16[320,5120]{1,0:T(8,128)(2,1)S(1)}, bf16[160,5120]{1,0:T(8,128)(2,1)S(1)}, f32[1,5120]{1,0:T(1,128)}, f32[8,128]{1,0:T(8,128)S(1)}) custom-call(bf16[1600,5120]{1,0:T(8,128)(2,1)} %bitcast.14, bf16[1600,5120]{1,0:T(8,128)(2,1)} %bitcast.17, bf16[1600,5120]{1,0:T(8,128)(2,1)} %refs_2_.5, f32[1,5120]{1,0:T(1,128)} %bitcast.22, ...), custom_call_target="tpu_custom_call" | custom-call | bytes 4915200 | tf_op jit(solution)/shard_map/fetch_weights/pallas_call | solution.py:171
  18.2 0.2 sort_rows.1.own_ref
  18.5 1.6 %collective-permute-done.7.peer_ref = bf16[32,5120]{1,0:T(8,128)(2,1)S(1)} collective-permute-done((bf16[32,5120]{1,0:T(8,128)(2,1)S(1)}, bf16[32,5120]{1,0:T(8,128)(2,1)S(1)}, u32[]{:S(2)}, u32[]{:S(2)}) %collective-permute-start.7) | collective-permute-done | bytes 327712 | tf_op jit(solution)/shard_map/ppermute | solution.py:90
  20.1 15.6 %hidden_pass.1 = (bf16[800,128]{1,0:T(8,128)(2,1)S(1)}, f32[16,5120]{1,0:T(8,128)S(1)}, bf16[18,5120]{1,0:T(8,128)(2,1)S(1)}, f32[1,5120]{1,0:T(1,128)S(1)}, bf16[64,5120]{1,0:T(8,128)(2,1)S(1)}) custom-call(bf16[32,5120]{1,0:T(8,128)(2,1)S(1)} %sort_rows.1.own_ref, bf16[32,5120]{1,0:T(8,128)(2,1)S(1)} %collective-permute-done.7.peer_ref, ...), custom_call_target="tpu_custom_call" | custom-call | flops 1310720000 | bytes 24576000 | tf_op jit(solution)/shard_map/hidden_pass/pallas_call | solution.py:266
  35.6 0.2 collective-permute-start.8
  35.8 0.4 collective-permute-start.11
  36.2 2.7 %weight_pass.3 = (bf16[1600,2560]{1,0:T(8,128)(2,1)}, bf16[1600,2560]{1,0:T(8,128)(2,1)}, bf16[1600,2560]{1,0:T(8,128)(2,1)}, f32[8,128]{1,0:T(8,128)S(1)}) custom-call(bf16[800,128]{1,0:T(8,128)(2,1)S(1)} %get-tuple-element.55.refs_0_, bf16[64,5120]{1,0:T(8,128)(2,1)S(1)} %get-tuple-element.56.refs_1_.refs_2_), custom_call_target="tpu_custom_call" | custom-call | flops 157286400 | bytes 4915200 | tf_op jit(solution)/shard_map/weight_pass/pallas_call | solution.py:341
  39.1 0.9 %collective-permute-start.9 = (bf16[8,5120]{1,0:T(8,128)(2,1)S(1)}, bf16[8,5120]{1,0:T(8,128)(2,1)S(1)}, u32[]{:S(2)}, u32[]{:S(2)}) collective-permute-start(bf16[8,5120]{1,0:T(8,128)(2,1)S(1)} %get-tuple-element.60.refs_6_), channel_id=1, source_target_pairs={{0,2},{2,0},{4,6},{6,4},{8,10},{10,8},{12,14},{14,12},{1,3},{3,1},... | collective-permute-start | bytes 245768 | tf_op jit(solution)/shard_map/ppermute | solution.py:90
  40.0 1.2 %collective-permute-start.10 = (bf16[2,5120]{1,0:T(2,128)(2,1)S(1)}, bf16[2,5120]{1,0:T(2,128)(2,1)S(1)}, u32[]{:S(2)}, u32[]{:S(2)}) collective-permute-start(bf16[2,5120]{1,0:T(2,128)(2,1)S(1)} %get-tuple-element.61), channel_id=1, source_target_pairs={{0,2},{2,0},{4,6},{6,4},{8,10},{10,8},{12,14},{14,12},{1,3},{3,1},... | collective-permute-start | bytes 61448 | tf_op jit(solution)/shard_map/ppermute | solution.py:90
  41.1 4.2 %weight_pass.4 = (bf16[1600,2560]{1,0:T(8,128)(2,1)}, bf16[1600,2560]{1,0:T(8,128)(2,1)}, bf16[1600,2560]{1,0:T(8,128)(2,1)}, f32[8,128]{1,0:T(8,128)S(1)}) custom-call(bf16[800,128]{1,0:T(8,128)(2,1)S(1)} %get-tuple-element.55.refs_0_, ...), custom_call_target="tpu_custom_call", output_to_operand_aliasing={{0}: (3, {}), {1}: (4, {}), {2}: (5, {})} | custom-call | flops 314572800 | bytes 9830400 | tf_op jit(solution)/shard_map/weight_pass/pallas_call | solution.py:341
  45.5 2.1 %collective-permute-start.13 = (bf16[4,5120]{1,0:T(4,128)(2,1)S(1)}, bf16[4,5120]{1,0:T(4,128)(2,1)S(1)}, u32[]{:S(2)}, u32[]{:S(2)}) collective-permute-start(bf16[4,5120]{1,0:T(4,128)(2,1)S(1)} %get-tuple-element.69), channel_id=1, source_target_pairs={{0,8},{2,10},{4,12},{6,14},{8,0},{10,2},{12,4},{14,6},{1,9},{3,11}... | collective-permute-start | bytes 122888 | tf_op jit(solution)/shard_map/ppermute | solution.py:90
  47.6 0.9 %collective-permute-start.14 = (bf16[4,5120]{1,0:T(4,128)(2,1)S(1)}, bf16[4,5120]{1,0:T(4,128)(2,1)S(1)}, u32[]{:S(2)}, u32[]{:S(2)}) collective-permute-start(bf16[4,5120]{1,0:T(4,128)(2,1)S(1)} %get-tuple-element.70), channel_id=1, source_target_pairs={{0,12},{2,14},{4,8},{6,10},{8,4},{10,6},{12,0},{14,2},{1,13},{3,15... | collective-permute-start | bytes 122888 | tf_op jit(solution)/shard_map/ppermute | solution.py:90
  48.5 0.5 collective-permute-start.12
  49.1 4.8 %weight_pass.5 = (bf16[1600,2560]{1,0:T(8,128)(2,1)}, bf16[1600,2560]{1,0:T(8,128)(2,1)}, bf16[1600,2560]{1,0:T(8,128)(2,1)}, f32[8,128]{1,0:T(8,128)}) custom-call(bf16[800,128]{1,0:T(8,128)(2,1)S(1)} %collective-permute-done.11.refs_1_.refs_0_, ...), custom_call_target="tpu_custom_call", output_to_operand_aliasing={{0}: (2, {}), {1}: (3, {}), {2}: (4, {})} | custom-call | flops 314572800 | bytes 9830400 | tf_op jit(solution)/shard_map/weight_pass/pallas_call | solution.py:341
  53.9 0.9 %finish.1 = (bf16[2,5120]{1,0:T(2,128)(2,1)}, f32[1,5120]{1,0:T(1,128)}) custom-call(bf16[2,5120]{1,0:T(2,128)(2,1)S(1)} %bitcast.10, bf16[2,5120]{1,0:T(2,128)(2,1)S(1)} %bitcast.12, f32[1,5120]{1,0:T(1,128)S(1)} %get-tuple-element.42.gain_ref.norm_gain_ref, f32[2,5120]{1,0:T(2,128)S(1)} %get-tuple-element.66.own_ref, ...), custom_call_target="tpu_custom_call" | custom-call | tf_op jit(solution)/shard_map/finish/pallas_call | solution.py:427
  (22 shorter events, 0.4 us)
Async XLA Ops:
  1.4 9.9 %collective-permute-start.2 = (bf16[4,5120]{1,0:T(4,128)(2,1)S(1)}, bf16[4,5120]{1,0:T(4,128)(2,1)S(1)}, u32[]{:S(2)}, u32[]{:S(2)}) collective-permute-start(bf16[4,5120]{1,0:T(4,128)(2,1)S(1)} %pad_maximum_fusion.refs_4_.refs_0_), channel_id=1, source_target_pairs={{0,12},{2,14},{4,8},{6,10},{8,4},{10,6},{12,0},{14,2},{1,13},{3,15... | collective-permute-start | bytes 122888 | tf_op jit(solution)/shard_map/ppermute | solution.py:90
  6.5 4.9 %collective-permute-start.1 = (bf16[4,5120]{1,0:T(4,128)(2,1)S(1)}, bf16[4,5120]{1,0:T(4,128)(2,1)S(1)}, u32[]{:S(2)}, u32[]{:S(2)}) collective-permute-start(bf16[4,5120]{1,0:T(4,128)(2,1)S(1)} %pad_maximum_fusion.refs_4_.refs_0_), channel_id=1, source_target_pairs={{0,8},{2,10},{4,12},{6,14},{8,0},{10,2},{12,4},{14,6},{1,9},{3,11}... | collective-permute-start | bytes 122888 | tf_op jit(solution)/shard_map/ppermute | solution.py:90
  6.5 4.9 %collective-permute-start = (bf16[4,5120]{1,0:T(4,128)(2,1)S(1)}, bf16[4,5120]{1,0:T(4,128)(2,1)S(1)}, u32[]{:S(2)}, u32[]{:S(2)}) collective-permute-start(bf16[4,5120]{1,0:T(4,128)(2,1)S(1)} %pad_maximum_fusion.refs_4_.refs_0_), channel_id=1, source_target_pairs={{0,4},{2,6},{4,0},{6,2},{8,12},{10,14},{12,8},{14,10},{1,5},{3,7},... | collective-permute-start | bytes 122888 | tf_op jit(solution)/shard_map/ppermute | solution.py:90
  7.2 10.9 %collective-permute-start.3 = (bf16[4,5120]{1,0:T(4,128)(2,1)S(1)}, bf16[4,5120]{1,0:T(4,128)(2,1)S(1)}, u32[]{:S(2)}, u32[]{:S(2)}) collective-permute-start(bf16[4,5120]{1,0:T(4,128)(2,1)S(1)} %pad_maximum_fusion.refs_4_.refs_0_), channel_id=1, source_target_pairs={{0,2},{2,0},{4,6},{6,4},{8,10},{10,8},{12,14},{14,12},{1,3},{3,1},... | collective-permute-start | bytes 122888 | tf_op jit(solution)/shard_map/ppermute | solution.py:90
  11.5 6.7 %collective-permute-start.5 = (bf16[4,5120]{1,0:T(4,128)(2,1)S(1)}, bf16[4,5120]{1,0:T(4,128)(2,1)S(1)}, u32[]{:S(2)}, u32[]{:S(2)}) collective-permute-start(bf16[4,5120]{1,0:T(4,128)(2,1)S(1)} %get-tuple-element.45.refs_2_), channel_id=1, source_target_pairs={{0,2},{2,0},{4,6},{6,4},{8,10},{10,8},{12,14},{14,12},{1,3},{3,1},... | collective-permute-start | bytes 122888 | tf_op jit(solution)/shard_map/ppermute | solution.py:90
  13.0 5.1 %collective-permute-start.6 = (bf16[4,5120]{1,0:T(4,128)(2,1)S(1)}, bf16[4,5120]{1,0:T(4,128)(2,1)S(1)}, u32[]{:S(2)}, u32[]{:S(2)}) collective-permute-start(bf16[4,5120]{1,0:T(4,128)(2,1)S(1)} %get-tuple-element.46.refs_3_), channel_id=1, source_target_pairs={{0,2},{2,0},{4,6},{6,4},{8,10},{10,8},{12,14},{14,12},{1,3},{3,1},... | collective-permute-start | bytes 122888 | tf_op jit(solution)/shard_map/ppermute | solution.py:90
  13.6 4.6 %collective-permute-start.4 = (bf16[4,5120]{1,0:T(4,128)(2,1)S(1)}, bf16[4,5120]{1,0:T(4,128)(2,1)S(1)}, u32[]{:S(2)}, u32[]{:S(2)}) collective-permute-start(bf16[4,5120]{1,0:T(4,128)(2,1)S(1)} %get-tuple-element.44.refs_4_.refs_1_), channel_id=1, source_target_pairs={{0,2},{2,0},{4,6},{6,4},{8,10},{10,8},{12,14},{14,12},{1,3},{3,1},... | collective-permute-start | bytes 122888 | tf_op jit(solution)/shard_map/ppermute | solution.py:90
  18.4 1.7 %collective-permute-start.7 = (bf16[32,5120]{1,0:T(8,128)(2,1)S(1)}, bf16[32,5120]{1,0:T(8,128)(2,1)S(1)}, u32[]{:S(2)}, u32[]{:S(2)}) collective-permute-start(bf16[32,5120]{1,0:T(8,128)(2,1)S(1)} %sort_rows.1.own_ref), channel_id=1, source_target_pairs={{0,1},{1,0},{2,3},{3,2},{4,5},{5,4},{6,7},{7,6},{8,9},{9,8},{10,11... | collective-permute-start | bytes 983048 | tf_op jit(solution)/shard_map/ppermute | solution.py:90
  35.6 3.3 %collective-permute-start.8 = (bf16[18,5120]{1,0:T(8,128)(2,1)S(1)}, bf16[18,5120]{1,0:T(8,128)(2,1)S(1)}, u32[]{:S(2)}, u32[]{:S(2)}) collective-permute-start(bf16[18,5120]{1,0:T(8,128)(2,1)S(1)} %get-tuple-element.54), channel_id=1, source_target_pairs={{0,1},{1,0},{2,3},{3,2},{4,5},{5,4},{6,7},{7,6},{8,9},{9,8},{10,11... | collective-permute-start | bytes 552968 | tf_op jit(solution)/shard_map/ppermute | solution.py:90
  35.8 5.3 %collective-permute-start.11 = (bf16[800,128]{1,0:T(8,128)(2,1)S(1)}, bf16[800,128]{1,0:T(8,128)(2,1)S(1)}, u32[]{:S(2)}, u32[]{:S(2)}) collective-permute-start(bf16[800,128]{1,0:T(8,128)(2,1)S(1)} %get-tuple-element.55.refs_0_), channel_id=1, source_target_pairs={{0,1},{1,0},{2,3},{3,2},{4,5},{5,4},{6,7},{7,6},{8,9},{9,8},{10,11... | collective-permute-start | bytes 614408 | tf_op jit(solution)/shard_map/ppermute | solution.py:90
  39.1 6.3 %collective-permute-start.9 = (bf16[8,5120]{1,0:T(8,128)(2,1)S(1)}, bf16[8,5120]{1,0:T(8,128)(2,1)S(1)}, u32[]{:S(2)}, u32[]{:S(2)}) collective-permute-start(bf16[8,5120]{1,0:T(8,128)(2,1)S(1)} %get-tuple-element.60.refs_6_), channel_id=1, source_target_pairs={{0,2},{2,0},{4,6},{6,4},{8,10},{10,8},{12,14},{14,12},{1,3},{3,1},... | collective-permute-start | bytes 245768 | tf_op jit(solution)/shard_map/ppermute | solution.py:90
  40.0 5.4 %collective-permute-start.10 = (bf16[2,5120]{1,0:T(2,128)(2,1)S(1)}, bf16[2,5120]{1,0:T(2,128)(2,1)S(1)}, u32[]{:S(2)}, u32[]{:S(2)}) collective-permute-start(bf16[2,5120]{1,0:T(2,128)(2,1)S(1)} %get-tuple-element.61), channel_id=1, source_target_pairs={{0,2},{2,0},{4,6},{6,4},{8,10},{10,8},{12,14},{14,12},{1,3},{3,1},... | collective-permute-start | bytes 61448 | tf_op jit(solution)/shard_map/ppermute | solution.py:90
  45.5 8.3 %collective-permute-start.13 = (bf16[4,5120]{1,0:T(4,128)(2,1)S(1)}, bf16[4,5120]{1,0:T(4,128)(2,1)S(1)}, u32[]{:S(2)}, u32[]{:S(2)}) collective-permute-start(bf16[4,5120]{1,0:T(4,128)(2,1)S(1)} %get-tuple-element.69), channel_id=1, source_target_pairs={{0,8},{2,10},{4,12},{6,14},{8,0},{10,2},{12,4},{14,6},{1,9},{3,11}... | collective-permute-start | bytes 122888 | tf_op jit(solution)/shard_map/ppermute | solution.py:90
  47.6 6.3 %collective-permute-start.14 = (bf16[4,5120]{1,0:T(4,128)(2,1)S(1)}, bf16[4,5120]{1,0:T(4,128)(2,1)S(1)}, u32[]{:S(2)}, u32[]{:S(2)}) collective-permute-start(bf16[4,5120]{1,0:T(4,128)(2,1)S(1)} %get-tuple-element.70), channel_id=1, source_target_pairs={{0,12},{2,14},{4,8},{6,10},{8,4},{10,6},{12,0},{14,2},{1,13},{3,15... | collective-permute-start | bytes 122888 | tf_op jit(solution)/shard_map/ppermute | solution.py:90
  48.5 5.4 %collective-permute-start.12 = (bf16[4,5120]{1,0:T(4,128)(2,1)S(1)}, bf16[4,5120]{1,0:T(4,128)(2,1)S(1)}, u32[]{:S(2)}, u32[]{:S(2)}) collective-permute-start(bf16[4,5120]{1,0:T(4,128)(2,1)S(1)} %get-tuple-element.68.refs_5_), channel_id=1, source_target_pairs={{0,4},{2,6},{4,0},{6,2},{8,12},{10,14},{12,8},{14,10},{1,5},{3,7},... | collective-permute-start | bytes 122888 | tf_op jit(solution)/shard_map/ppermute | solution.py:90
  49.0 4.8 %copy-start = (bf16[1,2,1,5120]{3,1,2,0:T(2,128)(2,1)S(1)}, bf16[1,2,1,5120]{3,1,2,0:T(2,128)(2,1)}, u32[]{:S(2)}) copy-start(bf16[1,2,1,5120]{3,1,2,0:T(2,128)(2,1)} %param.6) | copy-start | bytes 61444
  49.1 4.8 %copy-start.1 = (bf16[1,2,1,5120]{3,1,2,0:T(2,128)(2,1)S(1)}, bf16[1,2,1,5120]{3,1,2,0:T(2,128)(2,1)}, u32[]{:S(2)}) copy-start(bf16[1,2,1,5120]{3,1,2,0:T(2,128)(2,1)} %param.11) | copy-start | bytes 61444

commit v6 on v4

--- a/solution.py
+++ b/solution.py
@@ -10,7 +10,7 @@
 EPSILON = 1e-06
 LANES = 128
 MIB = 1 << 20
-CHUNK = 512
+CHUNK = 1024
 ALONG_Z = (2, 4, 6)
 
 
@@ -138,26 +138,41 @@
     )(*pieces, fetched)
 
 
-def chunk_copies(sources, top, chunk, pair_ref, down_ref, sems):
-    rows = down_ref.shape[0]
-    start = top + chunk * rows
-    at = pl.ds(start if isinstance(start, int) else pl.multiple_of(start, 16), rows)
-    targets = (pair_ref.at[pl.ds(0, rows)], pair_ref.at[pl.ds(rows, rows)], down_ref)
+def padded(count):
+    return -(-count // LANES) * LANES
+
+
+def chunk_copies(sources, chunk, pair_ref, down_ref, sems):
+    wide, width = down_ref.shape
+    half = sources[2].shape[0] // 2
+    top = pl.multiple_of(lax.axis_index("dp") * half, 16)
+    start = chunk * width
+    at = pl.ds(start if isinstance(start, int) else pl.multiple_of(start, LANES), width)
+    targets = (pair_ref.at[pl.ds(0, half)], pair_ref.at[pl.ds(wide, half)], down_ref.at[pl.ds(0, half)])
     return [
-        pltpu.make_async_copy(source.at[at], target, sems.at[w])
+        pltpu.make_async_copy(source.at[pl.ds(top, half), at], target, sems.at[w])
         for w, (source, target) in enumerate(zip(sources, targets))
     ]
+
+
+def clear_between(pair_ref, down_ref, half):
+    wide, width = down_ref.shape
+    if wide > half:
+        zeros = jnp.zeros((wide - half, width), jnp.bfloat16)
+        pair_ref[half:wide, :] = zeros
+        pair_ref[wide + half :, :] = zeros
+        down_ref[half:, :] = zeros
 
 
 def fetch_kernel(chunk, *refs):
     sources, gain_hbm = refs[:3], refs[3]
     pair_ref, down_ref, gain_ref, done_ref, sems, gain_sem = refs[-6:]
-    top = lax.axis_index("dp") * (sources[2].shape[0] // 2)
     copies = [pltpu.make_async_copy(gain_hbm, gain_ref, gain_sem)]
-    copies += chunk_copies(sources, top, chunk, pair_ref, down_ref, sems)
+    copies += chunk_copies(sources, chunk, pair_ref, down_ref, sems)
     for copy in copies:
         copy.start()
     done_ref[...] = jnp.zeros_like(done_ref)
+    clear_between(pair_ref, down_ref, sources[2].shape[0] // 2)
     for copy in copies:
         copy.wait()
 
@@ -166,13 +181,13 @@
     return [pltpu.with_memory_space_constraint(x, pltpu.HBM) for x in arrays]
 
 
-def fetch_weights(weights, gain, chunk, rows, after=()):
-    model = weights[0].shape[1]
+def fetch_weights(weights, gain, chunk, after=()):
+    half = weights[2].shape[0] // 2
     pair, down, gain, done = pl.pallas_call(
         functools.partial(fetch_kernel, chunk),
         out_shape=(
-            pltpu.VMEM((2 * rows, model), jnp.bfloat16),
-            pltpu.VMEM((rows, model), jnp.bfloat16),
+            pltpu.VMEM((2 * padded(half), CHUNK), jnp.bfloat16),
+            pltpu.VMEM((padded(half), CHUNK), jnp.bfloat16),
             pltpu.VMEM(gain.shape, gain.dtype),
             pltpu.VMEM((8, LANES), jnp.float32),
         ),
@@ -181,7 +196,7 @@
         scratch_shapes=[pltpu.SemaphoreType.DMA((3,)), pltpu.SemaphoreType.DMA(())],
         compiler_params=pltpu.CompilerParams(vmem_limit_bytes=4 * MIB),
         cost_estimate=pl.CostEstimate(
-            flops=0, bytes_accessed=6 * rows * model, transcendentals=0
+            flops=0, bytes_accessed=6 * half * CHUNK, transcendentals=0
         ),
         name="fetch_weights",
     )(*in_hbm((*weights, gain)), *after)
@@ -191,76 +206,94 @@
 def hidden_kernel(ready, own_ref, peer_ref, gain_ref, *refs):
     sources, fetched, refs = refs[:3], refs[3 : 3 + 2 * ready], refs[3 + 2 * ready :]
     packed_ref, mine_ref, theirs_ref, gain_part_ref, rows_ref = refs[:5]
-    pair_buf, down_buf, total, inverse_buf, sems = refs[5:]
-    rest, rows, model = down_buf.shape
-    toks = total.shape[0]
-    each = toks // 2
-    top = lax.axis_index("dp") * (sources[2].shape[0] // 2)
+    pair_buf, down_buf, acc, acc_grad, left, inverse_buf, sems = refs[5:]
+    rest, wide, width = down_buf.shape
+    toks, half = acc.shape[0], packed_ref.shape[0]
+    each, model = toks // 2, rows_ref.shape[1]
 
     def copies(c):
-        return chunk_copies(sources, top, ready + c, pair_buf.at[c], down_buf.at[c], sems.at[c])
+        return chunk_copies(sources, ready + c, pair_buf.at[c], down_buf.at[c], sems.at[c])
 
     for c in range(rest):
         for copy in copies(c):
             copy.start()
-
-    def pieces(first):
-        return [slice(at, at + CHUNK) for at in range(first, model, CHUNK)]
+    for c in range(rest):
+        clear_between(pair_buf.at[c], down_buf.at[c], half)
 
     squares = jnp.zeros((toks, 1), jnp.float32)
-    for at in pieces(0):
+    pieces = [slice(at, at + 512) for at in range(0, model, 512)]
+    for at in pieces:
         value = jnp.concatenate([own_ref[:each, at], peer_ref[:each, at]], axis=0)
         value = value.astype(jnp.float32)
         squares = squares + jnp.sum(value * value, axis=-1, keepdims=True)
     inverse = lax.rsqrt(squares / model + EPSILON)
     inverse_buf[...] = jnp.broadcast_to(inverse, inverse_buf.shape)
-    for at in pieces(0):
+    for at in pieces:
         value = jnp.concatenate([own_ref[:each, at], peer_ref[:each, at]], axis=0)
         normed = (value.astype(jnp.float32) * inverse * gain_ref[:, at]).astype(jnp.bfloat16)
         rows_ref[:toks, at] = normed
         rows_ref[toks:, at] = jnp.concatenate([own_ref[each:, at], peer_ref[each:, at]], axis=0)
-    total[...] = jnp.zeros_like(total)
-
-    def chunk_pass(pair_ref, down_ref, at):
-        both = contract(pair_ref[...], rows_ref[:toks, :], 1, 1)
-        grad = contract(down_ref[...], rows_ref[toks:, :], 1, 1)
-        gate, up = both[:rows], both[rows:]
-        sigmoid = jax.nn.sigmoid(gate)
-        active = gate * sigmoid
-        grad_gate = grad * up * sigmoid * (1.0 + gate * (1.0 - sigmoid))
-        grad_up = grad * active
-        parts = [grad_gate, grad_up, active * up, jnp.zeros_like(active)]
-        packed_ref[at, :] = jnp.concatenate(parts, axis=1).astype(jnp.bfloat16)
-        left = jnp.concatenate([grad_gate, grad_up], axis=0).astype(jnp.bfloat16)
-        total[...] += contract(left, pair_ref[...], 0, 0)
-
-    for c in range(ready):
-        chunk_pass(fetched[2 * c], fetched[2 * c + 1], pl.ds(c * rows, rows))
-
-    def step(c, carry):
-        for copy in copies(c):
-            copy.wait()
-        at = pl.ds(pl.multiple_of((ready + c) * rows, 16), rows)
-        chunk_pass(pair_buf.at[c], down_buf.at[c], at)
-        return carry
-
-    lax.fori_loop(0, rest, step, 0)
-
-    for at in pieces(0):
+    acc[...] = jnp.zeros_like(acc)
+    acc_grad[...] = jnp.zeros_like(acc_grad)
+
+    def forward(pair_ref, down_ref, at):
+        acc[...] += contract(rows_ref[:toks, at], pair_ref[...], 1, 1)
+        acc_grad[...] += contract(rows_ref[toks:, at], down_ref[...], 1, 1)
+
+    def backward(pair_ref, at):
+        part = jnp.dot(left[...], pair_ref[...], preferred_element_type=jnp.float32)
         value = jnp.concatenate([own_ref[:each, at], peer_ref[:each, at]], axis=0)
-        part = total[:, at]
-        gain = jnp.sum(part * (value.astype(jnp.float32) * inverse_buf[:, :1]), axis=0, keepdims=True)
+        scaled = value.astype(jnp.float32) * inverse_buf[:, :1]
+        gain = jnp.sum(part * scaled, axis=0, keepdims=True)
         gain_part_ref[:, at] = gain
         mine_ref[:, at] = part[:each]
         theirs_ref[:each, at] = part[each:].astype(jnp.bfloat16)
         theirs_ref[each : each + 1, at] = high_part(gain)
         theirs_ref[each + 1 : each + 2, at] = low_part(gain)
 
+    def place(c):
+        return pl.ds(pl.multiple_of((ready + c) * width, LANES), width)
+
+    for c in range(ready):
+        forward(fetched[2 * c], fetched[2 * c + 1], pl.ds(c * width, width))
+
+    def forward_step(c, carry):
+        for copy in copies(c):
+            copy.wait()
+        forward(pair_buf.at[c], down_buf.at[c], place(c))
+        return carry
+
+    lax.fori_loop(0, rest, forward_step, 0)
+
+    for first in range(0, wide, LANES):
+        at = slice(first, first + LANES)
+        up_at = slice(wide + first, wide + first + LANES)
+        gate, up, grad = acc[:, at], acc[:, up_at], acc_grad[:, at]
+        sigmoid = jax.nn.sigmoid(gate)
+        active = gate * sigmoid
+        grad_gate = grad * up * sigmoid * (1.0 + gate * (1.0 - sigmoid))
+        grad_up = grad * active
+        left[:, at] = grad_gate.astype(jnp.bfloat16)
+        left[:, up_at] = grad_up.astype(jnp.bfloat16)
+        parts = [grad_gate, grad_up, active * up, jnp.zeros_like(active)]
+        columns = jnp.concatenate(parts, axis=0).T.astype(jnp.bfloat16)
+        last = min(first + LANES, half)
+        packed_ref[first:last, :] = columns[: last - first]
+
+    for c in range(ready):
+        backward(fetched[2 * c], pl.ds(c * width, width))
+
+    def backward_step(c, carry):
+        backward(pair_buf.at[c], place(c))
+        return carry
+
+    lax.fori_loop(0, rest, backward_step, 0)
+
 
 def hidden_pass(own, peer, gain, weights, fetched):
     toks, model = own.shape
-    each, half, rows = toks // 2, weights[2].shape[0] // 2, fetched[0][1].shape[0]
-    rest = half // rows - len(fetched)
+    each, half = toks // 2, weights[2].shape[0] // 2
+    wide, rest = padded(half), model // CHUNK - len(fetched)
     ready = [pltpu.with_memory_space_constraint(x, pltpu.VMEM) for part in fetched for x in part]
     return pl.pallas_call(
         functools.partial(hidden_kernel, len(fetched)),
@@ -274,9 +307,11 @@
         in_specs=[VMEM_SPEC] * 3 + [ANY_SPEC] * 3 + [VMEM_SPEC] * len(ready),
         out_specs=(VMEM_SPEC,) * 5,
         scratch_shapes=[
-            pltpu.VMEM((rest, 2 * rows, model), jnp.bfloat16),
-            pltpu.VMEM((rest, rows, model), jnp.bfloat16),
-            pltpu.VMEM((toks, model), jnp.float32),
+            pltpu.VMEM((rest, 2 * wide, CHUNK), jnp.bfloat16),
+            pltpu.VMEM((rest, wide, CHUNK), jnp.bfloat16),
+            pltpu.VMEM((toks, 2 * wide), jnp.float32),
+            pltpu.VMEM((toks, wide), jnp.float32),
+            pltpu.VMEM((toks, 2 * wide), jnp.bfloat16),
             pltpu.VMEM((toks, LANES), jnp.float32),
             pltpu.SemaphoreType.DMA((rest, 3)),
         ],
@@ -290,7 +325,7 @@
 
 def weight_kernel(toks, spans, packs, *refs):
     rows_ref, refs = refs[packs], refs[:packs] + refs[packs + 1 :]
-    outs, written_ref, buf, sems = refs[-6:-3], refs[-3], refs[-2], refs[-1]
+    outs, written_ref, buf, right_buf, sems = refs[-7:-4], *refs[-4:]
     slots, _, rows, own_width = buf.shape
     half, each = outs[0].shape[0] // 2, toks // 2
     place = lax.axis_index("dp")
@@ -304,8 +339,14 @@
     done = 0
     for packed_ref, (swapped, first, last) in zip(refs[:packs], spans):
         top = (1 - place) * half if swapped else place * half
-
-        def step(i, carry, packed_ref=packed_ref, swapped=swapped, top=top, base=done - first):
+        if swapped:
+            for at in (0, toks):
+                mine, theirs = rows_ref[at : at + each, own], rows_ref[at + each : at + toks, own]
+                right_buf[at : at + toks, :] = jnp.concatenate([theirs, mine], axis=0)
+        else:
+            right_buf[...] = rows_ref[:, own]
+
+        def step(i, carry, packed_ref=packed_ref, top=top, base=done - first):
             slot = lax.rem(base + i, slots)
 
             @pl.when(base + i >= slots)
@@ -313,10 +354,7 @@
                 for k in range(3):
                     copy(k, slot, top + i * rows).wait()
 
-            normed, incoming = rows_ref[:toks, own], rows_ref[toks:, own]
-            if swapped:
-                normed = jnp.concatenate([normed[each:], normed[:each]], axis=0)
-                incoming = jnp.concatenate([incoming[each:], incoming[:each]], axis=0)
+            normed, incoming = right_buf[:toks, :], right_buf[toks:, :]
             at = pl.ds(pl.multiple_of(i * rows, 16), rows)
             for k, right in enumerate((normed, normed, incoming)):
                 left = packed_ref[at, :][:, k * toks : (k + 1) * toks]
@@ -344,6 +382,7 @@
         out_specs=(ANY_SPEC,) * 3 + (VMEM_SPEC,),
         scratch_shapes=[
             pltpu.VMEM((3, 3, step_rows, own_width), jnp.bfloat16),
+            pltpu.VMEM((2 * toks, own_width), jnp.bfloat16),
             pltpu.SemaphoreType.DMA((3, 3)),
         ],
         input_output_aliases={len(packs) + 1 + i: i for i in range(len(before))},
@@ -449,10 +488,10 @@
     piece = jnp.concatenate([own_tokens, own_incoming], axis=0)
     near = exchange(piece, "tp", 1)
     along = [exchange(piece, "tp", bits) for bits in ALONG_Z]
-    fetched, gain_row, done = fetch_weights(weights, gain_hbm, 0, step_rows, (piece,))
+    fetched, gain_row, done = fetch_weights(weights, gain_hbm, 0, (piece,))
     along = relay(along, done)
     across = [exchange(arrived, "tp", 1) for arrived in along]
-    more, _, done = fetch_weights(weights, gain_hbm, 1, step_rows, (along[0],))
+    more, _, done = fetch_weights(weights, gain_hbm, 1, (along[0],))
     own = sort_rows(rows, [piece, *along, near, *across], done)
     peer = exchange(own, "dp", 1)
     packed, kept, send, gain, all_rows = hidden_pass(own, peer, gain_row, weights, [fetched, more])

time: 55.6 us -> 54.1 us (0.973)
  Pallas kernels: 34.7 us -> 33.3 us
    pallas_call x1, Pallas kernels: 16.2 us -> 14.6 us  [hidden_pass(): pl.pallas_call(functools.partial(hidden_kernel, len(fetched)), out_shape=...]
  transfers between devices with their start and end apart: 15 -> 15, of which waited for: 2 -> 2; matrix products, arithmetic and copies ran while one was open for 0% -> 0% of each run, Pallas kernels for 31% -> 32%
where the time goes in v6:
time: 54.1 us; the launch traced here: 54 us
  Pallas kernels  33.3 us (62%)
  starting transfers between devices  17.3 us (32%)
  waiting for transfers between devices  1.77 us (3%)
  between operations  0.82 us (2%)
  other arithmetic  0.79 us (1%)
    ppermute x15, starting transfers between devices, exchange(): return lax.ppermute(value, axis, [(i, i ^ bits) for i in range(count)])  17.3 us
    pallas_call x1, Pallas kernels, hidden_pass(): pl.pallas_call(functools.partial(hidden_kernel, len(fetched)), out_shape=...  14.6 us
    pallas_call x3, Pallas kernels, weight_pass(): pl.pallas_call(functools.partial(weight_kernel, toks, spans, len(packs)),...  11.7 us
    pallas_call x2, Pallas kernels, fetch_weights(): pl.pallas_call(functools.partial(fetch_kernel, chunk), out_shape=(pltpu.V...  5.57 us
    ppermute x15, waiting for transfers between devices, exchange(): return lax.ppermute(value, axis, [(i, i ^ bits) for i in range(count)])  1.77 us
  transfers between devices with their start and end apart: 15, of which 2 were waited for; matrix products, arithmetic and copies ran while one was open for 0% of the time, Pallas kernels for 32%

profile of v6, /device:TPU:0, one launch (start us, length us, event | category | flops | bytes accessed | tf_op | source)
XLA Modules:
  0.0 54.0 jit_solution(2707172768398946071)
XLA Ops:
  0.6 0.8 %pad_maximum_fusion.refs_4_.refs_0_ = bf16[4,5120]{1,0:T(4,128)(2,1)S(1)} fusion(bf16[2,5120]{1,0:T(2,128)(2,1)} %bitcast.11, bf16[2,5120]{1,0:T(2,128)(2,1)} %bitcast.9), kind=kLoop, calls=%fused_computation | loop fusion | flops 81920 | bytes 81920 | tf_op jit(solution)/shard_map/concatenate | solution.py:488
  1.4 5.1 %collective-permute-start.2 = (bf16[4,5120]{1,0:T(4,128)(2,1)S(1)}, bf16[4,5120]{1,0:T(4,128)(2,1)S(1)}, u32[]{:S(2)}, u32[]{:S(2)}) collective-permute-start(bf16[4,5120]{1,0:T(4,128)(2,1)S(1)} %pad_maximum_fusion.refs_4_.refs_0_), channel_id=1, source_target_pairs={{0,12},{2,14},{4,8},{6,10},{8,4},{10,6},{12,0},{14,2},{1,13},{3,15... | collective-permute-start | bytes 122888 | tf_op jit(solution)/shard_map/ppermute | solution.py:90
  6.5 0.6 %collective-permute-start = (bf16[4,5120]{1,0:T(4,128)(2,1)S(1)}, bf16[4,5120]{1,0:T(4,128)(2,1)S(1)}, u32[]{:S(2)}, u32[]{:S(2)}) collective-permute-start(bf16[4,5120]{1,0:T(4,128)(2,1)S(1)} %pad_maximum_fusion.refs_4_.refs_0_), channel_id=1, source_target_pairs={{0,4},{2,6},{4,0},{6,2},{8,12},{10,14},{12,8},{14,10},{1,5},{3,7},... | collective-permute-start | bytes 122888 | tf_op jit(solution)/shard_map/ppermute | solution.py:90
  7.2 1.6 %collective-permute-start.3 = (bf16[4,5120]{1,0:T(4,128)(2,1)S(1)}, bf16[4,5120]{1,0:T(4,128)(2,1)S(1)}, u32[]{:S(2)}, u32[]{:S(2)}) collective-permute-start(bf16[4,5120]{1,0:T(4,128)(2,1)S(1)} %pad_maximum_fusion.refs_4_.refs_0_), channel_id=1, source_target_pairs={{0,2},{2,0},{4,6},{6,4},{8,10},{10,8},{12,14},{14,12},{1,3},{3,1},... | collective-permute-start | bytes 122888 | tf_op jit(solution)/shard_map/ppermute | solution.py:90
  8.8 2.5 %fetch_weights.2 = (bf16[1792,1024]{1,0:T(8,128)(2,1)S(1)}, bf16[896,1024]{1,0:T(8,128)(2,1)S(1)}, f32[1,5120]{1,0:T(1,128)S(1)}, f32[8,128]{1,0:T(8,128)S(1)}) custom-call(bf16[1600,5120]{1,0:T(8,128)(2,1)} %bitcast.13, bf16[1600,5120]{1,0:T(8,128)(2,1)} %bitcast.16, bf16[1600,5120]{1,0:T(8,128)(2,1)} %refs_2_.5, f32[1,5120]{1,0:T(1,128)} %bitcast.21, ...), custom_call_target="tpu_custom_call" | custom-call | bytes 4915200 | tf_op jit(solution)/shard_map/fetch_weights/pallas_call | solution.py:186
  11.5 1.6 %collective-permute-start.5 = (bf16[4,5120]{1,0:T(4,128)(2,1)S(1)}, bf16[4,5120]{1,0:T(4,128)(2,1)S(1)}, u32[]{:S(2)}, u32[]{:S(2)}) collective-permute-start(bf16[4,5120]{1,0:T(4,128)(2,1)S(1)} %get-tuple-element.45.refs_2_), channel_id=1, source_target_pairs={{0,2},{2,0},{4,6},{6,4},{8,10},{10,8},{12,14},{14,12},{1,3},{3,1},... | collective-permute-start | bytes 122888 | tf_op jit(solution)/shard_map/ppermute | solution.py:90
  13.0 0.5 collective-permute-start.6
  13.6 1.5 %collective-permute-start.4 = (bf16[4,5120]{1,0:T(4,128)(2,1)S(1)}, bf16[4,5120]{1,0:T(4,128)(2,1)S(1)}, u32[]{:S(2)}, u32[]{:S(2)}) collective-permute-start(bf16[4,5120]{1,0:T(4,128)(2,1)S(1)} %get-tuple-element.44.refs_4_.refs_1_), channel_id=1, source_target_pairs={{0,2},{2,0},{4,6},{6,4},{8,10},{10,8},{12,14},{14,12},{1,3},{3,1},... | collective-permute-start | bytes 122888 | tf_op jit(solution)/shard_map/ppermute | solution.py:90
  15.0 3.1 %fetch_weights.3 = (bf16[1792,1024]{1,0:T(8,128)(2,1)S(1)}, bf16[896,1024]{1,0:T(8,128)(2,1)S(1)}, f32[1,5120]{1,0:T(1,128)}, f32[8,128]{1,0:T(8,128)S(1)}) custom-call(bf16[1600,5120]{1,0:T(8,128)(2,1)} %bitcast.14, bf16[1600,5120]{1,0:T(8,128)(2,1)} %bitcast.17, bf16[1600,5120]{1,0:T(8,128)(2,1)} %refs_2_.5, f32[1,5120]{1,0:T(1,128)} %bitcast.22, ...), custom_call_target="tpu_custom_call" | custom-call | bytes 4915200 | tf_op jit(solution)/shard_map/fetch_weights/pallas_call | solution.py:186
  18.2 0.2 sort_rows.1.own_ref
  18.5 1.6 %collective-permute-done.7.peer_ref = bf16[32,5120]{1,0:T(8,128)(2,1)S(1)} collective-permute-done((bf16[32,5120]{1,0:T(8,128)(2,1)S(1)}, bf16[32,5120]{1,0:T(8,128)(2,1)S(1)}, u32[]{:S(2)}, u32[]{:S(2)}) %collective-permute-start.7) | collective-permute-done | bytes 327712 | tf_op jit(solution)/shard_map/ppermute | solution.py:90
  20.1 14.6 %hidden_pass.1 = (bf16[800,128]{1,0:T(8,128)(2,1)S(1)}, f32[16,5120]{1,0:T(8,128)S(1)}, bf16[18,5120]{1,0:T(8,128)(2,1)S(1)}, f32[1,5120]{1,0:T(1,128)S(1)}, bf16[64,5120]{1,0:T(8,128)(2,1)S(1)}) custom-call(bf16[32,5120]{1,0:T(8,128)(2,1)S(1)} %sort_rows.1.own_ref, bf16[32,5120]{1,0:T(8,128)(2,1)S(1)} %collective-permute-done.7.peer_ref, ...), custom_call_target="tpu_custom_call" | custom-call | flops 1310720000 | bytes 24576000 | tf_op jit(solution)/shard_map/hidden_pass/pallas_call | solution.py:298
  34.7 0.2 collective-permute-start.8
  34.9 0.4 collective-permute-start.11
  35.3 2.7 %weight_pass.3 = (bf16[1600,2560]{1,0:T(8,128)(2,1)}, bf16[1600,2560]{1,0:T(8,128)(2,1)}, bf16[1600,2560]{1,0:T(8,128)(2,1)}, f32[8,128]{1,0:T(8,128)S(1)}) custom-call(bf16[800,128]{1,0:T(8,128)(2,1)S(1)} %get-tuple-element.55.refs_0_, bf16[64,5120]{1,0:T(8,128)(2,1)S(1)} %get-tuple-element.56.refs_1_.refs_2_), custom_call_target="tpu_custom_call" | custom-call | flops 157286400 | bytes 4915200 | tf_op jit(solution)/shard_map/weight_pass/pallas_call | solution.py:378
  38.0 0.1 fold.1
  38.2 0.9 %collective-permute-start.9 = (bf16[8,5120]{1,0:T(8,128)(2,1)S(1)}, bf16[8,5120]{1,0:T(8,128)(2,1)S(1)}, u32[]{:S(2)}, u32[]{:S(2)}) collective-permute-start(bf16[8,5120]{1,0:T(8,128)(2,1)S(1)} %get-tuple-element.60.refs_6_), channel_id=1, source_target_pairs={{0,2},{2,0},{4,6},{6,4},{8,10},{10,8},{12,14},{14,12},{1,3},{3,1},... | collective-permute-start | bytes 245768 | tf_op jit(solution)/shard_map/ppermute | solution.py:90
  39.1 1.2 %collective-permute-start.10 = (bf16[2,5120]{1,0:T(2,128)(2,1)S(1)}, bf16[2,5120]{1,0:T(2,128)(2,1)S(1)}, u32[]{:S(2)}, u32[]{:S(2)}) collective-permute-start(bf16[2,5120]{1,0:T(2,128)(2,1)S(1)} %get-tuple-element.61), channel_id=1, source_target_pairs={{0,2},{2,0},{4,6},{6,4},{8,10},{10,8},{12,14},{14,12},{1,3},{3,1},... | collective-permute-start | bytes 61448 | tf_op jit(solution)/shard_map/ppermute | solution.py:90
  40.3 4.2 %weight_pass.4 = (bf16[1600,2560]{1,0:T(8,128)(2,1)}, bf16[1600,2560]{1,0:T(8,128)(2,1)}, bf16[1600,2560]{1,0:T(8,128)(2,1)}, f32[8,128]{1,0:T(8,128)S(1)}) custom-call(bf16[800,128]{1,0:T(8,128)(2,1)S(1)} %get-tuple-element.55.refs_0_, ...), custom_call_target="tpu_custom_call", output_to_operand_aliasing={{0}: (3, {}), {1}: (4, {}), {2}: (5, {})} | custom-call | flops 314572800 | bytes 9830400 | tf_op jit(solution)/shard_map/weight_pass/pallas_call | solution.py:378
  44.6 2.1 %collective-permute-start.13 = (bf16[4,5120]{1,0:T(4,128)(2,1)S(1)}, bf16[4,5120]{1,0:T(4,128)(2,1)S(1)}, u32[]{:S(2)}, u32[]{:S(2)}) collective-permute-start(bf16[4,5120]{1,0:T(4,128)(2,1)S(1)} %get-tuple-element.69), channel_id=1, source_target_pairs={{0,8},{2,10},{4,12},{6,14},{8,0},{10,2},{12,4},{14,6},{1,9},{3,11}... | collective-permute-start | bytes 122888 | tf_op jit(solution)/shard_map/ppermute | solution.py:90
  46.7 0.9 %collective-permute-start.14 = (bf16[4,5120]{1,0:T(4,128)(2,1)S(1)}, bf16[4,5120]{1,0:T(4,128)(2,1)S(1)}, u32[]{:S(2)}, u32[]{:S(2)}) collective-permute-start(bf16[4,5120]{1,0:T(4,128)(2,1)S(1)} %get-tuple-element.70), channel_id=1, source_target_pairs={{0,12},{2,14},{4,8},{6,10},{8,4},{10,6},{12,0},{14,2},{1,13},{3,15... | collective-permute-start | bytes 122888 | tf_op jit(solution)/shard_map/ppermute | solution.py:90
  47.6 0.5 collective-permute-start.12
  48.2 4.8 %weight_pass.5 = (bf16[1600,2560]{1,0:T(8,128)(2,1)}, bf16[1600,2560]{1,0:T(8,128)(2,1)}, bf16[1600,2560]{1,0:T(8,128)(2,1)}, f32[8,128]{1,0:T(8,128)}) custom-call(bf16[800,128]{1,0:T(8,128)(2,1)S(1)} %collective-permute-done.11.refs_1_.refs_0_, ...), custom_call_target="tpu_custom_call", output_to_operand_aliasing={{0}: (2, {}), {1}: (3, {}), {2}: (4, {})} | custom-call | flops 314572800 | bytes 9830400 | tf_op jit(solution)/shard_map/weight_pass/pallas_call | solution.py:378
  53.0 0.9 %finish.1 = (bf16[2,5120]{1,0:T(2,128)(2,1)}, f32[1,5120]{1,0:T(1,128)}) custom-call(bf16[2,5120]{1,0:T(2,128)(2,1)S(1)} %bitcast.10, bf16[2,5120]{1,0:T(2,128)(2,1)S(1)} %bitcast.12, f32[1,5120]{1,0:T(1,128)S(1)} %get-tuple-element.42.gain_ref.norm_gain_ref, f32[2,5120]{1,0:T(2,128)S(1)} %get-tuple-element.66.own_ref, ...), custom_call_target="tpu_custom_call" | custom-call | tf_op jit(solution)/shard_map/finish/pallas_call | solution.py:465
  (22 shorter events, 0.4 us)
Async XLA Ops:
  1.4 9.9 %collective-permute-start.2 = (bf16[4,5120]{1,0:T(4,128)(2,1)S(1)}, bf16[4,5120]{1,0:T(4,128)(2,1)S(1)}, u32[]{:S(2)}, u32[]{:S(2)}) collective-permute-start(bf16[4,5120]{1,0:T(4,128)(2,1)S(1)} %pad_maximum_fusion.refs_4_.refs_0_), channel_id=1, source_target_pairs={{0,12},{2,14},{4,8},{6,10},{8,4},{10,6},{12,0},{14,2},{1,13},{3,15... | collective-permute-start | bytes 122888 | tf_op jit(solution)/shard_map/ppermute | solution.py:90
  6.5 4.9 %collective-permute-start.1 = (bf16[4,5120]{1,0:T(4,128)(2,1)S(1)}, bf16[4,5120]{1,0:T(4,128)(2,1)S(1)}, u32[]{:S(2)}, u32[]{:S(2)}) collective-permute-start(bf16[4,5120]{1,0:T(4,128)(2,1)S(1)} %pad_maximum_fusion.refs_4_.refs_0_), channel_id=1, source_target_pairs={{0,8},{2,10},{4,12},{6,14},{8,0},{10,2},{12,4},{14,6},{1,9},{3,11}... | collective-permute-start | bytes 122888 | tf_op jit(solution)/shard_map/ppermute | solution.py:90
  6.5 4.9 %collective-permute-start = (bf16[4,5120]{1,0:T(4,128)(2,1)S(1)}, bf16[4,5120]{1,0:T(4,128)(2,1)S(1)}, u32[]{:S(2)}, u32[]{:S(2)}) collective-permute-start(bf16[4,5120]{1,0:T(4,128)(2,1)S(1)} %pad_maximum_fusion.refs_4_.refs_0_), channel_id=1, source_target_pairs={{0,4},{2,6},{4,0},{6,2},{8,12},{10,14},{12,8},{14,10},{1,5},{3,7},... | collective-permute-start | bytes 122888 | tf_op jit(solution)/shard_map/ppermute | solution.py:90
  7.2 11.0 %collective-permute-start.3 = (bf16[4,5120]{1,0:T(4,128)(2,1)S(1)}, bf16[4,5120]{1,0:T(4,128)(2,1)S(1)}, u32[]{:S(2)}, u32[]{:S(2)}) collective-permute-start(bf16[4,5120]{1,0:T(4,128)(2,1)S(1)} %pad_maximum_fusion.refs_4_.refs_0_), channel_id=1, source_target_pairs={{0,2},{2,0},{4,6},{6,4},{8,10},{10,8},{12,14},{14,12},{1,3},{3,1},... | collective-permute-start | bytes 122888 | tf_op jit(solution)/shard_map/ppermute | solution.py:90
  11.5 6.7 %collective-permute-start.5 = (bf16[4,5120]{1,0:T(4,128)(2,1)S(1)}, bf16[4,5120]{1,0:T(4,128)(2,1)S(1)}, u32[]{:S(2)}, u32[]{:S(2)}) collective-permute-start(bf16[4,5120]{1,0:T(4,128)(2,1)S(1)} %get-tuple-element.45.refs_2_), channel_id=1, source_target_pairs={{0,2},{2,0},{4,6},{6,4},{8,10},{10,8},{12,14},{14,12},{1,3},{3,1},... | collective-permute-start | bytes 122888 | tf_op jit(solution)/shard_map/ppermute | solution.py:90
  13.0 5.1 %collective-permute-start.6 = (bf16[4,5120]{1,0:T(4,128)(2,1)S(1)}, bf16[4,5120]{1,0:T(4,128)(2,1)S(1)}, u32[]{:S(2)}, u32[]{:S(2)}) collective-permute-start(bf16[4,5120]{1,0:T(4,128)(2,1)S(1)} %get-tuple-element.46.refs_3_), channel_id=1, source_target_pairs={{0,2},{2,0},{4,6},{6,4},{8,10},{10,8},{12,14},{14,12},{1,3},{3,1},... | collective-permute-start | bytes 122888 | tf_op jit(solution)/shard_map/ppermute | solution.py:90
  13.6 4.6 %collective-permute-start.4 = (bf16[4,5120]{1,0:T(4,128)(2,1)S(1)}, bf16[4,5120]{1,0:T(4,128)(2,1)S(1)}, u32[]{:S(2)}, u32[]{:S(2)}) collective-permute-start(bf16[4,5120]{1,0:T(4,128)(2,1)S(1)} %get-tuple-element.44.refs_4_.refs_1_), channel_id=1, source_target_pairs={{0,2},{2,0},{4,6},{6,4},{8,10},{10,8},{12,14},{14,12},{1,3},{3,1},... | collective-permute-start | bytes 122888 | tf_op jit(solution)/shard_map/ppermute | solution.py:90
  18.4 1.7 %collective-permute-start.7 = (bf16[32,5120]{1,0:T(8,128)(2,1)S(1)}, bf16[32,5120]{1,0:T(8,128)(2,1)S(1)}, u32[]{:S(2)}, u32[]{:S(2)}) collective-permute-start(bf16[32,5120]{1,0:T(8,128)(2,1)S(1)} %sort_rows.1.own_ref), channel_id=1, source_target_pairs={{0,1},{1,0},{2,3},{3,2},{4,5},{5,4},{6,7},{7,6},{8,9},{9,8},{10,11... | collective-permute-start | bytes 983048 | tf_op jit(solution)/shard_map/ppermute | solution.py:90
  34.7 3.3 %collective-permute-start.8 = (bf16[18,5120]{1,0:T(8,128)(2,1)S(1)}, bf16[18,5120]{1,0:T(8,128)(2,1)S(1)}, u32[]{:S(2)}, u32[]{:S(2)}) collective-permute-start(bf16[18,5120]{1,0:T(8,128)(2,1)S(1)} %get-tuple-element.54), channel_id=1, source_target_pairs={{0,1},{1,0},{2,3},{3,2},{4,5},{5,4},{6,7},{7,6},{8,9},{9,8},{10,11... | collective-permute-start | bytes 552968 | tf_op jit(solution)/shard_map/ppermute | solution.py:90
  34.9 5.3 %collective-permute-start.11 = (bf16[800,128]{1,0:T(8,128)(2,1)S(1)}, bf16[800,128]{1,0:T(8,128)(2,1)S(1)}, u32[]{:S(2)}, u32[]{:S(2)}) collective-permute-start(bf16[800,128]{1,0:T(8,128)(2,1)S(1)} %get-tuple-element.55.refs_0_), channel_id=1, source_target_pairs={{0,1},{1,0},{2,3},{3,2},{4,5},{5,4},{6,7},{7,6},{8,9},{9,8},{10,11... | collective-permute-start | bytes 614408 | tf_op jit(solution)/shard_map/ppermute | solution.py:90
  38.2 6.3 %collective-permute-start.9 = (bf16[8,5120]{1,0:T(8,128)(2,1)S(1)}, bf16[8,5120]{1,0:T(8,128)(2,1)S(1)}, u32[]{:S(2)}, u32[]{:S(2)}) collective-permute-start(bf16[8,5120]{1,0:T(8,128)(2,1)S(1)} %get-tuple-element.60.refs_6_), channel_id=1, source_target_pairs={{0,2},{2,0},{4,6},{6,4},{8,10},{10,8},{12,14},{14,12},{1,3},{3,1},... | collective-permute-start | bytes 245768 | tf_op jit(solution)/shard_map/ppermute | solution.py:90
  39.1 5.4 %collective-permute-start.10 = (bf16[2,5120]{1,0:T(2,128)(2,1)S(1)}, bf16[2,5120]{1,0:T(2,128)(2,1)S(1)}, u32[]{:S(2)}, u32[]{:S(2)}) collective-permute-start(bf16[2,5120]{1,0:T(2,128)(2,1)S(1)} %get-tuple-element.61), channel_id=1, source_target_pairs={{0,2},{2,0},{4,6},{6,4},{8,10},{10,8},{12,14},{14,12},{1,3},{3,1},... | collective-permute-start | bytes 61448 | tf_op jit(solution)/shard_map/ppermute | solution.py:90
  44.6 8.4 %collective-permute-start.13 = (bf16[4,5120]{1,0:T(4,128)(2,1)S(1)}, bf16[4,5120]{1,0:T(4,128)(2,1)S(1)}, u32[]{:S(2)}, u32[]{:S(2)}) collective-permute-start(bf16[4,5120]{1,0:T(4,128)(2,1)S(1)} %get-tuple-element.69), channel_id=1, source_target_pairs={{0,8},{2,10},{4,12},{6,14},{8,0},{10,2},{12,4},{14,6},{1,9},{3,11}... | collective-permute-start | bytes 122888 | tf_op jit(solution)/shard_map/ppermute | solution.py:90
  46.7 6.3 %collective-permute-start.14 = (bf16[4,5120]{1,0:T(4,128)(2,1)S(1)}, bf16[4,5120]{1,0:T(4,128)(2,1)S(1)}, u32[]{:S(2)}, u32[]{:S(2)}) collective-permute-start(bf16[4,5120]{1,0:T(4,128)(2,1)S(1)} %get-tuple-element.70), channel_id=1, source_target_pairs={{0,12},{2,14},{4,8},{6,10},{8,4},{10,6},{12,0},{14,2},{1,13},{3,15... | collective-permute-start | bytes 122888 | tf_op jit(solution)/shard_map/ppermute | solution.py:90
  47.6 5.4 %collective-permute-start.12 = (bf16[4,5120]{1,0:T(4,128)(2,1)S(1)}, bf16[4,5120]{1,0:T(4,128)(2,1)S(1)}, u32[]{:S(2)}, u32[]{:S(2)}) collective-permute-start(bf16[4,5120]{1,0:T(4,128)(2,1)S(1)} %get-tuple-element.68.refs_5_), channel_id=1, source_target_pairs={{0,4},{2,6},{4,0},{6,2},{8,12},{10,14},{12,8},{14,10},{1,5},{3,7},... | collective-permute-start | bytes 122888 | tf_op jit(solution)/shard_map/ppermute | solution.py:90
  48.2 4.8 %copy-start = (bf16[1,2,1,5120]{3,1,2,0:T(2,128)(2,1)S(1)}, bf16[1,2,1,5120]{3,1,2,0:T(2,128)(2,1)}, u32[]{:S(2)}) copy-start(bf16[1,2,1,5120]{3,1,2,0:T(2,128)(2,1)} %param.6) | copy-start | bytes 61444
  48.2 4.9 %copy-start.1 = (bf16[1,2,1,5120]{3,1,2,0:T(2,128)(2,1)S(1)}, bf16[1,2,1,5120]{3,1,2,0:T(2,128)(2,1)}, u32[]{:S(2)}) copy-start(bf16[1,2,1,5120]{3,1,2,0:T(2,128)(2,1)} %param.11) | copy-start | bytes 61444

commit v7 on v6

--- a/solution.py
+++ b/solution.py
@@ -161,7 +161,6 @@
         zeros = jnp.zeros((wide - half, width), jnp.bfloat16)
         pair_ref[half:wide, :] = zeros
         pair_ref[wide + half :, :] = zeros
-        down_ref[half:, :] = zeros
 
 
 def fetch_kernel(chunk, *refs):
@@ -208,7 +207,7 @@
     packed_ref, mine_ref, theirs_ref, gain_part_ref, rows_ref = refs[:5]
     pair_buf, down_buf, acc, acc_grad, left, inverse_buf, sems = refs[5:]
     rest, wide, width = down_buf.shape
-    toks, half = acc.shape[0], packed_ref.shape[0]
+    toks, half = acc.shape[1], packed_ref.shape[0]
     each, model = toks // 2, rows_ref.shape[1]
 
     def copies(c):
@@ -237,8 +236,10 @@
     acc_grad[...] = jnp.zeros_like(acc_grad)
 
     def forward(pair_ref, down_ref, at):
-        acc[...] += contract(rows_ref[:toks, at], pair_ref[...], 1, 1)
-        acc_grad[...] += contract(rows_ref[toks:, at], down_ref[...], 1, 1)
+        right = rows_ref[:toks, at]
+        acc[:half, :] += contract(pair_ref[:half, :], right, 1, 1)
+        acc[wide : wide + half, :] += contract(pair_ref[wide : wide + half, :], right, 1, 1)
+        acc_grad[:half, :] += contract(down_ref[:half, :], rows_ref[toks:, at], 1, 1)
 
     def backward(pair_ref, at):
         part = jnp.dot(left[...], pair_ref[...], preferred_element_type=jnp.float32)
@@ -268,7 +269,7 @@
     for first in range(0, wide, LANES):
         at = slice(first, first + LANES)
         up_at = slice(wide + first, wide + first + LANES)
-        gate, up, grad = acc[:, at], acc[:, up_at], acc_grad[:, at]
+        gate, up, grad = acc[at, :].T, acc[up_at, :].T, acc_grad[at, :].T
         sigmoid = jax.nn.sigmoid(gate)
         active = gate * sigmoid
         grad_gate = grad * up * sigmoid * (1.0 + gate * (1.0 - sigmoid))
@@ -309,8 +310,8 @@
         scratch_shapes=[
             pltpu.VMEM((rest, 2 * wide, CHUNK), jnp.bfloat16),
             pltpu.VMEM((rest, wide, CHUNK), jnp.bfloat16),
-            pltpu.VMEM((toks, 2 * wide), jnp.float32),
-            pltpu.VMEM((toks, wide), jnp.float32),
+            pltpu.VMEM((2 * wide, toks), jnp.float32),
+            pltpu.VMEM((wide, toks), jnp.float32),
             pltpu.VMEM((toks, 2 * wide), jnp.bfloat16),
             pltpu.VMEM((toks, LANES), jnp.float32),
             pltpu.SemaphoreType.DMA((rest, 3)),

time: 54.1 us -> 53.2 us (0.983)
  Pallas kernels: 33.3 us -> 32.3 us
    pallas_call x1, Pallas kernels: 14.6 us -> 13.7 us  [hidden_pass(): pl.pallas_call(functools.partial(hidden_kernel, len(fetched)), out_shape=...]
  transfers between devices with their start and end apart: 15 -> 15, of which waited for: 2 -> 2; matrix products, arithmetic and copies ran while one was open for 0% -> 0% of each run, Pallas kernels for 32% -> 33%
where the time goes in v7:
time: 53.2 us; the launch traced here: 53 us
  Pallas kernels  32.3 us (61%)
  starting transfers between devices  17.3 us (33%)
  waiting for transfers between devices  1.77 us (3%)
  between operations  0.82 us (2%)
  other arithmetic  0.79 us (1%)
    ppermute x15, starting transfers between devices, exchange(): return lax.ppermute(value, axis, [(i, i ^ bits) for i in range(count)])  17.3 us
    pallas_call x1, Pallas kernels, hidden_pass(): pl.pallas_call(functools.partial(hidden_kernel, len(fetched)), out_shape=...  13.7 us
    pallas_call x3, Pallas kernels, weight_pass(): pl.pallas_call(functools.partial(weight_kernel, toks, spans, len(packs)),...  11.7 us
    pallas_call x2, Pallas kernels, fetch_weights(): pl.pallas_call(functools.partial(fetch_kernel, chunk), out_shape=(pltpu.V...  5.57 us
    ppermute x15, waiting for transfers between devices, exchange(): return lax.ppermute(value, axis, [(i, i ^ bits) for i in range(count)])  1.77 us
  transfers between devices with their start and end apart: 15, of which 2 were waited for; matrix products, arithmetic and copies ran while one was open for 0% of the time, Pallas kernels for 33%

profile of v7, /device:TPU:0, one launch (start us, length us, event | category | flops | bytes accessed | tf_op | source)
XLA Modules:
  0.0 53.0 jit_solution(4609941710046658097)
XLA Ops:
  0.6 0.8 %pad_maximum_fusion.refs_4_.refs_0_ = bf16[4,5120]{1,0:T(4,128)(2,1)S(1)} fusion(bf16[2,5120]{1,0:T(2,128)(2,1)} %bitcast.11, bf16[2,5120]{1,0:T(2,128)(2,1)} %bitcast.9), kind=kLoop, calls=%fused_computation | loop fusion | flops 81920 | bytes 81920 | tf_op jit(solution)/shard_map/concatenate | solution.py:489
  1.4 5.1 %collective-permute-start.2 = (bf16[4,5120]{1,0:T(4,128)(2,1)S(1)}, bf16[4,5120]{1,0:T(4,128)(2,1)S(1)}, u32[]{:S(2)}, u32[]{:S(2)}) collective-permute-start(bf16[4,5120]{1,0:T(4,128)(2,1)S(1)} %pad_maximum_fusion.refs_4_.refs_0_), channel_id=1, source_target_pairs={{0,12},{2,14},{4,8},{6,10},{8,4},{10,6},{12,0},{14,2},{1,13},{3,15... | collective-permute-start | bytes 122888 | tf_op jit(solution)/shard_map/ppermute | solution.py:90
  6.5 0.6 %collective-permute-start = (bf16[4,5120]{1,0:T(4,128)(2,1)S(1)}, bf16[4,5120]{1,0:T(4,128)(2,1)S(1)}, u32[]{:S(2)}, u32[]{:S(2)}) collective-permute-start(bf16[4,5120]{1,0:T(4,128)(2,1)S(1)} %pad_maximum_fusion.refs_4_.refs_0_), channel_id=1, source_target_pairs={{0,4},{2,6},{4,0},{6,2},{8,12},{10,14},{12,8},{14,10},{1,5},{3,7},... | collective-permute-start | bytes 122888 | tf_op jit(solution)/shard_map/ppermute | solution.py:90
  7.2 1.6 %collective-permute-start.3 = (bf16[4,5120]{1,0:T(4,128)(2,1)S(1)}, bf16[4,5120]{1,0:T(4,128)(2,1)S(1)}, u32[]{:S(2)}, u32[]{:S(2)}) collective-permute-start(bf16[4,5120]{1,0:T(4,128)(2,1)S(1)} %pad_maximum_fusion.refs_4_.refs_0_), channel_id=1, source_target_pairs={{0,2},{2,0},{4,6},{6,4},{8,10},{10,8},{12,14},{14,12},{1,3},{3,1},... | collective-permute-start | bytes 122888 | tf_op jit(solution)/shard_map/ppermute | solution.py:90
  8.8 2.5 %fetch_weights.2 = (bf16[1792,1024]{1,0:T(8,128)(2,1)S(1)}, bf16[896,1024]{1,0:T(8,128)(2,1)S(1)}, f32[1,5120]{1,0:T(1,128)S(1)}, f32[8,128]{1,0:T(8,128)S(1)}) custom-call(bf16[1600,5120]{1,0:T(8,128)(2,1)} %bitcast.13, bf16[1600,5120]{1,0:T(8,128)(2,1)} %bitcast.16, bf16[1600,5120]{1,0:T(8,128)(2,1)} %refs_2_.5, f32[1,5120]{1,0:T(1,128)} %bitcast.21, ...), custom_call_target="tpu_custom_call" | custom-call | bytes 4915200 | tf_op jit(solution)/shard_map/fetch_weights/pallas_call | solution.py:185
  11.5 1.6 %collective-permute-start.5 = (bf16[4,5120]{1,0:T(4,128)(2,1)S(1)}, bf16[4,5120]{1,0:T(4,128)(2,1)S(1)}, u32[]{:S(2)}, u32[]{:S(2)}) collective-permute-start(bf16[4,5120]{1,0:T(4,128)(2,1)S(1)} %get-tuple-element.45.refs_2_), channel_id=1, source_target_pairs={{0,2},{2,0},{4,6},{6,4},{8,10},{10,8},{12,14},{14,12},{1,3},{3,1},... | collective-permute-start | bytes 122888 | tf_op jit(solution)/shard_map/ppermute | solution.py:90
  13.0 0.5 %collective-permute-start.6 = (bf16[4,5120]{1,0:T(4,128)(2,1)S(1)}, bf16[4,5120]{1,0:T(4,128)(2,1)S(1)}, u32[]{:S(2)}, u32[]{:S(2)}) collective-permute-start(bf16[4,5120]{1,0:T(4,128)(2,1)S(1)} %get-tuple-element.46.refs_3_), channel_id=1, source_target_pairs={{0,2},{2,0},{4,6},{6,4},{8,10},{10,8},{12,14},{14,12},{1,3},{3,1},... | collective-permute-start | bytes 122888 | tf_op jit(solution)/shard_map/ppermute | solution.py:90
  13.6 1.5 %collective-permute-start.4 = (bf16[4,5120]{1,0:T(4,128)(2,1)S(1)}, bf16[4,5120]{1,0:T(4,128)(2,1)S(1)}, u32[]{:S(2)}, u32[]{:S(2)}) collective-permute-start(bf16[4,5120]{1,0:T(4,128)(2,1)S(1)} %get-tuple-element.44.refs_4_.refs_1_), channel_id=1, source_target_pairs={{0,2},{2,0},{4,6},{6,4},{8,10},{10,8},{12,14},{14,12},{1,3},{3,1},... | collective-permute-start | bytes 122888 | tf_op jit(solution)/shard_map/ppermute | solution.py:90
  15.0 3.1 %fetch_weights.3 = (bf16[1792,1024]{1,0:T(8,128)(2,1)S(1)}, bf16[896,1024]{1,0:T(8,128)(2,1)S(1)}, f32[1,5120]{1,0:T(1,128)}, f32[8,128]{1,0:T(8,128)S(1)}) custom-call(bf16[1600,5120]{1,0:T(8,128)(2,1)} %bitcast.14, bf16[1600,5120]{1,0:T(8,128)(2,1)} %bitcast.17, bf16[1600,5120]{1,0:T(8,128)(2,1)} %refs_2_.5, f32[1,5120]{1,0:T(1,128)} %bitcast.22, ...), custom_call_target="tpu_custom_call" | custom-call | bytes 4915200 | tf_op jit(solution)/shard_map/fetch_weights/pallas_call | solution.py:185
  18.2 0.2 sort_rows.1.own_ref
  18.5 1.6 %collective-permute-done.7.peer_ref = bf16[32,5120]{1,0:T(8,128)(2,1)S(1)} collective-permute-done((bf16[32,5120]{1,0:T(8,128)(2,1)S(1)}, bf16[32,5120]{1,0:T(8,128)(2,1)S(1)}, u32[]{:S(2)}, u32[]{:S(2)}) %collective-permute-start.7) | collective-permute-done | bytes 327712 | tf_op jit(solution)/shard_map/ppermute | solution.py:90
  20.1 13.7 %hidden_pass.1 = (bf16[800,128]{1,0:T(8,128)(2,1)S(1)}, f32[16,5120]{1,0:T(8,128)S(1)}, bf16[18,5120]{1,0:T(8,128)(2,1)S(1)}, f32[1,5120]{1,0:T(1,128)S(1)}, bf16[64,5120]{1,0:T(8,128)(2,1)S(1)}) custom-call(bf16[32,5120]{1,0:T(8,128)(2,1)S(1)} %sort_rows.1.own_ref, bf16[32,5120]{1,0:T(8,128)(2,1)S(1)} %collective-permute-done.7.peer_ref, ...), custom_call_target="tpu_custom_call" | custom-call | flops 1310720000 | bytes 24576000 | tf_op jit(solution)/shard_map/hidden_pass/pallas_call | solution.py:299
  33.8 0.2 collective-permute-start.8
  34.0 0.4 collective-permute-start.11
  34.4 2.7 %weight_pass.3 = (bf16[1600,2560]{1,0:T(8,128)(2,1)}, bf16[1600,2560]{1,0:T(8,128)(2,1)}, bf16[1600,2560]{1,0:T(8,128)(2,1)}, f32[8,128]{1,0:T(8,128)S(1)}) custom-call(bf16[800,128]{1,0:T(8,128)(2,1)S(1)} %get-tuple-element.55.refs_0_, bf16[64,5120]{1,0:T(8,128)(2,1)S(1)} %get-tuple-element.56.refs_1_.refs_2_), custom_call_target="tpu_custom_call" | custom-call | flops 157286400 | bytes 4915200 | tf_op jit(solution)/shard_map/weight_pass/pallas_call | solution.py:379
  37.1 0.1 fold.1
  37.2 0.9 %collective-permute-start.9 = (bf16[8,5120]{1,0:T(8,128)(2,1)S(1)}, bf16[8,5120]{1,0:T(8,128)(2,1)S(1)}, u32[]{:S(2)}, u32[]{:S(2)}) collective-permute-start(bf16[8,5120]{1,0:T(8,128)(2,1)S(1)} %get-tuple-element.60.refs_6_), channel_id=1, source_target_pairs={{0,2},{2,0},{4,6},{6,4},{8,10},{10,8},{12,14},{14,12},{1,3},{3,1},... | collective-permute-start | bytes 245768 | tf_op jit(solution)/shard_map/ppermute | solution.py:90
  38.1 1.2 %collective-permute-start.10 = (bf16[2,5120]{1,0:T(2,128)(2,1)S(1)}, bf16[2,5120]{1,0:T(2,128)(2,1)S(1)}, u32[]{:S(2)}, u32[]{:S(2)}) collective-permute-start(bf16[2,5120]{1,0:T(2,128)(2,1)S(1)} %get-tuple-element.61), channel_id=1, source_target_pairs={{0,2},{2,0},{4,6},{6,4},{8,10},{10,8},{12,14},{14,12},{1,3},{3,1},... | collective-permute-start | bytes 61448 | tf_op jit(solution)/shard_map/ppermute | solution.py:90
  39.3 4.2 %weight_pass.4 = (bf16[1600,2560]{1,0:T(8,128)(2,1)}, bf16[1600,2560]{1,0:T(8,128)(2,1)}, bf16[1600,2560]{1,0:T(8,128)(2,1)}, f32[8,128]{1,0:T(8,128)S(1)}) custom-call(bf16[800,128]{1,0:T(8,128)(2,1)S(1)} %get-tuple-element.55.refs_0_, ...), custom_call_target="tpu_custom_call", output_to_operand_aliasing={{0}: (3, {}), {1}: (4, {}), {2}: (5, {})} | custom-call | flops 314572800 | bytes 9830400 | tf_op jit(solution)/shard_map/weight_pass/pallas_call | solution.py:379
  43.7 2.1 %collective-permute-start.13 = (bf16[4,5120]{1,0:T(4,128)(2,1)S(1)}, bf16[4,5120]{1,0:T(4,128)(2,1)S(1)}, u32[]{:S(2)}, u32[]{:S(2)}) collective-permute-start(bf16[4,5120]{1,0:T(4,128)(2,1)S(1)} %get-tuple-element.69), channel_id=1, source_target_pairs={{0,8},{2,10},{4,12},{6,14},{8,0},{10,2},{12,4},{14,6},{1,9},{3,11}... | collective-permute-start | bytes 122888 | tf_op jit(solution)/shard_map/ppermute | solution.py:90
  45.8 0.9 %collective-permute-start.14 = (bf16[4,5120]{1,0:T(4,128)(2,1)S(1)}, bf16[4,5120]{1,0:T(4,128)(2,1)S(1)}, u32[]{:S(2)}, u32[]{:S(2)}) collective-permute-start(bf16[4,5120]{1,0:T(4,128)(2,1)S(1)} %get-tuple-element.70), channel_id=1, source_target_pairs={{0,12},{2,14},{4,8},{6,10},{8,4},{10,6},{12,0},{14,2},{1,13},{3,15... | collective-permute-start | bytes 122888 | tf_op jit(solution)/shard_map/ppermute | solution.py:90
  46.7 0.5 %collective-permute-start.12 = (bf16[4,5120]{1,0:T(4,128)(2,1)S(1)}, bf16[4,5120]{1,0:T(4,128)(2,1)S(1)}, u32[]{:S(2)}, u32[]{:S(2)}) collective-permute-start(bf16[4,5120]{1,0:T(4,128)(2,1)S(1)} %get-tuple-element.68.refs_5_), channel_id=1, source_target_pairs={{0,4},{2,6},{4,0},{6,2},{8,12},{10,14},{12,8},{14,10},{1,5},{3,7},... | collective-permute-start | bytes 122888 | tf_op jit(solution)/shard_map/ppermute | solution.py:90
  47.2 4.8 %weight_pass.5 = (bf16[1600,2560]{1,0:T(8,128)(2,1)}, bf16[1600,2560]{1,0:T(8,128)(2,1)}, bf16[1600,2560]{1,0:T(8,128)(2,1)}, f32[8,128]{1,0:T(8,128)}) custom-call(bf16[800,128]{1,0:T(8,128)(2,1)S(1)} %collective-permute-done.11.refs_1_.refs_0_, ...), custom_call_target="tpu_custom_call", output_to_operand_aliasing={{0}: (2, {}), {1}: (3, {}), {2}: (4, {})} | custom-call | flops 314572800 | bytes 9830400 | tf_op jit(solution)/shard_map/weight_pass/pallas_call | solution.py:379
  52.1 0.9 %finish.1 = (bf16[2,5120]{1,0:T(2,128)(2,1)}, f32[1,5120]{1,0:T(1,128)}) custom-call(bf16[2,5120]{1,0:T(2,128)(2,1)S(1)} %bitcast.10, bf16[2,5120]{1,0:T(2,128)(2,1)S(1)} %bitcast.12, f32[1,5120]{1,0:T(1,128)S(1)} %get-tuple-element.42.gain_ref.norm_gain_ref, f32[2,5120]{1,0:T(2,128)S(1)} %get-tuple-element.66.own_ref, ...), custom_call_target="tpu_custom_call" | custom-call | tf_op jit(solution)/shard_map/finish/pallas_call | solution.py:466
  (22 shorter events, 0.4 us)
Async XLA Ops:
  1.4 9.9 %collective-permute-start.2 = (bf16[4,5120]{1,0:T(4,128)(2,1)S(1)}, bf16[4,5120]{1,0:T(4,128)(2,1)S(1)}, u32[]{:S(2)}, u32[]{:S(2)}) collective-permute-start(bf16[4,5120]{1,0:T(4,128)(2,1)S(1)} %pad_maximum_fusion.refs_4_.refs_0_), channel_id=1, source_target_pairs={{0,12},{2,14},{4,8},{6,10},{8,4},{10,6},{12,0},{14,2},{1,13},{3,15... | collective-permute-start | bytes 122888 | tf_op jit(solution)/shard_map/ppermute | solution.py:90
  6.5 4.9 %collective-permute-start.1 = (bf16[4,5120]{1,0:T(4,128)(2,1)S(1)}, bf16[4,5120]{1,0:T(4,128)(2,1)S(1)}, u32[]{:S(2)}, u32[]{:S(2)}) collective-permute-start(bf16[4,5120]{1,0:T(4,128)(2,1)S(1)} %pad_maximum_fusion.refs_4_.refs_0_), channel_id=1, source_target_pairs={{0,8},{2,10},{4,12},{6,14},{8,0},{10,2},{12,4},{14,6},{1,9},{3,11}... | collective-permute-start | bytes 122888 | tf_op jit(solution)/shard_map/ppermute | solution.py:90
  6.5 4.9 %collective-permute-start = (bf16[4,5120]{1,0:T(4,128)(2,1)S(1)}, bf16[4,5120]{1,0:T(4,128)(2,1)S(1)}, u32[]{:S(2)}, u32[]{:S(2)}) collective-permute-start(bf16[4,5120]{1,0:T(4,128)(2,1)S(1)} %pad_maximum_fusion.refs_4_.refs_0_), channel_id=1, source_target_pairs={{0,4},{2,6},{4,0},{6,2},{8,12},{10,14},{12,8},{14,10},{1,5},{3,7},... | collective-permute-start | bytes 122888 | tf_op jit(solution)/shard_map/ppermute | solution.py:90
  7.2 11.0 %collective-permute-start.3 = (bf16[4,5120]{1,0:T(4,128)(2,1)S(1)}, bf16[4,5120]{1,0:T(4,128)(2,1)S(1)}, u32[]{:S(2)}, u32[]{:S(2)}) collective-permute-start(bf16[4,5120]{1,0:T(4,128)(2,1)S(1)} %pad_maximum_fusion.refs_4_.refs_0_), channel_id=1, source_target_pairs={{0,2},{2,0},{4,6},{6,4},{8,10},{10,8},{12,14},{14,12},{1,3},{3,1},... | collective-permute-start | bytes 122888 | tf_op jit(solution)/shard_map/ppermute | solution.py:90
  11.5 6.7 %collective-permute-start.5 = (bf16[4,5120]{1,0:T(4,128)(2,1)S(1)}, bf16[4,5120]{1,0:T(4,128)(2,1)S(1)}, u32[]{:S(2)}, u32[]{:S(2)}) collective-permute-start(bf16[4,5120]{1,0:T(4,128)(2,1)S(1)} %get-tuple-element.45.refs_2_), channel_id=1, source_target_pairs={{0,2},{2,0},{4,6},{6,4},{8,10},{10,8},{12,14},{14,12},{1,3},{3,1},... | collective-permute-start | bytes 122888 | tf_op jit(solution)/shard_map/ppermute | solution.py:90
  13.0 5.1 %collective-permute-start.6 = (bf16[4,5120]{1,0:T(4,128)(2,1)S(1)}, bf16[4,5120]{1,0:T(4,128)(2,1)S(1)}, u32[]{:S(2)}, u32[]{:S(2)}) collective-permute-start(bf16[4,5120]{1,0:T(4,128)(2,1)S(1)} %get-tuple-element.46.refs_3_), channel_id=1, source_target_pairs={{0,2},{2,0},{4,6},{6,4},{8,10},{10,8},{12,14},{14,12},{1,3},{3,1},... | collective-permute-start | bytes 122888 | tf_op jit(solution)/shard_map/ppermute | solution.py:90
  13.6 4.6 %collective-permute-start.4 = (bf16[4,5120]{1,0:T(4,128)(2,1)S(1)}, bf16[4,5120]{1,0:T(4,128)(2,1)S(1)}, u32[]{:S(2)}, u32[]{:S(2)}) collective-permute-start(bf16[4,5120]{1,0:T(4,128)(2,1)S(1)} %get-tuple-element.44.refs_4_.refs_1_), channel_id=1, source_target_pairs={{0,2},{2,0},{4,6},{6,4},{8,10},{10,8},{12,14},{14,12},{1,3},{3,1},... | collective-permute-start | bytes 122888 | tf_op jit(solution)/shard_map/ppermute | solution.py:90
  18.4 1.7 %collective-permute-start.7 = (bf16[32,5120]{1,0:T(8,128)(2,1)S(1)}, bf16[32,5120]{1,0:T(8,128)(2,1)S(1)}, u32[]{:S(2)}, u32[]{:S(2)}) collective-permute-start(bf16[32,5120]{1,0:T(8,128)(2,1)S(1)} %sort_rows.1.own_ref), channel_id=1, source_target_pairs={{0,1},{1,0},{2,3},{3,2},{4,5},{5,4},{6,7},{7,6},{8,9},{9,8},{10,11... | collective-permute-start | bytes 983048 | tf_op jit(solution)/shard_map/ppermute | solution.py:90
  33.8 3.3 %collective-permute-start.8 = (bf16[18,5120]{1,0:T(8,128)(2,1)S(1)}, bf16[18,5120]{1,0:T(8,128)(2,1)S(1)}, u32[]{:S(2)}, u32[]{:S(2)}) collective-permute-start(bf16[18,5120]{1,0:T(8,128)(2,1)S(1)} %get-tuple-element.54), channel_id=1, source_target_pairs={{0,1},{1,0},{2,3},{3,2},{4,5},{5,4},{6,7},{7,6},{8,9},{9,8},{10,11... | collective-permute-start | bytes 552968 | tf_op jit(solution)/shard_map/ppermute | solution.py:90
  34.0 5.3 %collective-permute-start.11 = (bf16[800,128]{1,0:T(8,128)(2,1)S(1)}, bf16[800,128]{1,0:T(8,128)(2,1)S(1)}, u32[]{:S(2)}, u32[]{:S(2)}) collective-permute-start(bf16[800,128]{1,0:T(8,128)(2,1)S(1)} %get-tuple-element.55.refs_0_), channel_id=1, source_target_pairs={{0,1},{1,0},{2,3},{3,2},{4,5},{5,4},{6,7},{7,6},{8,9},{9,8},{10,11... | collective-permute-start | bytes 614408 | tf_op jit(solution)/shard_map/ppermute | solution.py:90
  37.2 6.3 %collective-permute-start.9 = (bf16[8,5120]{1,0:T(8,128)(2,1)S(1)}, bf16[8,5120]{1,0:T(8,128)(2,1)S(1)}, u32[]{:S(2)}, u32[]{:S(2)}) collective-permute-start(bf16[8,5120]{1,0:T(8,128)(2,1)S(1)} %get-tuple-element.60.refs_6_), channel_id=1, source_target_pairs={{0,2},{2,0},{4,6},{6,4},{8,10},{10,8},{12,14},{14,12},{1,3},{3,1},... | collective-permute-start | bytes 245768 | tf_op jit(solution)/shard_map/ppermute | solution.py:90
  38.1 5.4 %collective-permute-start.10 = (bf16[2,5120]{1,0:T(2,128)(2,1)S(1)}, bf16[2,5120]{1,0:T(2,128)(2,1)S(1)}, u32[]{:S(2)}, u32[]{:S(2)}) collective-permute-start(bf16[2,5120]{1,0:T(2,128)(2,1)S(1)} %get-tuple-element.61), channel_id=1, source_target_pairs={{0,2},{2,0},{4,6},{6,4},{8,10},{10,8},{12,14},{14,12},{1,3},{3,1},... | collective-permute-start | bytes 61448 | tf_op jit(solution)/shard_map/ppermute | solution.py:90
  43.7 8.4 %collective-permute-start.13 = (bf16[4,5120]{1,0:T(4,128)(2,1)S(1)}, bf16[4,5120]{1,0:T(4,128)(2,1)S(1)}, u32[]{:S(2)}, u32[]{:S(2)}) collective-permute-start(bf16[4,5120]{1,0:T(4,128)(2,1)S(1)} %get-tuple-element.69), channel_id=1, source_target_pairs={{0,8},{2,10},{4,12},{6,14},{8,0},{10,2},{12,4},{14,6},{1,9},{3,11}... | collective-permute-start | bytes 122888 | tf_op jit(solution)/shard_map/ppermute | solution.py:90
  45.8 6.3 %collective-permute-start.14 = (bf16[4,5120]{1,0:T(4,128)(2,1)S(1)}, bf16[4,5120]{1,0:T(4,128)(2,1)S(1)}, u32[]{:S(2)}, u32[]{:S(2)}) collective-permute-start(bf16[4,5120]{1,0:T(4,128)(2,1)S(1)} %get-tuple-element.70), channel_id=1, source_target_pairs={{0,12},{2,14},{4,8},{6,10},{8,4},{10,6},{12,0},{14,2},{1,13},{3,15... | collective-permute-start | bytes 122888 | tf_op jit(solution)/shard_map/ppermute | solution.py:90
  46.7 5.4 %collective-permute-start.12 = (bf16[4,5120]{1,0:T(4,128)(2,1)S(1)}, bf16[4,5120]{1,0:T(4,128)(2,1)S(1)}, u32[]{:S(2)}, u32[]{:S(2)}) collective-permute-start(bf16[4,5120]{1,0:T(4,128)(2,1)S(1)} %get-tuple-element.68.refs_5_), channel_id=1, source_target_pairs={{0,4},{2,6},{4,0},{6,2},{8,12},{10,14},{12,8},{14,10},{1,5},{3,7},... | collective-permute-start | bytes 122888 | tf_op jit(solution)/shard_map/ppermute | solution.py:90
  47.2 4.8 %copy-start = (bf16[1,2,1,5120]{3,1,2,0:T(2,128)(2,1)S(1)}, bf16[1,2,1,5120]{3,1,2,0:T(2,128)(2,1)}, u32[]{:S(2)}) copy-start(bf16[1,2,1,5120]{3,1,2,0:T(2,128)(2,1)} %param.6) | copy-start | bytes 61444
  47.2 4.8 %copy-start.1 = (bf16[1,2,1,5120]{3,1,2,0:T(2,128)(2,1)S(1)}, bf16[1,2,1,5120]{3,1,2,0:T(2,128)(2,1)}, u32[]{:S(2)}) copy-start(bf16[1,2,1,5120]{3,1,2,0:T(2,128)(2,1)} %param.11) | copy-start | bytes 61444

commit v8 on v7

--- a/solution.py
+++ b/solution.py
@@ -10,7 +10,7 @@
 EPSILON = 1e-06
 LANES = 128
 MIB = 1 << 20
-CHUNK = 1024
+CHUNK = 512
 ALONG_Z = (2, 4, 6)
 
 
@@ -163,15 +163,18 @@
         pair_ref[wide + half :, :] = zeros
 
 
-def fetch_kernel(chunk, *refs):
+def fetch_kernel(first, count, *refs):
     sources, gain_hbm = refs[:3], refs[3]
-    pair_ref, down_ref, gain_ref, done_ref, sems, gain_sem = refs[-6:]
+    gain_ref, done_ref, sems, gain_sem = refs[-4:]
+    targets = refs[-4 - 2 * count : -4]
     copies = [pltpu.make_async_copy(gain_hbm, gain_ref, gain_sem)]
-    copies += chunk_copies(sources, chunk, pair_ref, down_ref, sems)
+    for c in range(count):
+        copies += chunk_copies(sources, first + c, *targets[2 * c : 2 * c + 2], sems.at[c])
     for copy in copies:
         copy.start()
     done_ref[...] = jnp.zeros_like(done_ref)
-    clear_between(pair_ref, down_ref, sources[2].shape[0] // 2)
+    for c in range(count):
+        clear_between(*targets[2 * c : 2 * c + 2], sources[2].shape[0] // 2)
     for copy in copies:
         copy.wait()
 
@@ -180,26 +183,29 @@
     return [pltpu.with_memory_space_constraint(x, pltpu.HBM) for x in arrays]
 
 
-def fetch_weights(weights, gain, chunk, after=()):
+def fetch_weights(weights, gain, first, count, after=()):
     half = weights[2].shape[0] // 2
-    pair, down, gain, done = pl.pallas_call(
-        functools.partial(fetch_kernel, chunk),
+    *chunks, gain, done = pl.pallas_call(
+        functools.partial(fetch_kernel, first, count),
         out_shape=(
             pltpu.VMEM((2 * padded(half), CHUNK), jnp.bfloat16),
             pltpu.VMEM((padded(half), CHUNK), jnp.bfloat16),
+        )
+        * count
+        + (
             pltpu.VMEM(gain.shape, gain.dtype),
             pltpu.VMEM((8, LANES), jnp.float32),
         ),
         in_specs=[ANY_SPEC] * (4 + len(after)),
-        out_specs=(VMEM_SPEC,) * 4,
-        scratch_shapes=[pltpu.SemaphoreType.DMA((3,)), pltpu.SemaphoreType.DMA(())],
+        out_specs=(VMEM_SPEC,) * (2 * count + 2),
+        scratch_shapes=[pltpu.SemaphoreType.DMA((count, 3)), pltpu.SemaphoreType.DMA(())],
         compiler_params=pltpu.CompilerParams(vmem_limit_bytes=4 * MIB),
         cost_estimate=pl.CostEstimate(
-            flops=0, bytes_accessed=6 * half * CHUNK, transcendentals=0
+            flops=0, bytes_accessed=6 * half * CHUNK * count, transcendentals=0
         ),
         name="fetch_weights",
     )(*in_hbm((*weights, gain)), *after)
-    return (pair, down), gain, done
+    return list(zip(chunks[::2], chunks[1::2])), gain, done
 
 
 def hidden_kernel(ready, own_ref, peer_ref, gain_ref, *refs):
@@ -489,13 +495,13 @@
     piece = jnp.concatenate([own_tokens, own_incoming], axis=0)
     near = exchange(piece, "tp", 1)
     along = [exchange(piece, "tp", bits) for bits in ALONG_Z]
-    fetched, gain_row, done = fetch_weights(weights, gain_hbm, 0, (piece,))
+    fetched, gain_row, done = fetch_weights(weights, gain_hbm, 0, 2, (piece,))
     along = relay(along, done)
     across = [exchange(arrived, "tp", 1) for arrived in along]
-    more, _, done = fetch_weights(weights, gain_hbm, 1, (along[0],))
+    more, _, done = fetch_weights(weights, gain_hbm, 2, 1, (along[0],))
     own = sort_rows(rows, [piece, *along, near, *across], done)
     peer = exchange(own, "dp", 1)
-    packed, kept, send, gain, all_rows = hidden_pass(own, peer, gain_row, weights, [fetched, more])
+    packed, kept, send, gain, all_rows = hidden_pass(own, peer, gain_row, weights, fetched + more)
     arrived = exchange(send, "dp", 1)
     peer_packed = exchange(packed, "dp", 1)
     cut, turn = blocks // 2, blocks // 3

time: 53.2 us -> 53.4 us (level)
  starting transfers between devices: 17.3 us -> 17.9 us
    pallas_call x2, Pallas kernels: 5.57 us -> 4.8 us  [fetch_weights(): pl.pallas_call(functools.partial(fetch_kernel, first, count), out_shape=(...]
    ppermute x15, starting transfers between devices: 17.3 us -> 17.9 us  [exchange(): return lax.ppermute(value, axis, [(i, i ^ bits) for i in range(count)])]
  transfers between devices with their start and end apart: 15 -> 15, of which waited for: 2 -> 3; matrix products, arithmetic and copies ran while one was open for 0% -> 0% of each run, Pallas kernels for 33% -> 31%
where the time goes in v8:
time: 53.4 us; the launch traced here: 53.2 us
  Pallas kernels  31.8 us (60%)
  starting transfers between devices  17.9 us (34%)
  waiting for transfers between devices  1.93 us (4%)
  between operations  0.81 us (2%)
  other arithmetic  0.79 us (1%)
    ppermute x15, starting transfers between devices, exchange(): return lax.ppermute(value, axis, [(i, i ^ bits) for i in range(count)])  17.9 us
    pallas_call x1, Pallas kernels, hidden_pass(): pl.pallas_call(functools.partial(hidden_kernel, len(fetched)), out_shape=...  14 us
    pallas_call x3, Pallas kernels, weight_pass(): pl.pallas_call(functools.partial(weight_kernel, toks, spans, len(packs)),...  11.7 us
    pallas_call x2, Pallas kernels, fetch_weights(): pl.pallas_call(functools.partial(fetch_kernel, first, count), out_shape=(...  4.8 us
    ppermute x15, waiting for transfers between devices, exchange(): return lax.ppermute(value, axis, [(i, i ^ bits) for i in range(count)])  1.93 us
  transfers between devices with their start and end apart: 15, of which 3 were waited for; matrix products, arithmetic and copies ran while one was open for 0% of the time, Pallas kernels for 31%

profile of v8, /device:TPU:0, one launch (start us, length us, event | category | flops | bytes accessed | tf_op | source)
XLA Modules:
  0.0 53.2 jit_solution(3246723208512328519)
XLA Ops:
  0.6 0.8 %pad_maximum_fusion.refs_4_.refs_0_ = bf16[4,5120]{1,0:T(4,128)(2,1)S(1)} fusion(bf16[2,5120]{1,0:T(2,128)(2,1)} %bitcast.11, bf16[2,5120]{1,0:T(2,128)(2,1)} %bitcast.9), kind=kLoop, calls=%fused_computation | loop fusion | flops 81920 | bytes 81920 | tf_op jit(solution)/shard_map/concatenate | solution.py:495
  1.4 5.1 %collective-permute-start.2 = (bf16[4,5120]{1,0:T(4,128)(2,1)S(1)}, bf16[4,5120]{1,0:T(4,128)(2,1)S(1)}, u32[]{:S(2)}, u32[]{:S(2)}) collective-permute-start(bf16[4,5120]{1,0:T(4,128)(2,1)S(1)} %pad_maximum_fusion.refs_4_.refs_0_), channel_id=1, source_target_pairs={{0,12},{2,14},{4,8},{6,10},{8,4},{10,6},{12,0},{14,2},{1,13},{3,15... | collective-permute-start | bytes 122888 | tf_op jit(solution)/shard_map/ppermute | solution.py:90
  6.5 0.6 %collective-permute-start = (bf16[4,5120]{1,0:T(4,128)(2,1)S(1)}, bf16[4,5120]{1,0:T(4,128)(2,1)S(1)}, u32[]{:S(2)}, u32[]{:S(2)}) collective-permute-start(bf16[4,5120]{1,0:T(4,128)(2,1)S(1)} %pad_maximum_fusion.refs_4_.refs_0_), channel_id=1, source_target_pairs={{0,4},{2,6},{4,0},{6,2},{8,12},{10,14},{12,8},{14,10},{1,5},{3,7},... | collective-permute-start | bytes 122888 | tf_op jit(solution)/shard_map/ppermute | solution.py:90
  7.2 1.6 %collective-permute-start.3 = (bf16[4,5120]{1,0:T(4,128)(2,1)S(1)}, bf16[4,5120]{1,0:T(4,128)(2,1)S(1)}, u32[]{:S(2)}, u32[]{:S(2)}) collective-permute-start(bf16[4,5120]{1,0:T(4,128)(2,1)S(1)} %pad_maximum_fusion.refs_4_.refs_0_), channel_id=1, source_target_pairs={{0,2},{2,0},{4,6},{6,4},{8,10},{10,8},{12,14},{14,12},{1,3},{3,1},... | collective-permute-start | bytes 122888 | tf_op jit(solution)/shard_map/ppermute | solution.py:90
  8.8 2.5 %fetch_weights.2 = (bf16[1792,512]{1,0:T(8,128)(2,1)S(1)}, bf16[896,512]{1,0:T(8,128)(2,1)S(1)}, bf16[1792,512]{1,0:T(8,128)(2,1)S(1)}, bf16[896,512]{1,0:T(8,12...) custom-call(bf16[1600,5120]{1,0:T(8,128)(2,1)} %bitcast.13, bf16[1600,5120]{1,0:T(8,128)(2,1)} %bitcast.16, ...), custom_call_target="tpu_custom_call" | custom-call | bytes 4915200 | tf_op jit(solution)/shard_map/fetch_weights/pallas_call | solution.py:188
  11.5 1.6 %collective-permute-start.5 = (bf16[4,5120]{1,0:T(4,128)(2,1)S(1)}, bf16[4,5120]{1,0:T(4,128)(2,1)S(1)}, u32[]{:S(2)}, u32[]{:S(2)}) collective-permute-start(bf16[4,5120]{1,0:T(4,128)(2,1)S(1)} %get-tuple-element.47.refs_2_), channel_id=1, source_target_pairs={{0,2},{2,0},{4,6},{6,4},{8,10},{10,8},{12,14},{14,12},{1,3},{3,1},... | collective-permute-start | bytes 122888 | tf_op jit(solution)/shard_map/ppermute | solution.py:90
  13.0 0.5 %collective-permute-start.6 = (bf16[4,5120]{1,0:T(4,128)(2,1)S(1)}, bf16[4,5120]{1,0:T(4,128)(2,1)S(1)}, u32[]{:S(2)}, u32[]{:S(2)}) collective-permute-start(bf16[4,5120]{1,0:T(4,128)(2,1)S(1)} %get-tuple-element.48.refs_3_), channel_id=1, source_target_pairs={{0,2},{2,0},{4,6},{6,4},{8,10},{10,8},{12,14},{14,12},{1,3},{3,1},... | collective-permute-start | bytes 122888 | tf_op jit(solution)/shard_map/ppermute | solution.py:90
  13.6 1.5 %collective-permute-start.4 = (bf16[4,5120]{1,0:T(4,128)(2,1)S(1)}, bf16[4,5120]{1,0:T(4,128)(2,1)S(1)}, u32[]{:S(2)}, u32[]{:S(2)}) collective-permute-start(bf16[4,5120]{1,0:T(4,128)(2,1)S(1)} %get-tuple-element.46.refs_4_.refs_1_), channel_id=1, source_target_pairs={{0,2},{2,0},{4,6},{6,4},{8,10},{10,8},{12,14},{14,12},{1,3},{3,1},... | collective-permute-start | bytes 122888 | tf_op jit(solution)/shard_map/ppermute | solution.py:90
  15.0 2.3 %fetch_weights.3 = (bf16[1792,512]{1,0:T(8,128)(2,1)S(1)}, bf16[896,512]{1,0:T(8,128)(2,1)S(1)}, f32[1,5120]{1,0:T(1,128)}, f32[8,128]{1,0:T(8,128)S(1)}) custom-call(bf16[1600,5120]{1,0:T(8,128)(2,1)} %bitcast.14, bf16[1600,5120]{1,0:T(8,128)(2,1)} %bitcast.17, bf16[1600,5120]{1,0:T(8,128)(2,1)} %refs_2_.5, f32[1,5120]{1,0:T(1,128)} %bitcast.22, ...), custom_call_target="tpu_custom_call" | custom-call | bytes 2457600 | tf_op jit(solution)/shard_map/fetch_weights/pallas_call | solution.py:188
  17.4 0.2 collective-permute-done.4.refs_5_
  17.6 0.2 sort_rows.1.own_ref
  17.8 1.6 %collective-permute-done.7.peer_ref = bf16[32,5120]{1,0:T(8,128)(2,1)S(1)} collective-permute-done((bf16[32,5120]{1,0:T(8,128)(2,1)S(1)}, bf16[32,5120]{1,0:T(8,128)(2,1)S(1)}, u32[]{:S(2)}, u32[]{:S(2)}) %collective-permute-start.7) | collective-permute-done | bytes 327712 | tf_op jit(solution)/shard_map/ppermute | solution.py:90
  19.5 14.0 %hidden_pass.1 = (bf16[800,128]{1,0:T(8,128)(2,1)S(1)}, f32[16,5120]{1,0:T(8,128)S(1)}, bf16[18,5120]{1,0:T(8,128)(2,1)S(1)}, f32[1,5120]{1,0:T(1,128)S(1)}, bf16[64,5120]{1,0:T(8,128)(2,1)S(1)}) custom-call(bf16[32,5120]{1,0:T(8,128)(2,1)S(1)} %sort_rows.1.own_ref, bf16[32,5120]{1,0:T(8,128)(2,1)S(1)} %collective-permute-done.7.peer_ref, ...), custom_call_target="tpu_custom_call" | custom-call | flops 1310720000 | bytes 24576000 | tf_op jit(solution)/shard_map/hidden_pass/pallas_call | solution.py:305
  33.4 0.2 collective-permute-start.8
  33.6 0.4 collective-permute-start.11
  34.0 2.7 %weight_pass.3 = (bf16[1600,2560]{1,0:T(8,128)(2,1)}, bf16[1600,2560]{1,0:T(8,128)(2,1)}, bf16[1600,2560]{1,0:T(8,128)(2,1)}, f32[8,128]{1,0:T(8,128)S(1)}) custom-call(bf16[800,128]{1,0:T(8,128)(2,1)S(1)} %get-tuple-element.59.refs_0_, bf16[64,5120]{1,0:T(8,128)(2,1)S(1)} %get-tuple-element.60.refs_1_.refs_2_), custom_call_target="tpu_custom_call" | custom-call | flops 157286400 | bytes 4915200 | tf_op jit(solution)/shard_map/weight_pass/pallas_call | solution.py:385
  36.8 1.6 %collective-permute-start.9 = (bf16[8,5120]{1,0:T(8,128)(2,1)S(1)}, bf16[8,5120]{1,0:T(8,128)(2,1)S(1)}, u32[]{:S(2)}, u32[]{:S(2)}) collective-permute-start(bf16[8,5120]{1,0:T(8,128)(2,1)S(1)} %get-tuple-element.64.refs_6_), channel_id=1, source_target_pairs={{0,2},{2,0},{4,6},{6,4},{8,10},{10,8},{12,14},{14,12},{1,3},{3,1},... | collective-permute-start | bytes 245768 | tf_op jit(solution)/shard_map/ppermute | solution.py:90
  38.4 0.5 collective-permute-start.10
  38.9 4.2 %weight_pass.4 = (bf16[1600,2560]{1,0:T(8,128)(2,1)}, bf16[1600,2560]{1,0:T(8,128)(2,1)}, bf16[1600,2560]{1,0:T(8,128)(2,1)}, f32[8,128]{1,0:T(8,128)S(1)}) custom-call(bf16[800,128]{1,0:T(8,128)(2,1)S(1)} %get-tuple-element.59.refs_0_, ...), custom_call_target="tpu_custom_call", output_to_operand_aliasing={{0}: (3, {}), {1}: (4, {}), {2}: (5, {})} | custom-call | flops 314572800 | bytes 9830400 | tf_op jit(solution)/shard_map/weight_pass/pallas_call | solution.py:385
  43.3 2.1 %collective-permute-start.13 = (bf16[4,5120]{1,0:T(4,128)(2,1)S(1)}, bf16[4,5120]{1,0:T(4,128)(2,1)S(1)}, u32[]{:S(2)}, u32[]{:S(2)}) collective-permute-start(bf16[4,5120]{1,0:T(4,128)(2,1)S(1)} %get-tuple-element.73), channel_id=1, source_target_pairs={{0,8},{2,10},{4,12},{6,14},{8,0},{10,2},{12,4},{14,6},{1,9},{3,11}... | collective-permute-start | bytes 122888 | tf_op jit(solution)/shard_map/ppermute | solution.py:90
  45.4 1.5 %collective-permute-start.14 = (bf16[4,5120]{1,0:T(4,128)(2,1)S(1)}, bf16[4,5120]{1,0:T(4,128)(2,1)S(1)}, u32[]{:S(2)}, u32[]{:S(2)}) collective-permute-start(bf16[4,5120]{1,0:T(4,128)(2,1)S(1)} %get-tuple-element.74), channel_id=1, source_target_pairs={{0,12},{2,14},{4,8},{6,10},{8,4},{10,6},{12,0},{14,2},{1,13},{3,15... | collective-permute-start | bytes 122888 | tf_op jit(solution)/shard_map/ppermute | solution.py:90
  47.0 0.5 collective-permute-start.12
  47.4 4.8 %weight_pass.5 = (bf16[1600,2560]{1,0:T(8,128)(2,1)}, bf16[1600,2560]{1,0:T(8,128)(2,1)}, bf16[1600,2560]{1,0:T(8,128)(2,1)}, f32[8,128]{1,0:T(8,128)}) custom-call(bf16[800,128]{1,0:T(8,128)(2,1)S(1)} %collective-permute-done.11.refs_1_.refs_0_, ...), custom_call_target="tpu_custom_call", output_to_operand_aliasing={{0}: (2, {}), {1}: (3, {}), {2}: (4, {})} | custom-call | flops 314572800 | bytes 9830400 | tf_op jit(solution)/shard_map/weight_pass/pallas_call | solution.py:385
  52.3 0.9 %finish.1 = (bf16[2,5120]{1,0:T(2,128)(2,1)}, f32[1,5120]{1,0:T(1,128)}) custom-call(bf16[2,5120]{1,0:T(2,128)(2,1)S(1)} %bitcast.10, bf16[2,5120]{1,0:T(2,128)(2,1)S(1)} %bitcast.12, f32[1,5120]{1,0:T(1,128)S(1)} %get-tuple-element.44.gain_ref.norm_gain_ref, f32[2,5120]{1,0:T(2,128)S(1)} %get-tuple-element.70.own_ref, ...), custom_call_target="tpu_custom_call" | custom-call | tf_op jit(solution)/shard_map/finish/pallas_call | solution.py:472
  (22 shorter events, 0.5 us)
Async XLA Ops:
  1.4 9.9 %collective-permute-start.2 = (bf16[4,5120]{1,0:T(4,128)(2,1)S(1)}, bf16[4,5120]{1,0:T(4,128)(2,1)S(1)}, u32[]{:S(2)}, u32[]{:S(2)}) collective-permute-start(bf16[4,5120]{1,0:T(4,128)(2,1)S(1)} %pad_maximum_fusion.refs_4_.refs_0_), channel_id=1, source_target_pairs={{0,12},{2,14},{4,8},{6,10},{8,4},{10,6},{12,0},{14,2},{1,13},{3,15... | collective-permute-start | bytes 122888 | tf_op jit(solution)/shard_map/ppermute | solution.py:90
  6.5 4.9 %collective-permute-start.1 = (bf16[4,5120]{1,0:T(4,128)(2,1)S(1)}, bf16[4,5120]{1,0:T(4,128)(2,1)S(1)}, u32[]{:S(2)}, u32[]{:S(2)}) collective-permute-start(bf16[4,5120]{1,0:T(4,128)(2,1)S(1)} %pad_maximum_fusion.refs_4_.refs_0_), channel_id=1, source_target_pairs={{0,8},{2,10},{4,12},{6,14},{8,0},{10,2},{12,4},{14,6},{1,9},{3,11}... | collective-permute-start | bytes 122888 | tf_op jit(solution)/shard_map/ppermute | solution.py:90
  6.5 4.9 %collective-permute-start = (bf16[4,5120]{1,0:T(4,128)(2,1)S(1)}, bf16[4,5120]{1,0:T(4,128)(2,1)S(1)}, u32[]{:S(2)}, u32[]{:S(2)}) collective-permute-start(bf16[4,5120]{1,0:T(4,128)(2,1)S(1)} %pad_maximum_fusion.refs_4_.refs_0_), channel_id=1, source_target_pairs={{0,4},{2,6},{4,0},{6,2},{8,12},{10,14},{12,8},{14,10},{1,5},{3,7},... | collective-permute-start | bytes 122888 | tf_op jit(solution)/shard_map/ppermute | solution.py:90
  7.2 10.2 %collective-permute-start.3 = (bf16[4,5120]{1,0:T(4,128)(2,1)S(1)}, bf16[4,5120]{1,0:T(4,128)(2,1)S(1)}, u32[]{:S(2)}, u32[]{:S(2)}) collective-permute-start(bf16[4,5120]{1,0:T(4,128)(2,1)S(1)} %pad_maximum_fusion.refs_4_.refs_0_), channel_id=1, source_target_pairs={{0,2},{2,0},{4,6},{6,4},{8,10},{10,8},{12,14},{14,12},{1,3},{3,1},... | collective-permute-start | bytes 122888 | tf_op jit(solution)/shard_map/ppermute | solution.py:90
  11.5 5.9 %collective-permute-start.5 = (bf16[4,5120]{1,0:T(4,128)(2,1)S(1)}, bf16[4,5120]{1,0:T(4,128)(2,1)S(1)}, u32[]{:S(2)}, u32[]{:S(2)}) collective-permute-start(bf16[4,5120]{1,0:T(4,128)(2,1)S(1)} %get-tuple-element.47.refs_2_), channel_id=1, source_target_pairs={{0,2},{2,0},{4,6},{6,4},{8,10},{10,8},{12,14},{14,12},{1,3},{3,1},... | collective-permute-start | bytes 122888 | tf_op jit(solution)/shard_map/ppermute | solution.py:90
  13.0 4.4 %collective-permute-start.6 = (bf16[4,5120]{1,0:T(4,128)(2,1)S(1)}, bf16[4,5120]{1,0:T(4,128)(2,1)S(1)}, u32[]{:S(2)}, u32[]{:S(2)}) collective-permute-start(bf16[4,5120]{1,0:T(4,128)(2,1)S(1)} %get-tuple-element.48.refs_3_), channel_id=1, source_target_pairs={{0,2},{2,0},{4,6},{6,4},{8,10},{10,8},{12,14},{14,12},{1,3},{3,1},... | collective-permute-start | bytes 122888 | tf_op jit(solution)/shard_map/ppermute | solution.py:90
  13.6 4.0 %collective-permute-start.4 = (bf16[4,5120]{1,0:T(4,128)(2,1)S(1)}, bf16[4,5120]{1,0:T(4,128)(2,1)S(1)}, u32[]{:S(2)}, u32[]{:S(2)}) collective-permute-start(bf16[4,5120]{1,0:T(4,128)(2,1)S(1)} %get-tuple-element.46.refs_4_.refs_1_), channel_id=1, source_target_pairs={{0,2},{2,0},{4,6},{6,4},{8,10},{10,8},{12,14},{14,12},{1,3},{3,1},... | collective-permute-start | bytes 122888 | tf_op jit(solution)/shard_map/ppermute | solution.py:90
  17.8 1.7 %collective-permute-start.7 = (bf16[32,5120]{1,0:T(8,128)(2,1)S(1)}, bf16[32,5120]{1,0:T(8,128)(2,1)S(1)}, u32[]{:S(2)}, u32[]{:S(2)}) collective-permute-start(bf16[32,5120]{1,0:T(8,128)(2,1)S(1)} %sort_rows.1.own_ref), channel_id=1, source_target_pairs={{0,1},{1,0},{2,3},{3,2},{4,5},{5,4},{6,7},{7,6},{8,9},{9,8},{10,11... | collective-permute-start | bytes 983048 | tf_op jit(solution)/shard_map/ppermute | solution.py:90
  33.4 3.3 %collective-permute-start.8 = (bf16[18,5120]{1,0:T(8,128)(2,1)S(1)}, bf16[18,5120]{1,0:T(8,128)(2,1)S(1)}, u32[]{:S(2)}, u32[]{:S(2)}) collective-permute-start(bf16[18,5120]{1,0:T(8,128)(2,1)S(1)} %get-tuple-element.58), channel_id=1, source_target_pairs={{0,1},{1,0},{2,3},{3,2},{4,5},{5,4},{6,7},{7,6},{8,9},{9,8},{10,11... | collective-permute-start | bytes 552968 | tf_op jit(solution)/shard_map/ppermute | solution.py:90
  33.6 5.3 %collective-permute-start.11 = (bf16[800,128]{1,0:T(8,128)(2,1)S(1)}, bf16[800,128]{1,0:T(8,128)(2,1)S(1)}, u32[]{:S(2)}, u32[]{:S(2)}) collective-permute-start(bf16[800,128]{1,0:T(8,128)(2,1)S(1)} %get-tuple-element.59.refs_0_), channel_id=1, source_target_pairs={{0,1},{1,0},{2,3},{3,2},{4,5},{5,4},{6,7},{7,6},{8,9},{9,8},{10,11... | collective-permute-start | bytes 614408 | tf_op jit(solution)/shard_map/ppermute | solution.py:90
  36.8 6.3 %collective-permute-start.9 = (bf16[8,5120]{1,0:T(8,128)(2,1)S(1)}, bf16[8,5120]{1,0:T(8,128)(2,1)S(1)}, u32[]{:S(2)}, u32[]{:S(2)}) collective-permute-start(bf16[8,5120]{1,0:T(8,128)(2,1)S(1)} %get-tuple-element.64.refs_6_), channel_id=1, source_target_pairs={{0,2},{2,0},{4,6},{6,4},{8,10},{10,8},{12,14},{14,12},{1,3},{3,1},... | collective-permute-start | bytes 245768 | tf_op jit(solution)/shard_map/ppermute | solution.py:90
  38.4 4.7 %collective-permute-start.10 = (bf16[2,5120]{1,0:T(2,128)(2,1)S(1)}, bf16[2,5120]{1,0:T(2,128)(2,1)S(1)}, u32[]{:S(2)}, u32[]{:S(2)}) collective-permute-start(bf16[2,5120]{1,0:T(2,128)(2,1)S(1)} %get-tuple-element.65), channel_id=1, source_target_pairs={{0,2},{2,0},{4,6},{6,4},{8,10},{10,8},{12,14},{14,12},{1,3},{3,1},... | collective-permute-start | bytes 61448 | tf_op jit(solution)/shard_map/ppermute | solution.py:90
  43.3 8.9 %collective-permute-start.13 = (bf16[4,5120]{1,0:T(4,128)(2,1)S(1)}, bf16[4,5120]{1,0:T(4,128)(2,1)S(1)}, u32[]{:S(2)}, u32[]{:S(2)}) collective-permute-start(bf16[4,5120]{1,0:T(4,128)(2,1)S(1)} %get-tuple-element.73), channel_id=1, source_target_pairs={{0,8},{2,10},{4,12},{6,14},{8,0},{10,2},{12,4},{14,6},{1,9},{3,11}... | collective-permute-start | bytes 122888 | tf_op jit(solution)/shard_map/ppermute | solution.py:90
  45.4 6.8 %collective-permute-start.14 = (bf16[4,5120]{1,0:T(4,128)(2,1)S(1)}, bf16[4,5120]{1,0:T(4,128)(2,1)S(1)}, u32[]{:S(2)}, u32[]{:S(2)}) collective-permute-start(bf16[4,5120]{1,0:T(4,128)(2,1)S(1)} %get-tuple-element.74), channel_id=1, source_target_pairs={{0,12},{2,14},{4,8},{6,10},{8,4},{10,6},{12,0},{14,2},{1,13},{3,15... | collective-permute-start | bytes 122888 | tf_op jit(solution)/shard_map/ppermute | solution.py:90
  47.0 5.3 %collective-permute-start.12 = (bf16[4,5120]{1,0:T(4,128)(2,1)S(1)}, bf16[4,5120]{1,0:T(4,128)(2,1)S(1)}, u32[]{:S(2)}, u32[]{:S(2)}) collective-permute-start(bf16[4,5120]{1,0:T(4,128)(2,1)S(1)} %get-tuple-element.72.refs_5_), channel_id=1, source_target_pairs={{0,4},{2,6},{4,0},{6,2},{8,12},{10,14},{12,8},{14,10},{1,5},{3,7},... | collective-permute-start | bytes 122888 | tf_op jit(solution)/shard_map/ppermute | solution.py:90
  47.4 4.8 %copy-start = (bf16[1,2,1,5120]{3,1,2,0:T(2,128)(2,1)S(1)}, bf16[1,2,1,5120]{3,1,2,0:T(2,128)(2,1)}, u32[]{:S(2)}) copy-start(bf16[1,2,1,5120]{3,1,2,0:T(2,128)(2,1)} %param.6) | copy-start | bytes 61444
  47.4 4.8 %copy-start.1 = (bf16[1,2,1,5120]{3,1,2,0:T(2,128)(2,1)S(1)}, bf16[1,2,1,5120]{3,1,2,0:T(2,128)(2,1)}, u32[]{:S(2)}) copy-start(bf16[1,2,1,5120]{3,1,2,0:T(2,128)(2,1)} %param.11) | copy-start | bytes 61444

commit v9 on v8

--- a/solution.py
+++ b/solution.py
@@ -490,7 +490,7 @@
     gain_hbm = norm_gain.reshape(1, model)
 
     weights = (gate_weight.T, up_weight.T, down_weight)
-    step_rows = 160
+    step_rows = 80
     blocks = ffw // 2 // step_rows
     piece = jnp.concatenate([own_tokens, own_incoming], axis=0)
     near = exchange(piece, "tp", 1)

time: 53.4 us -> 54.2 us (1.015)
  Pallas kernels: 31.8 us -> 32.6 us
    pallas_call x3, Pallas kernels: 11.7 us -> 12.5 us  [weight_pass(): pl.pallas_call(functools.partial(weight_kernel, toks, spans, len(packs)),...]
  transfers between devices with their start and end apart: 15 -> 15, of which waited for: 3 -> 3; matrix products, arithmetic and copies ran while one was open for 0% -> 0% of each run, Pallas kernels for 31% -> 32%
where the time goes in v9:
time: 54.2 us; the launch traced here: 54 us
  Pallas kernels  32.6 us (60%)
  starting transfers between devices  17.8 us (33%)
  waiting for transfers between devices  1.93 us (4%)
  between operations  0.81 us (1%)
  other arithmetic  0.79 us (1%)
    ppermute x15, starting transfers between devices, exchange(): return lax.ppermute(value, axis, [(i, i ^ bits) for i in range(count)])  17.8 us
    pallas_call x1, Pallas kernels, hidden_pass(): pl.pallas_call(functools.partial(hidden_kernel, len(fetched)), out_shape=...  14 us
    pallas_call x3, Pallas kernels, weight_pass(): pl.pallas_call(functools.partial(weight_kernel, toks, spans, len(packs)),...  12.5 us
    pallas_call x2, Pallas kernels, fetch_weights(): pl.pallas_call(functools.partial(fetch_kernel, first, count), out_shape=(...  4.8 us
    ppermute x15, waiting for transfers between devices, exchange(): return lax.ppermute(value, axis, [(i, i ^ bits) for i in range(count)])  1.93 us
  transfers between devices with their start and end apart: 15, of which 3 were waited for; matrix products, arithmetic and copies ran while one was open for 0% of the time, Pallas kernels for 32%

profile of v9, /device:TPU:0, one launch (start us, length us, event | category | flops | bytes accessed | tf_op | source)
XLA Modules:
  0.0 54.0 jit_solution(3921127696373271876)
XLA Ops:
  0.6 0.8 %pad_maximum_fusion.refs_4_.refs_0_ = bf16[4,5120]{1,0:T(4,128)(2,1)S(1)} fusion(bf16[2,5120]{1,0:T(2,128)(2,1)} %bitcast.11, bf16[2,5120]{1,0:T(2,128)(2,1)} %bitcast.9), kind=kLoop, calls=%fused_computation | loop fusion | flops 81920 | bytes 81920 | tf_op jit(solution)/shard_map/concatenate | solution.py:495
  1.4 5.1 %collective-permute-start.2 = (bf16[4,5120]{1,0:T(4,128)(2,1)S(1)}, bf16[4,5120]{1,0:T(4,128)(2,1)S(1)}, u32[]{:S(2)}, u32[]{:S(2)}) collective-permute-start(bf16[4,5120]{1,0:T(4,128)(2,1)S(1)} %pad_maximum_fusion.refs_4_.refs_0_), channel_id=1, source_target_pairs={{0,12},{2,14},{4,8},{6,10},{8,4},{10,6},{12,0},{14,2},{1,13},{3,15... | collective-permute-start | bytes 122888 | tf_op jit(solution)/shard_map/ppermute | solution.py:90
  6.5 0.6 %collective-permute-start = (bf16[4,5120]{1,0:T(4,128)(2,1)S(1)}, bf16[4,5120]{1,0:T(4,128)(2,1)S(1)}, u32[]{:S(2)}, u32[]{:S(2)}) collective-permute-start(bf16[4,5120]{1,0:T(4,128)(2,1)S(1)} %pad_maximum_fusion.refs_4_.refs_0_), channel_id=1, source_target_pairs={{0,4},{2,6},{4,0},{6,2},{8,12},{10,14},{12,8},{14,10},{1,5},{3,7},... | collective-permute-start | bytes 122888 | tf_op jit(solution)/shard_map/ppermute | solution.py:90
  7.2 1.6 %collective-permute-start.3 = (bf16[4,5120]{1,0:T(4,128)(2,1)S(1)}, bf16[4,5120]{1,0:T(4,128)(2,1)S(1)}, u32[]{:S(2)}, u32[]{:S(2)}) collective-permute-start(bf16[4,5120]{1,0:T(4,128)(2,1)S(1)} %pad_maximum_fusion.refs_4_.refs_0_), channel_id=1, source_target_pairs={{0,2},{2,0},{4,6},{6,4},{8,10},{10,8},{12,14},{14,12},{1,3},{3,1},... | collective-permute-start | bytes 122888 | tf_op jit(solution)/shard_map/ppermute | solution.py:90
  8.8 2.5 %fetch_weights.2 = (bf16[1792,512]{1,0:T(8,128)(2,1)S(1)}, bf16[896,512]{1,0:T(8,128)(2,1)S(1)}, bf16[1792,512]{1,0:T(8,128)(2,1)S(1)}, bf16[896,512]{1,0:T(8,12...) custom-call(bf16[1600,5120]{1,0:T(8,128)(2,1)} %bitcast.13, bf16[1600,5120]{1,0:T(8,128)(2,1)} %bitcast.16, ...), custom_call_target="tpu_custom_call" | custom-call | bytes 4915200 | tf_op jit(solution)/shard_map/fetch_weights/pallas_call | solution.py:188
  11.5 1.6 %collective-permute-start.5 = (bf16[4,5120]{1,0:T(4,128)(2,1)S(1)}, bf16[4,5120]{1,0:T(4,128)(2,1)S(1)}, u32[]{:S(2)}, u32[]{:S(2)}) collective-permute-start(bf16[4,5120]{1,0:T(4,128)(2,1)S(1)} %get-tuple-element.47.refs_2_), channel_id=1, source_target_pairs={{0,2},{2,0},{4,6},{6,4},{8,10},{10,8},{12,14},{14,12},{1,3},{3,1},... | collective-permute-start | bytes 122888 | tf_op jit(solution)/shard_map/ppermute | solution.py:90
  13.0 0.5 collective-permute-start.6
  13.6 1.5 %collective-permute-start.4 = (bf16[4,5120]{1,0:T(4,128)(2,1)S(1)}, bf16[4,5120]{1,0:T(4,128)(2,1)S(1)}, u32[]{:S(2)}, u32[]{:S(2)}) collective-permute-start(bf16[4,5120]{1,0:T(4,128)(2,1)S(1)} %get-tuple-element.46.refs_4_.refs_1_), channel_id=1, source_target_pairs={{0,2},{2,0},{4,6},{6,4},{8,10},{10,8},{12,14},{14,12},{1,3},{3,1},... | collective-permute-start | bytes 122888 | tf_op jit(solution)/shard_map/ppermute | solution.py:90
  15.0 2.3 %fetch_weights.3 = (bf16[1792,512]{1,0:T(8,128)(2,1)S(1)}, bf16[896,512]{1,0:T(8,128)(2,1)S(1)}, f32[1,5120]{1,0:T(1,128)}, f32[8,128]{1,0:T(8,128)S(1)}) custom-call(bf16[1600,5120]{1,0:T(8,128)(2,1)} %bitcast.14, bf16[1600,5120]{1,0:T(8,128)(2,1)} %bitcast.17, bf16[1600,5120]{1,0:T(8,128)(2,1)} %refs_2_.5, f32[1,5120]{1,0:T(1,128)} %bitcast.22, ...), custom_call_target="tpu_custom_call" | custom-call | bytes 2457600 | tf_op jit(solution)/shard_map/fetch_weights/pallas_call | solution.py:188
  17.4 0.2 collective-permute-done.4.refs_5_
  17.6 0.2 sort_rows.1.own_ref
  17.8 1.6 %collective-permute-done.7.peer_ref = bf16[32,5120]{1,0:T(8,128)(2,1)S(1)} collective-permute-done((bf16[32,5120]{1,0:T(8,128)(2,1)S(1)}, bf16[32,5120]{1,0:T(8,128)(2,1)S(1)}, u32[]{:S(2)}, u32[]{:S(2)}) %collective-permute-start.7) | collective-permute-done | bytes 327712 | tf_op jit(solution)/shard_map/ppermute | solution.py:90
  19.5 14.0 %hidden_pass.1 = (bf16[800,128]{1,0:T(8,128)(2,1)S(1)}, f32[16,5120]{1,0:T(8,128)S(1)}, bf16[18,5120]{1,0:T(8,128)(2,1)S(1)}, f32[1,5120]{1,0:T(1,128)S(1)}, bf16[64,5120]{1,0:T(8,128)(2,1)S(1)}) custom-call(bf16[32,5120]{1,0:T(8,128)(2,1)S(1)} %sort_rows.1.own_ref, bf16[32,5120]{1,0:T(8,128)(2,1)S(1)} %collective-permute-done.7.peer_ref, ...), custom_call_target="tpu_custom_call" | custom-call | flops 1310720000 | bytes 24576000 | tf_op jit(solution)/shard_map/hidden_pass/pallas_call | solution.py:305
  33.4 0.2 collective-permute-start.8
  33.6 0.4 collective-permute-start.11
  34.0 3.2 %weight_pass.3 = (bf16[1600,2560]{1,0:T(8,128)(2,1)}, bf16[1600,2560]{1,0:T(8,128)(2,1)}, bf16[1600,2560]{1,0:T(8,128)(2,1)}, f32[8,128]{1,0:T(8,128)S(1)}) custom-call(bf16[800,128]{1,0:T(8,128)(2,1)S(1)} %get-tuple-element.59.refs_0_, bf16[64,5120]{1,0:T(8,128)(2,1)S(1)} %get-tuple-element.60.refs_1_.refs_2_), custom_call_target="tpu_custom_call" | custom-call | flops 196608000 | bytes 6144000 | tf_op jit(solution)/shard_map/weight_pass/pallas_call | solution.py:385
  37.3 1.6 %collective-permute-start.9 = (bf16[8,5120]{1,0:T(8,128)(2,1)S(1)}, bf16[8,5120]{1,0:T(8,128)(2,1)S(1)}, u32[]{:S(2)}, u32[]{:S(2)}) collective-permute-start(bf16[8,5120]{1,0:T(8,128)(2,1)S(1)} %get-tuple-element.64.refs_6_), channel_id=1, source_target_pairs={{0,2},{2,0},{4,6},{6,4},{8,10},{10,8},{12,14},{14,12},{1,3},{3,1},... | collective-permute-start | bytes 245768 | tf_op jit(solution)/shard_map/ppermute | solution.py:90
  38.9 0.5 collective-permute-start.10
  39.4 4.6 %weight_pass.4 = (bf16[1600,2560]{1,0:T(8,128)(2,1)}, bf16[1600,2560]{1,0:T(8,128)(2,1)}, bf16[1600,2560]{1,0:T(8,128)(2,1)}, f32[8,128]{1,0:T(8,128)S(1)}) custom-call(bf16[800,128]{1,0:T(8,128)(2,1)S(1)} %get-tuple-element.59.refs_0_, ...), custom_call_target="tpu_custom_call", output_to_operand_aliasing={{0}: (3, {}), {1}: (4, {}), {2}: (5, {})} | custom-call | flops 314572800 | bytes 9830400 | tf_op jit(solution)/shard_map/weight_pass/pallas_call | solution.py:385
  44.2 2.1 %collective-permute-start.13 = (bf16[4,5120]{1,0:T(4,128)(2,1)S(1)}, bf16[4,5120]{1,0:T(4,128)(2,1)S(1)}, u32[]{:S(2)}, u32[]{:S(2)}) collective-permute-start(bf16[4,5120]{1,0:T(4,128)(2,1)S(1)} %get-tuple-element.73), channel_id=1, source_target_pairs={{0,8},{2,10},{4,12},{6,14},{8,0},{10,2},{12,4},{14,6},{1,9},{3,11}... | collective-permute-start | bytes 122888 | tf_op jit(solution)/shard_map/ppermute | solution.py:90
  46.3 1.5 %collective-permute-start.14 = (bf16[4,5120]{1,0:T(4,128)(2,1)S(1)}, bf16[4,5120]{1,0:T(4,128)(2,1)S(1)}, u32[]{:S(2)}, u32[]{:S(2)}) collective-permute-start(bf16[4,5120]{1,0:T(4,128)(2,1)S(1)} %get-tuple-element.74), channel_id=1, source_target_pairs={{0,12},{2,14},{4,8},{6,10},{8,4},{10,6},{12,0},{14,2},{1,13},{3,15... | collective-permute-start | bytes 122888 | tf_op jit(solution)/shard_map/ppermute | solution.py:90
  47.8 0.5 collective-permute-start.12
  48.3 4.7 %weight_pass.5 = (bf16[1600,2560]{1,0:T(8,128)(2,1)}, bf16[1600,2560]{1,0:T(8,128)(2,1)}, bf16[1600,2560]{1,0:T(8,128)(2,1)}, f32[8,128]{1,0:T(8,128)}) custom-call(bf16[800,128]{1,0:T(8,128)(2,1)S(1)} %collective-permute-done.11.refs_1_.refs_0_, ...), custom_call_target="tpu_custom_call", output_to_operand_aliasing={{0}: (2, {}), {1}: (3, {}), {2}: (4, {})} | custom-call | flops 275251200 | bytes 8601600 | tf_op jit(solution)/shard_map/weight_pass/pallas_call | solution.py:385
  53.1 0.9 %finish.1 = (bf16[2,5120]{1,0:T(2,128)(2,1)}, f32[1,5120]{1,0:T(1,128)}) custom-call(bf16[2,5120]{1,0:T(2,128)(2,1)S(1)} %bitcast.10, bf16[2,5120]{1,0:T(2,128)(2,1)S(1)} %bitcast.12, f32[1,5120]{1,0:T(1,128)S(1)} %get-tuple-element.44.gain_ref.norm_gain_ref, f32[2,5120]{1,0:T(2,128)S(1)} %get-tuple-element.70.own_ref, ...), custom_call_target="tpu_custom_call" | custom-call | tf_op jit(solution)/shard_map/finish/pallas_call | solution.py:472
  (22 shorter events, 0.5 us)
Async XLA Ops:
  1.4 9.9 %collective-permute-start.2 = (bf16[4,5120]{1,0:T(4,128)(2,1)S(1)}, bf16[4,5120]{1,0:T(4,128)(2,1)S(1)}, u32[]{:S(2)}, u32[]{:S(2)}) collective-permute-start(bf16[4,5120]{1,0:T(4,128)(2,1)S(1)} %pad_maximum_fusion.refs_4_.refs_0_), channel_id=1, source_target_pairs={{0,12},{2,14},{4,8},{6,10},{8,4},{10,6},{12,0},{14,2},{1,13},{3,15... | collective-permute-start | bytes 122888 | tf_op jit(solution)/shard_map/ppermute | solution.py:90
  6.5 4.9 %collective-permute-start.1 = (bf16[4,5120]{1,0:T(4,128)(2,1)S(1)}, bf16[4,5120]{1,0:T(4,128)(2,1)S(1)}, u32[]{:S(2)}, u32[]{:S(2)}) collective-permute-start(bf16[4,5120]{1,0:T(4,128)(2,1)S(1)} %pad_maximum_fusion.refs_4_.refs_0_), channel_id=1, source_target_pairs={{0,8},{2,10},{4,12},{6,14},{8,0},{10,2},{12,4},{14,6},{1,9},{3,11}... | collective-permute-start | bytes 122888 | tf_op jit(solution)/shard_map/ppermute | solution.py:90
  6.5 4.9 %collective-permute-start = (bf16[4,5120]{1,0:T(4,128)(2,1)S(1)}, bf16[4,5120]{1,0:T(4,128)(2,1)S(1)}, u32[]{:S(2)}, u32[]{:S(2)}) collective-permute-start(bf16[4,5120]{1,0:T(4,128)(2,1)S(1)} %pad_maximum_fusion.refs_4_.refs_0_), channel_id=1, source_target_pairs={{0,4},{2,6},{4,0},{6,2},{8,12},{10,14},{12,8},{14,10},{1,5},{3,7},... | collective-permute-start | bytes 122888 | tf_op jit(solution)/shard_map/ppermute | solution.py:90
  7.2 10.2 %collective-permute-start.3 = (bf16[4,5120]{1,0:T(4,128)(2,1)S(1)}, bf16[4,5120]{1,0:T(4,128)(2,1)S(1)}, u32[]{:S(2)}, u32[]{:S(2)}) collective-permute-start(bf16[4,5120]{1,0:T(4,128)(2,1)S(1)} %pad_maximum_fusion.refs_4_.refs_0_), channel_id=1, source_target_pairs={{0,2},{2,0},{4,6},{6,4},{8,10},{10,8},{12,14},{14,12},{1,3},{3,1},... | collective-permute-start | bytes 122888 | tf_op jit(solution)/shard_map/ppermute | solution.py:90
  11.5 5.9 %collective-permute-start.5 = (bf16[4,5120]{1,0:T(4,128)(2,1)S(1)}, bf16[4,5120]{1,0:T(4,128)(2,1)S(1)}, u32[]{:S(2)}, u32[]{:S(2)}) collective-permute-start(bf16[4,5120]{1,0:T(4,128)(2,1)S(1)} %get-tuple-element.47.refs_2_), channel_id=1, source_target_pairs={{0,2},{2,0},{4,6},{6,4},{8,10},{10,8},{12,14},{14,12},{1,3},{3,1},... | collective-permute-start | bytes 122888 | tf_op jit(solution)/shard_map/ppermute | solution.py:90
  13.0 4.4 %collective-permute-start.6 = (bf16[4,5120]{1,0:T(4,128)(2,1)S(1)}, bf16[4,5120]{1,0:T(4,128)(2,1)S(1)}, u32[]{:S(2)}, u32[]{:S(2)}) collective-permute-start(bf16[4,5120]{1,0:T(4,128)(2,1)S(1)} %get-tuple-element.48.refs_3_), channel_id=1, source_target_pairs={{0,2},{2,0},{4,6},{6,4},{8,10},{10,8},{12,14},{14,12},{1,3},{3,1},... | collective-permute-start | bytes 122888 | tf_op jit(solution)/shard_map/ppermute | solution.py:90
  13.6 4.0 %collective-permute-start.4 = (bf16[4,5120]{1,0:T(4,128)(2,1)S(1)}, bf16[4,5120]{1,0:T(4,128)(2,1)S(1)}, u32[]{:S(2)}, u32[]{:S(2)}) collective-permute-start(bf16[4,5120]{1,0:T(4,128)(2,1)S(1)} %get-tuple-element.46.refs_4_.refs_1_), channel_id=1, source_target_pairs={{0,2},{2,0},{4,6},{6,4},{8,10},{10,8},{12,14},{14,12},{1,3},{3,1},... | collective-permute-start | bytes 122888 | tf_op jit(solution)/shard_map/ppermute | solution.py:90
  17.8 1.7 %collective-permute-start.7 = (bf16[32,5120]{1,0:T(8,128)(2,1)S(1)}, bf16[32,5120]{1,0:T(8,128)(2,1)S(1)}, u32[]{:S(2)}, u32[]{:S(2)}) collective-permute-start(bf16[32,5120]{1,0:T(8,128)(2,1)S(1)} %sort_rows.1.own_ref), channel_id=1, source_target_pairs={{0,1},{1,0},{2,3},{3,2},{4,5},{5,4},{6,7},{7,6},{8,9},{9,8},{10,11... | collective-permute-start | bytes 983048 | tf_op jit(solution)/shard_map/ppermute | solution.py:90
  33.4 3.8 %collective-permute-start.8 = (bf16[18,5120]{1,0:T(8,128)(2,1)S(1)}, bf16[18,5120]{1,0:T(8,128)(2,1)S(1)}, u32[]{:S(2)}, u32[]{:S(2)}) collective-permute-start(bf16[18,5120]{1,0:T(8,128)(2,1)S(1)} %get-tuple-element.58), channel_id=1, source_target_pairs={{0,1},{1,0},{2,3},{3,2},{4,5},{5,4},{6,7},{7,6},{8,9},{9,8},{10,11... | collective-permute-start | bytes 552968 | tf_op jit(solution)/shard_map/ppermute | solution.py:90
  33.6 5.8 %collective-permute-start.11 = (bf16[800,128]{1,0:T(8,128)(2,1)S(1)}, bf16[800,128]{1,0:T(8,128)(2,1)S(1)}, u32[]{:S(2)}, u32[]{:S(2)}) collective-permute-start(bf16[800,128]{1,0:T(8,128)(2,1)S(1)} %get-tuple-element.59.refs_0_), channel_id=1, source_target_pairs={{0,1},{1,0},{2,3},{3,2},{4,5},{5,4},{6,7},{7,6},{8,9},{9,8},{10,11... | collective-permute-start | bytes 614408 | tf_op jit(solution)/shard_map/ppermute | solution.py:90
  37.3 6.7 %collective-permute-start.9 = (bf16[8,5120]{1,0:T(8,128)(2,1)S(1)}, bf16[8,5120]{1,0:T(8,128)(2,1)S(1)}, u32[]{:S(2)}, u32[]{:S(2)}) collective-permute-start(bf16[8,5120]{1,0:T(8,128)(2,1)S(1)} %get-tuple-element.64.refs_6_), channel_id=1, source_target_pairs={{0,2},{2,0},{4,6},{6,4},{8,10},{10,8},{12,14},{14,12},{1,3},{3,1},... | collective-permute-start | bytes 245768 | tf_op jit(solution)/shard_map/ppermute | solution.py:90
  38.9 5.1 %collective-permute-start.10 = (bf16[2,5120]{1,0:T(2,128)(2,1)S(1)}, bf16[2,5120]{1,0:T(2,128)(2,1)S(1)}, u32[]{:S(2)}, u32[]{:S(2)}) collective-permute-start(bf16[2,5120]{1,0:T(2,128)(2,1)S(1)} %get-tuple-element.65), channel_id=1, source_target_pairs={{0,2},{2,0},{4,6},{6,4},{8,10},{10,8},{12,14},{14,12},{1,3},{3,1},... | collective-permute-start | bytes 61448 | tf_op jit(solution)/shard_map/ppermute | solution.py:90
  44.2 8.8 %collective-permute-start.13 = (bf16[4,5120]{1,0:T(4,128)(2,1)S(1)}, bf16[4,5120]{1,0:T(4,128)(2,1)S(1)}, u32[]{:S(2)}, u32[]{:S(2)}) collective-permute-start(bf16[4,5120]{1,0:T(4,128)(2,1)S(1)} %get-tuple-element.73), channel_id=1, source_target_pairs={{0,8},{2,10},{4,12},{6,14},{8,0},{10,2},{12,4},{14,6},{1,9},{3,11}... | collective-permute-start | bytes 122888 | tf_op jit(solution)/shard_map/ppermute | solution.py:90
  46.3 6.7 %collective-permute-start.14 = (bf16[4,5120]{1,0:T(4,128)(2,1)S(1)}, bf16[4,5120]{1,0:T(4,128)(2,1)S(1)}, u32[]{:S(2)}, u32[]{:S(2)}) collective-permute-start(bf16[4,5120]{1,0:T(4,128)(2,1)S(1)} %get-tuple-element.74), channel_id=1, source_target_pairs={{0,12},{2,14},{4,8},{6,10},{8,4},{10,6},{12,0},{14,2},{1,13},{3,15... | collective-permute-start | bytes 122888 | tf_op jit(solution)/shard_map/ppermute | solution.py:90
  47.8 5.2 %collective-permute-start.12 = (bf16[4,5120]{1,0:T(4,128)(2,1)S(1)}, bf16[4,5120]{1,0:T(4,128)(2,1)S(1)}, u32[]{:S(2)}, u32[]{:S(2)}) collective-permute-start(bf16[4,5120]{1,0:T(4,128)(2,1)S(1)} %get-tuple-element.72.refs_5_), channel_id=1, source_target_pairs={{0,4},{2,6},{4,0},{6,2},{8,12},{10,14},{12,8},{14,10},{1,5},{3,7},... | collective-permute-start | bytes 122888 | tf_op jit(solution)/shard_map/ppermute | solution.py:90
  48.3 4.7 %copy-start = (bf16[1,2,1,5120]{3,1,2,0:T(2,128)(2,1)S(1)}, bf16[1,2,1,5120]{3,1,2,0:T(2,128)(2,1)}, u32[]{:S(2)}) copy-start(bf16[1,2,1,5120]{3,1,2,0:T(2,128)(2,1)} %param.6) | copy-start | bytes 61444
  48.3 4.7 %copy-start.1 = (bf16[1,2,1,5120]{3,1,2,0:T(2,128)(2,1)S(1)}, bf16[1,2,1,5120]{3,1,2,0:T(2,128)(2,1)}, u32[]{:S(2)}) copy-start(bf16[1,2,1,5120]{3,1,2,0:T(2,128)(2,1)} %param.11) | copy-start | bytes 61444
